TPU v7x, 128 devices: a whole 4x4x4 slice. The times are simulated.
128 devices in a mesh: dp: 4 (over z), ctx: 32 (over x, y, core).
Axes of the slice: x: 4, y: 4, z: 4, core: 2. Of those that a mesh axis runs over, the one named last changes fastest.
Arguments:
- queries: bfloat16 [4, 4096, 3072], P('dp', 'ctx'), may hold values from -48 to 48
- key_rows: bfloat16 [4, 4096, 512], P('dp', 'ctx'), may hold values from -6 to 6
- value_rows: bfloat16 [4, 4096, 512], P('dp', 'ctx'), may hold values from -6 to 6
- upstream: bfloat16 [4, 4096, 3072], P('dp', 'ctx'), may hold values from -6 to 6
- loss_weight: float32 [4, 4096], P('dp', 'ctx'), may hold values from 0.25 to 12
- doc_lengths: int32 [4, 8], P('dp'), may hold values from 1 to 2048, 4096 in all within a row
Outputs:
- attended: bfloat16 [4, 4096, 3072], P('dp', 'ctx')
- query_grad: bfloat16 [4, 4096, 3072], P('dp', 'ctx')
- key_grad: bfloat16 [4, 4096, 512], P('dp', 'ctx')
- value_grad: bfloat16 [4, 4096, 512], P('dp', 'ctx')
Inputs may be any that keep to these rules, and one draw needn't show every extreme that they name: `doc_lengths`: each row holds 8 lengths that sum to 4096; the largest is exactly 2048.
All inputs are finite; a program needn't handle non-finite values.
Results may differ from a plain program's by a relative error of at most 0.025.
Values may be sent and summed in bfloat16 or wider, within the bound.
No kernel may reach another device: no remote copies, remote signals or barrier semaphores. Data moves between devices by JAX's collectives and lax.ppermute only.
A program may use at most 128 MiB of HBM per device.

v0:
```python
import math

import jax
import jax.numpy as jnp
from jax import lax
from jax.sharding import PartitionSpec as P

QH = 24
KVH = 4
HD = 128


logit_cap = 30.0


def doc_index(positions, lengths_row):
    boundary = jnp.cumsum(lengths_row)
    return jnp.sum((positions[:, None] >= boundary[None, :]).astype(jnp.int32), axis=1)


def capped(query_heads, key_piece):
    raw = jnp.einsum(
        "rhgd,bhd->hgrb", query_heads, key_piece, preferred_element_type=jnp.float32
    ) * HD ** (-0.5)
    return jnp.tanh(raw / logit_cap)


def body(queries, key_rows, value_rows, upstream, loss_weight, doc_lengths):
    row_count = queries.shape[1]
    ctx_count = lax.axis_size("ctx")
    capacity = (5 * row_count + 4 * ctx_count - 1) // (4 * ctx_count)
    slot_count = ctx_count * capacity
    group_size = QH // KVH
    length = ctx_count * row_count
    lengths_row = doc_lengths[0]
    keys_own = key_rows[0]
    values_own = value_rows[0]
    weights_row = loss_weight[0]
    weight_sum = lax.psum(jnp.sum(weights_row), ("dp", "ctx"))
    cotangent = (upstream[0].astype(jnp.float32) * (weights_row / weight_sum)[:, None]).astype(
        jnp.bfloat16
    )
    local_rows = jnp.arange(row_count, dtype=jnp.int32)
    destination = (local_rows * ctx_count // row_count + lax.axis_index("ctx")) % ctx_count
    hits = (destination[:, None] == jnp.arange(ctx_count, dtype=jnp.int32)[None, :]).astype(
        jnp.int32
    )
    earlier = jnp.cumsum(hits, axis=0) - hits
    slot_of = destination * capacity + jnp.sum(earlier * hits, axis=1)
    placing = slot_of[:, None] == jnp.arange(slot_count, dtype=jnp.int32)[None, :]
    placing_bf = placing.astype(jnp.bfloat16)
    home_pos = lax.axis_index("ctx") * row_count + local_rows
    query_send = jnp.einsum(
        "ts,tw->sw", placing_bf, queries[0], preferred_element_type=jnp.float32
    ).astype(jnp.bfloat16)
    grad_send = jnp.einsum(
        "ts,tw->sw", placing_bf, cotangent, preferred_element_type=jnp.float32
    ).astype(jnp.bfloat16)
    pos_send = jnp.sum(jnp.where(placing, home_pos[:, None] + 1, 0), axis=0)
    query_slots, grad_slots, pos_slots = (
        lax.all_to_all(query_send, "ctx", split_axis=0, concat_axis=0, tiled=True),
        lax.all_to_all(grad_send, "ctx", split_axis=0, concat_axis=0, tiled=True),
        lax.all_to_all(pos_send, "ctx", split_axis=0, concat_axis=0, tiled=True),
    )
    valid = pos_slots > 0
    query_pos = pos_slots - 1
    query_doc = doc_index(query_pos, lengths_row)
    query_heads = query_slots.reshape(slot_count, KVH, group_size, HD)
    grad_heads = grad_slots.reshape(slot_count, KVH, group_size, HD)

    def allowed_for(key_pos):
        key_doc = doc_index(key_pos, lengths_row)
        return (
            (query_doc[:, None] == key_doc[None, :])
            & (key_pos[None, :] <= query_pos[:, None])
            & valid[:, None]
        )

    def attend(state_now, key_piece, value_piece, offset):
        denom_sum, weighted = state_now
        width = key_piece.shape[0]
        key_pos = offset + jnp.arange(width, dtype=jnp.int32)
        squashed = capped(query_heads, key_piece.reshape(width, KVH, HD))
        expo = jnp.where(
            allowed_for(key_pos)[None, None], jnp.exp(logit_cap * squashed - logit_cap), 0.0
        )
        mixed_vals = jnp.einsum(
            "hgrb,bhd->rhgd",
            expo.astype(jnp.bfloat16),
            value_piece.reshape(width, KVH, HD),
            preferred_element_type=jnp.float32,
        )
        return (
            denom_sum + jnp.sum(expo, axis=-1),
            weighted + mixed_vals.reshape(slot_count, QH * HD),
        )

    initial = (
        jnp.zeros((KVH, group_size, slot_count), jnp.float32),
        jnp.zeros((slot_count, QH * HD), jnp.float32),
    )
    key_piece = lax.all_gather(keys_own, "ctx", axis=0, tiled=True)
    value_piece = lax.all_gather(values_own, "ctx", axis=0, tiled=True)
    width = key_piece.shape[0]
    step_rows = math.gcd(width, 512)

    def inner_step(block_number, state_in):
        block_start = block_number * step_rows
        return attend(
            state_in,
            lax.dynamic_slice_in_dim(key_piece, block_start, step_rows, 0),
            lax.dynamic_slice_in_dim(value_piece, block_start, step_rows, 0),
            block_start,
        )

    denom_sum, weighted = lax.fori_loop(0, width // step_rows, inner_step, initial)
    safe_denom = jnp.where(valid[None, None, :], denom_sum, 1.0)
    out_heads = (
        weighted.reshape(slot_count, KVH, group_size, HD)
        / jnp.transpose(safe_denom, (2, 0, 1))[..., None]
    ).astype(jnp.bfloat16)
    out_slots = out_heads.reshape(slot_count, QH * HD)
    out_back = lax.all_to_all(out_slots, "ctx", split_axis=0, concat_axis=0, tiled=True)
    keys_back, values_back = (
        lax.all_gather(keys_own, "ctx", axis=0, tiled=True),
        lax.all_gather(values_own, "ctx", axis=0, tiled=True),
    )
    row_dot = jnp.transpose(
        jnp.sum(grad_heads.astype(jnp.float32) * out_heads.astype(jnp.float32), axis=-1), (1, 2, 0)
    )
    key_block = min(length, 512)

    def block_terms(block_start, width):
        key_piece = lax.dynamic_slice_in_dim(keys_back, block_start, width, 0).reshape(
            width, KVH, HD
        )
        value_piece = lax.dynamic_slice_in_dim(values_back, block_start, width, 0).reshape(
            width, KVH, HD
        )
        key_pos = block_start + jnp.arange(width, dtype=jnp.int32)
        squashed = capped(query_heads, key_piece)
        expo = jnp.where(
            allowed_for(key_pos)[None, None], jnp.exp(logit_cap * squashed - logit_cap), 0.0
        )
        probs = expo / safe_denom[..., None]
        grad_prob = jnp.einsum(
            "rhgd,bhd->hgrb", grad_heads, value_piece, preferred_element_type=jnp.float32
        )
        grad_score = (
            probs * (grad_prob - row_dot[..., None]) * (1.0 - squashed * squashed)
        ).astype(jnp.bfloat16)
        return (key_piece, probs, grad_score)

    def key_value_terms(probs, grad_score, width):
        key_term = jnp.einsum(
            "hgrb,rhgd->bhd", grad_score, query_heads, preferred_element_type=jnp.float32
        ) * HD ** (-0.5)
        value_term = jnp.einsum(
            "hgrb,rhgd->bhd",
            probs.astype(jnp.bfloat16),
            grad_heads,
            preferred_element_type=jnp.float32,
        )
        return jnp.concatenate(
            (key_term.reshape(width, KVH * HD), value_term.reshape(width, KVH * HD)), axis=1
        )

    def query_term(dq_sum, key_piece, grad_score):
        return dq_sum + jnp.einsum(
            "hgrb,bhd->rhgd", grad_score, key_piece, preferred_element_type=jnp.float32
        )

    dq_start = jnp.zeros((slot_count, KVH, group_size, HD), jnp.float32)
    block_numbers = jnp.arange(length // key_block, dtype=jnp.int32)

    def backward_block(dq_sum, block_number):
        key_piece, probs, grad_score = block_terms(block_number * key_block, key_block)
        return (
            query_term(dq_sum, key_piece, grad_score),
            key_value_terms(probs, grad_score, key_block),
        )

    dq_sum, kv_terms = lax.scan(backward_block, dq_start, block_numbers)
    kv_terms = kv_terms.reshape(length, 2 * KVH * HD)
    kv_grads = lax.psum_scatter(
        kv_terms.astype(jnp.bfloat16), "ctx", scatter_dimension=0, tiled=True
    ).astype(jnp.float32)
    dq_slots = (dq_sum * HD ** (-0.5)).astype(jnp.bfloat16).reshape(slot_count, QH * HD)
    dq_back = lax.all_to_all(dq_slots, "ctx", split_axis=0, concat_axis=0, tiled=True)
    out_rows = jnp.einsum(
        "ts,sw->tw", placing_bf, out_back, preferred_element_type=jnp.float32
    ).astype(jnp.bfloat16)
    dq_rows = jnp.einsum(
        "ts,sw->tw", placing_bf, dq_back, preferred_element_type=jnp.float32
    ).astype(jnp.bfloat16)
    half_width = KVH * HD
    key_out = kv_grads[:, :half_width].astype(jnp.bfloat16)
    value_out = kv_grads[:, half_width:].astype(jnp.bfloat16)
    return (out_rows[None], dq_rows[None], key_out[None], value_out[None])


def solution(mesh):
    in_specs = (
        P("dp", "ctx", None),
        P("dp", "ctx", None),
        P("dp", "ctx", None),
        P("dp", "ctx", None),
        P("dp", "ctx"),
        P("dp", None),
    )
    out_specs = (
        P("dp", "ctx", None),
        P("dp", "ctx", None),
        P("dp", "ctx", None),
        P("dp", "ctx", None),
    )
    return jax.shard_map(body, mesh=mesh, in_specs=in_specs, out_specs=out_specs, check_vma=False)
```

profile of v0, /device:TPU:1, one launch (start us, length us, event | category | flops | bytes accessed | tf_op | source)
XLA Modules:
  0.0 525.0 jit_solution(8942310291126786245)
XLA Ops:
  13.4 8.6 %all-to-all-start = ((s32[32,5,1]{1,2,0:T(1,128)}), s32[32,5,1]{1,2,0:T(1,128)S(1)}, u32[]{:S(2)}, u32[]{:S(2)}) async-start(s32[32,5,1]{1,2,0:T(1,128)} %bitcast), calls=%async_computation | async-start | bytes 32768 | tf_op jit(solution)/shard_map/all_to_all | solution.py:63
  22.0 68.5 %psum.7 = f32[]{:T(128)} all-reduce(f32[]{:T(128)} %reduce_sum.92), channel_id=1, replica_groups=mesh['dp'=4,'ctx'=32] {'dp','ctx'}, use_global_device_ids=true, to_apply=%region_11.12 | all-reduce | flops 1 | bytes 8 | tf_op jit(solution)/shard_map/psum | solution.py:39
  94.9 4.9 all-to-all-start.3
  101.6 23.7 %all-to-all-done.3 = bf16[32,5,3072]{2,1,0:T(8,128)(2,1)S(1)} async-done(((bf16[32,5,3072]{2,1,0:T(8,128)(2,1)}), bf16[32,5,3072]{2,1,0:T(8,128)(2,1)S(1)}, u32[]{:S(2)}, u32[]{:S(2)}) %all-to-all-start.3) | async-done | bytes 983072 | tf_op jit(solution)/shard_map/all_to_all | solution.py:62
  125.3 6.1 %all-to-all-start.1 = ((bf16[32,5,3072]{2,1,0:T(8,128)(2,1)}), bf16[32,5,3072]{2,1,0:T(8,128)(2,1)}, u32[]{:S(2)}, u32[]{:S(2)}) async-start(bf16[32,5,3072]{2,1,0:T(8,128)(2,1)} %all_to_all.36), calls=%async_computation.1 | async-start | bytes 3145728 | tf_op jit(solution)/shard_map/all_to_all | solution.py:61
  136.6 17.4 %all-to-all-done.1 = bf16[32,5,3072]{2,1,0:T(8,128)(2,1)} async-done(((bf16[32,5,3072]{2,1,0:T(8,128)(2,1)}), bf16[32,5,3072]{2,1,0:T(8,128)(2,1)}, u32[]{:S(2)}, u32[]{:S(2)}) %all-to-all-start.1) | async-done | bytes 983072 | tf_op jit(solution)/shard_map/all_to_all | solution.py:61
  157.3 109.1 %while.33 = (s32[]{:T(128)}, f32[4,6,160]{2,1,0:T(8,128)S(1)}, f32[160,3072]{1,0:T(8,128)}, s32[160]{0:T(256)S(1)}, s32[1,8]{1,0:T(1,128)S(1)}, /*index=5*/s32[1...) while((s32[]{:T(128)}, f32[4,6,160]{2,1,0:T(8,128)S(1)}, ...), condition=%wide.region_9.10_spmd.clone, body=%wide.region_6.9_spmd.clone.sunk | while | flops 1027620608 | bytes 43769540 | solution.py:116
  180.4 3.8 select_add_fusion.5
  194.1 3.8 select_add_fusion.5
  207.9 3.8 select_add_fusion.5
  221.6 3.8 select_add_fusion.5
  235.3 3.8 select_add_fusion.5
  249.0 3.8 select_add_fusion.5
  262.7 3.8 select_add_fusion.5
  267.5 3.5 reshape.357
  274.4 131.1 %while.34 = (s32[]{:T(128)}, f32[160,4,6,128]{3,0,2,1:T(8,128)S(1)}, bf16[8,512,1024]{1,2,0:T(8,128)(2,1)}, s32[8]{0:T(128)S(1)}, bf16[4096,512]{0,1:T(8,128)(2,...) while((s32[]{:T(128)}, ...), condition=%wide.region_15.16_spmd.clone, body=%wide.region_13.15_spmd.clone.sunk | while | flops 2553950208 | bytes 58237684 | solution.py:183
  283.3 4.4 fusion.91
  299.7 4.4 fusion.91
  316.0 4.4 fusion.91
  332.4 4.4 fusion.91
  348.7 4.4 fusion.91
  365.1 4.4 fusion.91
  381.4 4.4 fusion.91
  394.3 3.4 fusion.92
  397.8 4.4 fusion.91
  405.4 11.4 %copy.56 = bf16[8,512,1024]{2,1,0:T(8,128)(2,1)} copy(bf16[8,512,1024]{1,2,0:T(8,128)(2,1)} %get-tuple-element.430) | data formatting | bytes 16777216 | tf_op jit(solution)/shard_map/convert_element_type | solution.py:186
  422.8 3.6 divide_convert_fusion.1
  428.8 4.9 all-to-all-start.2
  436.4 20.2 %all-to-all-done.2 = bf16[32,5,3072]{2,1,0:T(8,128)(2,1)} async-done(((bf16[32,5,3072]{2,1,0:T(8,128)(2,1)}), bf16[32,5,3072]{2,1,0:T(8,128)(2,1)}, u32[]{:S(2)}, u32[]{:S(2)}) %all-to-all-start.2) | async-done | bytes 983072 | tf_op jit(solution)/shard_map/all_to_all | solution.py:123
  456.6 4.3 all-to-all-start.4
  462.6 34.4 %all-to-all-done.4 = bf16[32,5,3072]{2,1,0:T(8,128)(2,1)S(1)} async-done(((bf16[32,5,3072]{2,1,0:T(8,128)(2,1)}), bf16[32,5,3072]{2,1,0:T(8,128)(2,1)S(1)}, u32[]{:S(2)}, u32[]{:S(2)}) %all-to-all-start.4) | async-done | bytes 983072 | tf_op jit(solution)/shard_map/all_to_all | solution.py:189
  502.0 14.8 %reduce-scatter.2.cloned.1.call-done = bf16[128,1024]{1,0:T(8,128)(2,1)} async-done(((bf16[4096,1024]{1,0:T(8,128)(2,1)}), bf16[128,1024]{1,0:T(8,128)(2,1)}) %reduce-scatter.2.cloned.1.call-update) | async-done | bytes 262160 | tf_op jit(solution)/shard_map/reduce_scatter | solution.py:185
  (295 shorter events, 213.3 us)
Async XLA Ops:
  7.2 92.6 %copy-start = (bf16[1,128,3072]{2,1,0:T(8,128)(2,1)S(1)}, bf16[1,128,3072]{2,1,0:T(8,128)(2,1)}, u32[]{:S(2)}) copy-start(bf16[1,128,3072]{2,1,0:T(8,128)(2,1)} %param.10) | copy-start | bytes 2359300
  7.2 150.1 %all-gather.5.cloned.1.call-start = ((), (), s32[]{:S(2)}) async-start(), calls=%async_computation.7 | async-start | bytes 4325376 | tf_op jit(solution)/shard_map/all_gather | solution.py:102
  9.0 148.4 %all-gather.7.cloned.1.call-start = ((), (), s32[]{:S(2)}) async-start(), calls=%async_computation.8 | async-start | bytes 4325376 | tf_op jit(solution)/shard_map/all_gather | solution.py:103
  11.2 88.9 %copy-start.12 = (s32[128]{0:T(128)}, s32[128]{0:T(128)S(1)}, u32[]{:S(2)}) copy-start(s32[128]{0:T(128)S(1)} %multiply_add_fusion) | copy-start | bytes 1540
  13.4 81.5 %all-to-all-start = ((s32[32,5,1]{1,2,0:T(1,128)}), s32[32,5,1]{1,2,0:T(1,128)S(1)}, u32[]{:S(2)}, u32[]{:S(2)}) async-start(s32[32,5,1]{1,2,0:T(1,128)} %bitcast), calls=%async_computation | async-start | bytes 32768 | tf_op jit(solution)/shard_map/all_to_all | solution.py:63
  94.9 30.4 %all-to-all-start.3 = ((bf16[32,5,3072]{2,1,0:T(8,128)(2,1)}), bf16[32,5,3072]{2,1,0:T(8,128)(2,1)S(1)}, u32[]{:S(2)}, u32[]{:S(2)}) async-start(bf16[32,5,3072]{2,1,0:T(8,128)(2,1)} %all_to_all.41), calls=%async_computation.3 | async-start | bytes 3145728 | tf_op jit(solution)/shard_map/all_to_all | solution.py:62
  99.7 31.9 %copy-start.14 = (s32[1,8]{1,0:T(1,128)S(1)}, s32[1,8]{1,0:T(1,128)}, u32[]{:S(2)}) copy-start(s32[1,8]{1,0:T(1,128)} %param.15) | copy-start | bytes 100
  125.3 7.0 %copy-start.8 = (bf16[32,5,3072]{2,1,0:T(8,128)(2,1)}, bf16[32,5,3072]{2,1,0:T(8,128)(2,1)S(1)}, u32[]{:S(2)}) copy-start(bf16[32,5,3072]{2,1,0:T(8,128)(2,1)S(1)} %all-to-all-done.3) | copy-start | bytes 2949124
  125.3 28.8 %all-to-all-start.1 = ((bf16[32,5,3072]{2,1,0:T(8,128)(2,1)}), bf16[32,5,3072]{2,1,0:T(8,128)(2,1)}, u32[]{:S(2)}, u32[]{:S(2)}) async-start(bf16[32,5,3072]{2,1,0:T(8,128)(2,1)} %all_to_all.36), calls=%async_computation.1 | async-start | bytes 3145728 | tf_op jit(solution)/shard_map/all_to_all | solution.py:61
  131.3 385.4 %reduce-scatter.2.cloned.1.call-start = ((), (), s32[]{:S(2)}) async-start(), calls=%async_computation.6 | async-start | bytes 8650752 | tf_op jit(solution)/shard_map/reduce_scatter | solution.py:185
  135.2 18.8 %copy-start.7 = (bf16[160,4,6,128]{3,2,1,0:T(8,128)(2,1)}, bf16[160,4,6,128]{3,2,1,0:T(8,128)(2,1)S(1)}, u32[]{:S(2)}) copy-start(bf16[160,4,6,128]{3,2,1,0:T(8,128)(2,1)S(1)} %reshape.356) | copy-start | bytes 2949124
  157.4 4.9 copy-start.3
  170.5 4.9 copy-start.3
  184.2 4.9 copy-start.3
  197.9 4.9 copy-start.3
  211.6 4.9 copy-start.3
  225.3 4.9 copy-start.3
  239.0 4.9 copy-start.3
  252.8 4.9 copy-start.3
  267.5 6.7 %copy-start.9 = (f32[160,4,6]{2,1,0:T(4,128)}, f32[160,4,6]{2,1,0:T(4,128)S(1)}, u32[]{:S(2)}) copy-start(f32[160,4,6]{2,1,0:T(4,128)S(1)} %copy.51) | copy-start | bytes 46084
  267.5 6.9 %copy-start.2 = (f32[160,4,6,128]{3,0,2,1:T(8,128)S(1)}, f32[160,4,6,128]{3,0,2,1:T(8,128)}, u32[]{:S(2)}) copy-start(f32[160,4,6,128]{3,0,2,1:T(8,128)} %custom-call.2) | copy-start | bytes 5898244
  283.3 4.4 copy-start.6
  299.6 4.4 copy-start.6
  316.0 4.4 copy-start.6
  332.4 4.4 copy-start.6
  348.7 4.4 copy-start.6
  365.0 4.4 copy-start.6
  381.4 4.4 copy-start.6
  428.8 27.8 %all-to-all-start.2 = ((bf16[32,5,3072]{2,1,0:T(8,128)(2,1)}), bf16[32,5,3072]{2,1,0:T(8,128)(2,1)}, u32[]{:S(2)}, u32[]{:S(2)}) async-start(bf16[32,5,3072]{2,1,0:T(8,128)(2,1)} %all_to_all.38), calls=%async_computation.2 | async-start | bytes 3145728 | tf_op jit(solution)/shard_map/all_to_all | solution.py:123
  436.4 61.8 %copy-start.13 = (s32[128]{0:T(128)S(1)}, s32[128]{0:T(128)}, u32[]{:S(2)}) copy-start(s32[128]{0:T(128)} %copy-done.12) | copy-start | bytes 1540
  456.6 40.4 %all-to-all-start.4 = ((bf16[32,5,3072]{2,1,0:T(8,128)(2,1)}), bf16[32,5,3072]{2,1,0:T(8,128)(2,1)S(1)}, u32[]{:S(2)}, u32[]{:S(2)}) async-start(bf16[32,5,3072]{2,1,0:T(8,128)(2,1)} %all_to_all.43), calls=%async_computation.4 | async-start | bytes 3145728 | tf_op jit(solution)/shard_map/all_to_all | solution.py:189
  460.9 57.5 %copy-start.1 = (bf16[1,128,3072]{2,1,0:T(8,128)(2,1)S(1)}, bf16[1,128,3072]{2,1,0:T(8,128)(2,1)}, u32[]{:S(2)}) copy-start(bf16[1,128,3072]{2,1,0:T(8,128)(2,1)} %param.10) | copy-start | bytes 2359300
  (19 other events, 55.6 us)
Sparse Core Ops, SparseCore 0:
  10.8 53.1 all-gather.4
  66.7 62.6 all-gather.6
  417.0 99.6 reduce-scatter.1
where the time goes:
time: 528 us; the launch traced here: 525 us
  matrix products  149 us (28%)
  waiting for transfers between devices  110 us (21%)
  local copies, waits for them, and re-layouts  94.3 us (18%)
  blocking collectives  68.5 us (13%)
  other arithmetic  52.8 us (10%)
  starting transfers between devices  29 us (5%)
  between operations  14.1 us (3%)
  loops' own time  6.62 us (1%)
    psum x1, blocking collectives, body(): weight_sum = lax.psum(jnp.sum(weights_row), ('dp', 'ctx'))  68.5 us
    dot_general x16, matrix products, capped(): jnp.einsum('rhgd,bhd->hgrb', query_heads, key_piece, preferred_element_ty...  45.8 us
    dot_general x8, matrix products, block_terms(): jnp.einsum('rhgd,bhd->hgrb', grad_heads, value_piece, preferred_element_t...  34.9 us
    all_to_all x1, waiting for transfers between devices, body(): lax.all_to_all(dq_slots, 'ctx', split_axis=0, concat_axis=0, tiled=True)  34.4 us
    add x8, other arithmetic, attend(): weighted + mixed_vals.reshape(slot_count, QH * HD)  29.5 us
    dot_general x8, matrix products, key_value_terms(): jnp.einsum('hgrb,rhgd->bhd', probs.astype(jnp.bfloat16), grad_heads, pref...  27.5 us
    all_to_all x1, waiting for transfers between devices, body(): lax.all_to_all(grad_send, 'ctx', split_axis=0, concat_axis=0, tiled=True)  23.7 us
    all_to_all x1, waiting for transfers between devices, body(): lax.all_to_all(out_slots, 'ctx', split_axis=0, concat_axis=0, tiled=True)  20.2 us
  transfers between devices with their start and end apart: 8, of which 5 were waited for; matrix products, arithmetic and copies ran while one was open for 5% of the time, Pallas kernels for 0%

commit v1 on v0

v1 whole, which is shorter than its diff:
```python
import functools
import math

import jax
import jax.numpy as jnp
from jax import lax
from jax.experimental import pallas as pl
from jax.experimental.pallas import tpu as pltpu
from jax.sharding import Mesh, PartitionSpec as P

QH = 24
KVH = 4
HD = 128
CAP = 30.0
NEAR = 2
GROUP = QH // KVH
ROWS = 256
HALF = 128
WIDE = GROUP * ROWS
SLOTS = 9
BF = jnp.bfloat16
F32 = jnp.float32
SCALE = HD ** (-0.5)


def dot(a, b):
    return jnp.dot(a, b, preferred_element_type=F32)


def attention_kernel(
    at_ref, len_ref, ws_ref, qm_ref, qo_ref, gm_ref, go_ref, kv_ref,
    att_ref, dq_ref, dkv_ref,
    qt, qs, gt, gs, expo, slope, out_t, dq_t, den, row_dot, ds_buf,
):
    chip = at_ref[0]
    core = at_ref[1]
    lane = lax.broadcasted_iota(jnp.int32, (1, ROWS), 1)
    flip = jnp.where(lane < HALF, core * HALF, (1 - core) * HALF - HALF)
    row_pos = chip * ROWS + lane + flip
    sub = lax.broadcasted_iota(jnp.int32, (ROWS, 1), 0)
    key_off = sub + jnp.where(sub < HALF, core * HALF, (1 - core) * HALF - HALF)

    start = jnp.zeros((1, ROWS), jnp.int32)
    low = jnp.int32(0)
    high = jnp.int32(0)
    edge = jnp.int32(0)
    for j in range(8):
        edge = edge + len_ref[j]
        start = jnp.maximum(start, jnp.where(row_pos >= edge, edge, 0))
        low = jnp.maximum(low, jnp.where(chip * ROWS >= edge, edge, 0))
        high = jnp.maximum(high, jnp.where(chip * ROWS + ROWS - 1 >= edge, edge, 0))

    for h in range(NEAR):
        for j in range(GROUP):
            for part, (q_in, g_in) in enumerate(((qm_ref, gm_ref), (qo_ref, go_ref))):
                cols = slice((h * GROUP + j) * HD, (h * GROUP + j + 1) * HD)
                rows = slice(j * ROWS + part * HALF, j * ROWS + (part + 1) * HALF)
                tile = q_in[:, cols]
                qs[h, rows, :] = tile
                qt[h, :, rows] = tile.T
                gt[h, :, rows] = g_in[:, cols].T
    out_t[...] = jnp.zeros_like(out_t)
    dq_t[...] = jnp.zeros_like(dq_t)
    den[...] = jnp.zeros_like(den)

    def forward(slot, masked):
        block = chip - slot
        for h in range(NEAR):
            keys = kv_ref[slot, :, h * HD:(h + 1) * HD]
            values_t = kv_ref[slot, :, (NEAR + h) * HD:(NEAR + h + 1) * HD].T
            for j in range(GROUP):
                cols = slice(j * ROWS, (j + 1) * ROWS)
                sq = jnp.tanh(dot(keys, qt[h, :, cols]) * (SCALE / CAP))
                e = jnp.exp2(sq * (CAP / math.log(2.0)))
                if masked:
                    key_pos = block * ROWS + key_off
                    e = jnp.where((key_pos >= start) & (key_pos <= row_pos), e, 0.0)
                eb = e.astype(BF)
                expo[slot, h, :, cols] = eb
                slope[slot, h, :, cols] = (e * (1.0 - sq * sq)).astype(BF)
                den[h, :, cols] += jnp.sum(e.reshape(ROWS // 8, 8, ROWS), axis=0)
                out_t[h, :, cols] += dot(values_t, eb)

    def needed(slot):
        return (slot <= chip) & ((chip - slot + 1) * ROWS > low)

    def forward_step(slot, carry):
        plain = (slot > 0) & ((chip - slot) * ROWS >= high)

        @pl.when(needed(slot) & plain)
        def _():
            forward(slot, False)

        @pl.when(needed(slot) & jnp.logical_not(plain))
        def _():
            forward(slot, True)

        return carry

    lax.fori_loop(0, SLOTS, forward_step, 0)

    inv_ws = 1.0 / ws_ref[0]
    for h in range(NEAR):
        for j in range(GROUP):
            cols = slice(j * ROWS, (j + 1) * ROWS)
            inv = 1.0 / jnp.sum(den[h, :, cols], axis=0, keepdims=True)
            out = (out_t[h, :, cols] * inv).astype(BF)
            hd = slice((h * GROUP + j) * HD, (h * GROUP + j + 1) * HD)
            att_ref[:, hd] = out.T
            g = (gt[h, :, cols].astype(F32) * (inv * inv_ws)).astype(BF)
            gt[h, :, cols] = g
            gs[h, cols, :] = g.T
            row_dot[h, :, cols] = jnp.sum(g.astype(F32) * out.astype(F32), axis=0, keepdims=True)

    def backward(slot):
        for h in range(NEAR):
            keys_t = kv_ref[slot, :, h * HD:(h + 1) * HD].T
            values = kv_ref[slot, :, (NEAR + h) * HD:(NEAR + h + 1) * HD]
            for j in range(GROUP):
                cols = slice(j * ROWS, (j + 1) * ROWS)
                dp = dot(values, gt[h, :, cols])
                ds = (slope[slot, h, :, cols].astype(F32) * (dp - row_dot[h, :, cols])).astype(BF)
                ds_buf[h, :, cols] = ds
                dq_t[h, :, cols] += dot(keys_t, ds)
            dkv_ref[slot, :, h * HD:(h + 1) * HD] = (dot(ds_buf[h], qs[h]) * SCALE).astype(BF)
            dkv_ref[slot, :, (NEAR + h) * HD:(NEAR + h + 1) * HD] = dot(expo[slot, h], gs[h]).astype(BF)

    def backward_step(slot, carry):
        @pl.when(needed(slot))
        def _():
            backward(slot)

        @pl.when(jnp.logical_not(needed(slot)))
        def _():
            dkv_ref[slot] = jnp.zeros((ROWS, 2 * NEAR * HD), BF)

        return carry

    lax.fori_loop(0, SLOTS, backward_step, 0)

    for h in range(NEAR):
        for j in range(GROUP):
            cols = slice(j * ROWS, (j + 1) * ROWS)
            hd = slice((h * GROUP + j) * HD, (h * GROUP + j + 1) * HD)
            dq_ref[:, hd] = (dq_t[h, :, cols] * SCALE).astype(BF).T


def attention(at, lengths, ws, qm, qo, gm, go, kv):
    smem = pl.BlockSpec(memory_space=pltpu.SMEM)
    vmem = pl.BlockSpec(memory_space=pltpu.VMEM)
    return pl.pallas_call(
        attention_kernel,
        out_shape=(
            jax.ShapeDtypeStruct((ROWS, NEAR * GROUP * HD), BF),
            jax.ShapeDtypeStruct((ROWS, NEAR * GROUP * HD), BF),
            jax.ShapeDtypeStruct((SLOTS, ROWS, 2 * NEAR * HD), BF),
        ),
        in_specs=[smem] * 3 + [vmem] * 5,
        out_specs=(vmem,) * 3,
        scratch_shapes=[
            pltpu.VMEM((NEAR, HD, WIDE), BF),
            pltpu.VMEM((NEAR, WIDE, HD), BF),
            pltpu.VMEM((NEAR, HD, WIDE), BF),
            pltpu.VMEM((NEAR, WIDE, HD), BF),
            pltpu.VMEM((SLOTS, NEAR, ROWS, WIDE), BF),
            pltpu.VMEM((SLOTS, NEAR, ROWS, WIDE), BF),
            pltpu.VMEM((NEAR, HD, WIDE), F32),
            pltpu.VMEM((NEAR, HD, WIDE), F32),
            pltpu.VMEM((NEAR, 8, WIDE), F32),
            pltpu.VMEM((NEAR, 1, WIDE), F32),
            pltpu.VMEM((NEAR, ROWS, WIDE), BF),
        ],
        compiler_params=pltpu.CompilerParams(vmem_limit_bytes=58 * 1024 * 1024),
        cost_estimate=pl.CostEstimate(
            flops=12 * NEAR * WIDE * HD * ROWS * 5, bytes_accessed=10_000_000, transcendentals=10_000_000
        ),
    )(at, lengths, ws, qm, qo, gm, go, kv)


SWAP = [(0, 1), (1, 0)]


def ring(k):
    return [(i, (i + k) % 4) for i in range(4)]


def body(queries, key_rows, value_rows, upstream, loss_weight, doc_lengths):
    x, y, core = lax.axis_index("x"), lax.axis_index("y"), lax.axis_index("core")
    weights_row = loss_weight[0]
    mine_at, other_at = core, 1 - core

    def half(array, at):
        size = array.shape[1] // 2
        return lax.dynamic_slice_in_dim(array, at * size, size, 1)

    kv_mine = jnp.concatenate([half(key_rows[0], mine_at), half(value_rows[0], mine_at)], axis=1)
    kv_send = jnp.concatenate([half(key_rows[0], other_at), half(value_rows[0], other_at)], axis=1)
    kv_other = lax.ppermute(kv_send, "core", SWAP)
    own = jnp.concatenate([kv_mine, kv_other], axis=0)

    r1 = lax.ppermute(own, "x", [(i, i + 1) for i in range(3)])
    r2 = lax.ppermute(own, "x", [(i, i + 2) for i in range(2)])
    three = jnp.concatenate([own, r1, r2], axis=0)
    slots = [None] * SLOTS
    slots[0], slots[4], slots[8] = own, r1, r2
    for k in (1, 3, 2):
        pair = lax.dynamic_slice_in_dim(three, jnp.where(y + k >= 4, ROWS, 0), 2 * ROWS, 0)
        got = lax.ppermute(pair, "y", ring(k))
        slots[k], slots[4 + k] = got[:ROWS], got[ROWS:]
    kv = jnp.stack(slots)

    weighted = (upstream[0].astype(F32) * weights_row[:, None]).astype(BF)
    qm, gm = half(queries[0], mine_at), half(weighted, mine_at)
    qo = lax.ppermute(half(queries[0], other_at), "core", SWAP)
    go = lax.ppermute(half(weighted, other_at), "core", SWAP)

    total = jnp.full((8, 128), jnp.sum(weights_row))
    total = total + lax.ppermute(total, "core", SWAP)
    for axis in ("y", "x", "dp"):
        total = total + sum(lax.ppermute(total, axis, ring(k)) for k in (1, 2, 3))
    at = jnp.stack([4 * x + y, core]).astype(jnp.int32)
    att, dq, dkv = attention(at, doc_lengths[0], total[0, :1], qm, qo, gm, go, kv)

    sums = [dkv[0].astype(F32), dkv[4].astype(F32), dkv[8].astype(F32)]
    for k in (1, 3, 2):
        pair = jnp.concatenate([dkv[k], dkv[4 + k]], axis=0)
        got = lax.ppermute(pair, "y", ring(4 - k)).astype(F32)
        over = y + k >= 4
        first, second = got[:ROWS], got[ROWS:]
        sums[0] = sums[0] + jnp.where(over, 0.0, first)
        sums[1] = sums[1] + jnp.where(over, first, second)
        sums[2] = sums[2] + jnp.where(over, second, 0.0)
    t1 = lax.ppermute(sums[1].astype(BF), "x", [(i + 1, i) for i in range(3)])
    t2 = lax.ppermute(sums[2].astype(BF), "x", [(i + 2, i) for i in range(2)])
    own_grad = (sums[0] + t1.astype(F32) + t2.astype(F32)).astype(BF)

    def join(mine, other):
        got = lax.ppermute(other, "core", SWAP)
        return jnp.where(
            core == 0, jnp.concatenate([mine, got], axis=1), jnp.concatenate([got, mine], axis=1)
        )

    out_rows = join(att[:HALF], att[HALF:])
    dq_rows = join(dq[:HALF], dq[HALF:])
    got = lax.ppermute(own_grad[HALF:], "core", SWAP)
    mine = own_grad[:HALF]
    width = NEAR * HD

    def side(at):
        a, b = mine[:, at:at + width], got[:, at:at + width]
        return jnp.where(core == 0, jnp.concatenate([a, b], axis=1), jnp.concatenate([b, a], axis=1))

    return (out_rows[None], dq_rows[None], side(0)[None], side(width)[None])


def solution(mesh):
    split = Mesh(mesh.devices.reshape(4, 4, 4, 2), ("dp", "x", "y", "core"))
    ctx = ("x", "y", "core")
    rows = P("dp", ctx, None)
    return jax.shard_map(
        body,
        mesh=split,
        in_specs=(rows, rows, rows, rows, P("dp", ctx), P("dp", None)),
        out_specs=(rows, rows, rows, rows),
        check_vma=False,
    )
```

time: 528 us -> 183 us (0.35)
  the two profiles are of different devices: /device:TPU:1 before, /device:TPU:3 now
where the time goes in v1:
time: 183 us; the launch traced here: 182 us
  waiting for transfers between devices  75.3 us (41%)
  starting transfers between devices  60.2 us (33%)
  Pallas kernels  27 us (15%)
  other arithmetic  11.3 us (6%)
  local copies, waits for them, and re-layouts  7.23 us (4%)
    pallas_call x1, Pallas kernels, attention(): pl.pallas_call(attention_kernel, out_shape=(jax.ShapeDtypeStruct((ROWS, N...  27 us
    ppermute x1, waiting for transfers between devices, body(): t1 = lax.ppermute(sums[1].astype(BF), 'x', [(i + 1, i) for i in range(3)])  24.3 us
    ppermute x3, starting transfers between devices, body(): got = lax.ppermute(pair, 'y', ring(4 - k)).astype(F32)  24 us
    ppermute x3, waiting for transfers between devices, body(): got = lax.ppermute(pair, 'y', ring(k))  20.4 us
    ppermute x3, waiting for transfers between devices, body(): got = lax.ppermute(pair, 'y', ring(4 - k)).astype(F32)  20.1 us
    ppermute x9, starting transfers between devices, body(): total = total + sum((lax.ppermute(total, axis, ring(k)) for k in (1, 2, 3)))  15.5 us
    ppermute x1, waiting for transfers between devices, body(): t2 = lax.ppermute(sums[2].astype(BF), 'x', [(i + 2, i) for i in range(2)])  6.51 us
  transfers between devices with their start and end apart: 26, of which 10 were waited for; matrix products, arithmetic and copies ran while one was open for 7% of the time, Pallas kernels for 0%

profile of v1, /device:TPU:3, one launch (start us, length us, event | category | flops | bytes accessed | tf_op | source)
XLA Modules:
  0.0 182.0 jit_solution(1989338997831871078)
XLA Ops:
  2.5 1.3 reduce_sum.9
  4.5 1.3 fusion
  7.3 1.4 collective-permute-start.1
  8.7 2.6 %collective-permute-start.2 = (f32[8,128]{1,0:T(8,128)S(1)}, f32[8,128]{1,0:T(8,128)S(1)}, u32[]{:S(2)}, u32[]{:S(2)}) collective-permute-start(f32[8,128]{1,0:T(8,128)S(1)} %broadcast_add_fusion), channel_id=1, source_target_pairs={{0,4},{2,6},{4,0},{6,2},{1,5},{3,7},{5,1},{7,3},{8,12},{10,14},{12... | collective-permute-start | bytes 12296 | tf_op jit(solution)/shard_map/ppermute | solution.py:220
  11.3 1.1 collective-permute-start.3
  12.4 3.1 %collective-permute-start.13 = (bf16[256,512]{1,0:T(8,128)(2,1)S(1)}, bf16[256,512]{1,0:T(8,128)(2,1)S(1)}, u32[]{:S(2)}, u32[]{:S(2)}) collective-permute-start(bf16[256,512]{1,0:T(8,128)(2,1)S(1)} %pad_maximum_fusion.4), channel_id=1, source_target_pairs={{0,8},{8,16},{16,24},{1,9},{9,17},{17,25},{2,10},{10,18},{18,26},{... | collective-permute-start | bytes 786440 | tf_op jit(solution)/shard_map/ppermute | solution.py:201
  15.5 1.9 %collective-permute-start.14 = (bf16[256,512]{1,0:T(8,128)(2,1)S(1)}, bf16[256,512]{1,0:T(8,128)(2,1)S(1)}, u32[]{:S(2)}, u32[]{:S(2)}) collective-permute-start(bf16[256,512]{1,0:T(8,128)(2,1)S(1)} %pad_maximum_fusion.4), channel_id=1, source_target_pairs={{0,16},{8,24},{1,17},{9,25},{2,18},{10,26},{3,19},{11,27},{4,20},{... | collective-permute-start | bytes 786440 | tf_op jit(solution)/shard_map/ppermute | solution.py:202
  18.4 1.6 collective-permute-start.11
  21.0 4.5 %collective-permute-start.5 = (f32[8,128]{1,0:T(8,128)S(1)}, f32[8,128]{1,0:T(8,128)S(1)}, u32[]{:S(2)}, u32[]{:S(2)}) collective-permute-start(f32[8,128]{1,0:T(8,128)S(1)} %add_add_fusion.2), channel_id=1, source_target_pairs={{0,16},{8,24},{16,0},{24,8},{1,17},{9,25},{17,1},{25,9},{2,18},{10... | collective-permute-start | bytes 12296 | tf_op jit(solution)/shard_map/ppermute | solution.py:220
  28.0 1.6 collective-permute-start.7
  29.6 3.3 %collective-permute-start.8 = (f32[8,128]{1,0:T(8,128)S(1)}, f32[8,128]{1,0:T(8,128)S(1)}, u32[]{:S(2)}, u32[]{:S(2)}) collective-permute-start(f32[8,128]{1,0:T(8,128)S(1)} %add_add_fusion.1), channel_id=1, source_target_pairs={{0,64},{32,96},{64,0},{96,32},{1,65},{33,97},{65,1},{97,33},{2,66}... | collective-permute-start | bytes 12296 | tf_op jit(solution)/shard_map/ppermute | solution.py:220
  34.3 2.6 %collective-permute-start.10 = (bf16[128,1536]{1,0:T(8,128)(2,1)}, bf16[128,1536]{1,0:T(8,128)(2,1)}, u32[]{:S(2)}, u32[]{:S(2)}) collective-permute-start(bf16[128,1536]{1,0:T(8,128)(2,1)} %get-tuple-element.27), channel_id=1, source_target_pairs={{0,1},{1,0},{2,3},{3,2},{4,5},{5,4},{6,7},{7,6},{8,9},{9,8},{10,11... | collective-permute-start | bytes 1179656 | tf_op jit(solution)/shard_map/ppermute | solution.py:214
  37.4 2.7 %collective-permute-start.17 = (bf16[512,512]{1,0:T(8,128)(2,1)S(1)}, bf16[512,512]{1,0:T(8,128)(2,1)S(1)}, u32[]{:S(2)}, u32[]{:S(2)}) collective-permute-start(bf16[512,512]{1,0:T(8,128)(2,1)S(1)} %get-tuple-element.22), channel_id=1, source_target_pairs={{0,6},{2,0},{4,2},{6,4},{1,7},{3,1},{5,3},{7,5},{8,14},{10,8},{12,... | collective-permute-start | bytes 1572872 | tf_op jit(solution)/shard_map/ppermute | solution.py:208
  40.2 11.6 %collective-permute-done.16 = bf16[512,512]{1,0:T(8,128)(2,1)S(1)} collective-permute-done((bf16[512,512]{1,0:T(8,128)(2,1)S(1)}, bf16[512,512]{1,0:T(8,128)(2,1)S(1)}, u32[]{:S(2)}, u32[]{:S(2)}) %collective-permute-start.16) | collective-permute-done | bytes 524320 | tf_op jit(solution)/shard_map/ppermute | solution.py:208
  51.9 8.8 %collective-permute-done.17 = bf16[512,512]{1,0:T(8,128)(2,1)S(1)} collective-permute-done((bf16[512,512]{1,0:T(8,128)(2,1)S(1)}, bf16[512,512]{1,0:T(8,128)(2,1)S(1)}, u32[]{:S(2)}, u32[]{:S(2)}) %collective-permute-start.17) | collective-permute-done | bytes 524320 | tf_op jit(solution)/shard_map/ppermute | solution.py:208
  60.8 1.4 copy-done.3
  62.2 27.0 %shard_map.93 = (bf16[256,1536]{1,0:T(8,128)(2,1)}, bf16[256,1536]{1,0:T(8,128)(2,1)}, bf16[9,256,512]{2,1,0:T(8,128)(2,1)}) custom-call(s32[2]{0:T(128)} %pad_add_fusion.at_ref, s32[8]{0:T(128)} %bitcast.88, f32[1]{0:T(128)} %bitcast.3.ws_ref, bf16[128,1536]{1,0:T(8,128)(2,1)} %get-tuple-element.28.qm_ref, ...), custom_call_target="tpu_custom_call" | custom-call | flops 6039797760 | bytes 10000000 | tf_op jit(solution)/shard_map/pallas_call | solution.py:151
  89.2 1.4 slice_bitcast_fusion.13
  90.7 22.6 %collective-permute-start.20 = (bf16[512,512]{1,0:T(8,128)(2,1)S(1)}, bf16[512,512]{1,0:T(8,128)(2,1)S(1)}, u32[]{:S(2)}, u32[]{:S(2)}) collective-permute-start(bf16[512,512]{1,0:T(8,128)(2,1)S(1)} %pad_maximum_fusion.1), channel_id=1, source_target_pairs={{0,6},{2,0},{4,2},{6,4},{1,7},{3,1},{5,3},{7,5},{8,14},{10,8},{12,... | collective-permute-start | bytes 1572872 | tf_op jit(solution)/shard_map/ppermute | solution.py:227
  113.5 1.3 collective-permute-start.22
  114.9 1.1 collective-permute-start.19
  116.1 1.2 collective-permute-done.19
  118.4 17.1 %collective-permute-done.20 = bf16[512,512]{1,0:T(8,128)(2,1)S(1)} collective-permute-done((bf16[512,512]{1,0:T(8,128)(2,1)S(1)}, bf16[512,512]{1,0:T(8,128)(2,1)S(1)}, u32[]{:S(2)}, u32[]{:S(2)}) %collective-permute-start.20) | collective-permute-done | bytes 524320 | tf_op jit(solution)/shard_map/ppermute | solution.py:227
  135.6 3.1 %collective-permute-done.21 = bf16[512,512]{1,0:T(8,128)(2,1)S(1)} collective-permute-done((bf16[512,512]{1,0:T(8,128)(2,1)S(1)}, bf16[512,512]{1,0:T(8,128)(2,1)S(1)}, u32[]{:S(2)}, u32[]{:S(2)}) %collective-permute-start.21) | collective-permute-done | bytes 524320 | tf_op jit(solution)/shard_map/ppermute | solution.py:227
  138.9 1.5 fusion.6
  140.4 1.9 %collective-permute-start.23 = (bf16[256,512]{1,0:T(8,128)(2,1)S(1)}, bf16[256,512]{1,0:T(8,128)(2,1)S(1)}, u32[]{:S(2)}, u32[]{:S(2)}) collective-permute-start(bf16[256,512]{1,0:T(8,128)(2,1)S(1)} %get-tuple-element.10), channel_id=1, source_target_pairs={{8,0},{16,8},{24,16},{9,1},{17,9},{25,17},{10,2},{18,10},{26,18},{... | collective-permute-start | bytes 786440 | tf_op jit(solution)/shard_map/ppermute | solution.py:233
  142.3 1.3 collective-permute-start.24
  143.7 1.1 maximum_select_fusion
  144.7 24.3 %collective-permute-done.23 = bf16[256,512]{1,0:T(8,128)(2,1)S(1)} collective-permute-done((bf16[256,512]{1,0:T(8,128)(2,1)S(1)}, bf16[256,512]{1,0:T(8,128)(2,1)S(1)}, u32[]{:S(2)}, u32[]{:S(2)}) %collective-permute-start.23) | collective-permute-done | bytes 262176 | tf_op jit(solution)/shard_map/ppermute | solution.py:233
  169.0 6.5 %collective-permute-done.24 = bf16[256,512]{1,0:T(8,128)(2,1)S(1)} collective-permute-done((bf16[256,512]{1,0:T(8,128)(2,1)S(1)}, bf16[256,512]{1,0:T(8,128)(2,1)S(1)}, u32[]{:S(2)}, u32[]{:S(2)}) %collective-permute-start.24) | collective-permute-done | bytes 262176 | tf_op jit(solution)/shard_map/ppermute | solution.py:234
  175.5 1.2 fusion.11
  176.7 2.9 %collective-permute-start.25 = (bf16[128,512]{1,0:T(8,128)(2,1)S(1)}, bf16[128,512]{1,0:T(8,128)(2,1)S(1)}, u32[]{:S(2)}, u32[]{:S(2)}) collective-permute-start(bf16[128,512]{1,0:T(8,128)(2,1)S(1)} %slice.140), channel_id=1, source_target_pairs={{0,1},{1,0},{2,3},{3,2},{4,5},{5,4},{6,7},{7,6},{8,9},{9,8},{10,11... | collective-permute-start | bytes 393224 | tf_op jit(solution)/shard_map/ppermute | solution.py:245
  (72 shorter events, 14.8 us)
Async XLA Ops:
  0.6 16.8 %copy-start.2 = (bf16[1,128,3072]{2,1,0:T(8,128)(2,1)S(1)}, bf16[1,128,3072]{2,1,0:T(8,128)(2,1)}, u32[]{:S(2)}) copy-start(bf16[1,128,3072]{2,1,0:T(8,128)(2,1)} %param.6) | copy-start | bytes 2359300
  1.7 10.7 %collective-permute-start.12 = (bf16[128,512]{1,0:T(8,128)(2,1)S(1)}, bf16[128,512]{1,0:T(8,128)(2,1)S(1)}, u32[]{:S(2)}, u32[]{:S(2)}) collective-permute-start(bf16[128,512]{1,0:T(8,128)(2,1)S(1)} %pad_maximum_fusion.5), channel_id=1, source_target_pairs={{0,1},{1,0},{2,3},{3,2},{4,5},{5,4},{6,7},{7,6},{8,9},{9,8},{10,11... | collective-permute-start | bytes 393224 | tf_op jit(solution)/shard_map/ppermute | solution.py:198
  4.4 2.3 %collective-permute-start = (f32[8,128]{1,0:T(8,128)S(1)}, f32[8,128]{1,0:T(8,128)S(1)}, u32[]{:S(2)}, u32[]{:S(2)}) collective-permute-start(f32[8,128]{1,0:T(8,128)S(1)} %broadcast_in_dim.17), channel_id=1, source_target_pairs={{0,1},{1,0},{2,3},{3,2},{4,5},{5,4},{6,7},{7,6},{8,9},{9,8},{10,11... | collective-permute-start | bytes 12296 | tf_op jit(solution)/shard_map/ppermute | solution.py:218
  7.3 11.1 %collective-permute-start.1 = (f32[8,128]{1,0:T(8,128)S(1)}, f32[8,128]{1,0:T(8,128)S(1)}, u32[]{:S(2)}, u32[]{:S(2)}) collective-permute-start(f32[8,128]{1,0:T(8,128)S(1)} %broadcast_add_fusion), channel_id=1, source_target_pairs={{0,2},{2,4},{4,6},{6,0},{1,3},{3,5},{5,7},{7,1},{8,10},{10,12},{12... | collective-permute-start | bytes 12296 | tf_op jit(solution)/shard_map/ppermute | solution.py:220
  8.7 11.4 %collective-permute-start.2 = (f32[8,128]{1,0:T(8,128)S(1)}, f32[8,128]{1,0:T(8,128)S(1)}, u32[]{:S(2)}, u32[]{:S(2)}) collective-permute-start(f32[8,128]{1,0:T(8,128)S(1)} %broadcast_add_fusion), channel_id=1, source_target_pairs={{0,4},{2,6},{4,0},{6,2},{1,5},{3,7},{5,1},{7,3},{8,12},{10,14},{12... | collective-permute-start | bytes 12296 | tf_op jit(solution)/shard_map/ppermute | solution.py:220
  11.3 8.8 %collective-permute-start.3 = (f32[8,128]{1,0:T(8,128)S(1)}, f32[8,128]{1,0:T(8,128)S(1)}, u32[]{:S(2)}, u32[]{:S(2)}) collective-permute-start(f32[8,128]{1,0:T(8,128)S(1)} %broadcast_add_fusion), channel_id=1, source_target_pairs={{0,6},{2,0},{4,2},{6,4},{1,7},{3,1},{5,3},{7,5},{8,14},{10,8},{12,... | collective-permute-start | bytes 12296 | tf_op jit(solution)/shard_map/ppermute | solution.py:220
  12.4 13.1 %collective-permute-start.13 = (bf16[256,512]{1,0:T(8,128)(2,1)S(1)}, bf16[256,512]{1,0:T(8,128)(2,1)S(1)}, u32[]{:S(2)}, u32[]{:S(2)}) collective-permute-start(bf16[256,512]{1,0:T(8,128)(2,1)S(1)} %pad_maximum_fusion.4), channel_id=1, source_target_pairs={{0,8},{8,16},{16,24},{1,9},{9,17},{17,25},{2,10},{10,18},{18,26},{... | collective-permute-start | bytes 786440 | tf_op jit(solution)/shard_map/ppermute | solution.py:201
  15.5 10.0 %collective-permute-start.14 = (bf16[256,512]{1,0:T(8,128)(2,1)S(1)}, bf16[256,512]{1,0:T(8,128)(2,1)S(1)}, u32[]{:S(2)}, u32[]{:S(2)}) collective-permute-start(bf16[256,512]{1,0:T(8,128)(2,1)S(1)} %pad_maximum_fusion.4), channel_id=1, source_target_pairs={{0,16},{8,24},{1,17},{9,25},{2,18},{10,26},{3,19},{11,27},{4,20},{... | collective-permute-start | bytes 786440 | tf_op jit(solution)/shard_map/ppermute | solution.py:202
  18.4 42.4 %collective-permute-start.11 = (bf16[128,1536]{1,0:T(8,128)(2,1)S(1)}, bf16[128,1536]{1,0:T(8,128)(2,1)}, u32[]{:S(2)}, u32[]{:S(2)}) collective-permute-start(bf16[128,1536]{1,0:T(8,128)(2,1)S(1)} %get-tuple-element.25), channel_id=1, source_target_pairs={{0,1},{1,0},{2,3},{3,2},{4,5},{5,4},{6,7},{7,6},{8,9},{9,8},{10,11... | collective-permute-start | bytes 1179656 | tf_op jit(solution)/shard_map/ppermute | solution.py:215
  20.7 6.5 %collective-permute-start.4 = (f32[8,128]{1,0:T(8,128)S(1)}, f32[8,128]{1,0:T(8,128)S(1)}, u32[]{:S(2)}, u32[]{:S(2)}) collective-permute-start(f32[8,128]{1,0:T(8,128)S(1)} %add_add_fusion.2), channel_id=1, source_target_pairs={{0,8},{8,16},{16,24},{24,0},{1,9},{9,17},{17,25},{25,1},{2,10},{10... | collective-permute-start | bytes 12296 | tf_op jit(solution)/shard_map/ppermute | solution.py:220
  21.0 6.1 %collective-permute-start.5 = (f32[8,128]{1,0:T(8,128)S(1)}, f32[8,128]{1,0:T(8,128)S(1)}, u32[]{:S(2)}, u32[]{:S(2)}) collective-permute-start(f32[8,128]{1,0:T(8,128)S(1)} %add_add_fusion.2), channel_id=1, source_target_pairs={{0,16},{8,24},{16,0},{24,8},{1,17},{9,25},{17,1},{25,9},{2,18},{10... | collective-permute-start | bytes 12296 | tf_op jit(solution)/shard_map/ppermute | solution.py:220
  25.5 2.5 %collective-permute-start.6 = (f32[8,128]{1,0:T(8,128)S(1)}, f32[8,128]{1,0:T(8,128)S(1)}, u32[]{:S(2)}, u32[]{:S(2)}) collective-permute-start(f32[8,128]{1,0:T(8,128)S(1)} %add_add_fusion.2), channel_id=1, source_target_pairs={{0,24},{8,0},{16,8},{24,16},{1,25},{9,1},{17,9},{25,17},{2,26},{10... | collective-permute-start | bytes 12296 | tf_op jit(solution)/shard_map/ppermute | solution.py:220
  25.7 14.5 %collective-permute-start.15 = (bf16[512,512]{1,0:T(8,128)(2,1)S(1)}, bf16[512,512]{1,0:T(8,128)(2,1)S(1)}, u32[]{:S(2)}, u32[]{:S(2)}) collective-permute-start(bf16[512,512]{1,0:T(8,128)(2,1)S(1)} %get-tuple-element.24), channel_id=1, source_target_pairs={{0,2},{2,4},{4,6},{6,0},{1,3},{3,5},{5,7},{7,1},{8,10},{10,12},{12... | collective-permute-start | bytes 1572872 | tf_op jit(solution)/shard_map/ppermute | solution.py:208
  28.0 6.3 %collective-permute-start.7 = (f32[8,128]{1,0:T(8,128)S(1)}, f32[8,128]{1,0:T(8,128)S(1)}, u32[]{:S(2)}, u32[]{:S(2)}) collective-permute-start(f32[8,128]{1,0:T(8,128)S(1)} %add_add_fusion.1), channel_id=1, source_target_pairs={{0,32},{32,64},{64,96},{96,0},{1,33},{33,65},{65,97},{97,1},{2,34}... | collective-permute-start | bytes 12296 | tf_op jit(solution)/shard_map/ppermute | solution.py:220
  29.6 7.2 %collective-permute-start.8 = (f32[8,128]{1,0:T(8,128)S(1)}, f32[8,128]{1,0:T(8,128)S(1)}, u32[]{:S(2)}, u32[]{:S(2)}) collective-permute-start(f32[8,128]{1,0:T(8,128)S(1)} %add_add_fusion.1), channel_id=1, source_target_pairs={{0,64},{32,96},{64,0},{96,32},{1,65},{33,97},{65,1},{97,33},{2,66}... | collective-permute-start | bytes 12296 | tf_op jit(solution)/shard_map/ppermute | solution.py:220
  32.9 4.0 %collective-permute-start.9 = (f32[8,128]{1,0:T(8,128)S(1)}, f32[8,128]{1,0:T(8,128)S(1)}, u32[]{:S(2)}, u32[]{:S(2)}) collective-permute-start(f32[8,128]{1,0:T(8,128)S(1)} %add_add_fusion.1), channel_id=1, source_target_pairs={{0,96},{32,0},{64,32},{96,64},{1,97},{33,1},{65,33},{97,65},{2,98}... | collective-permute-start | bytes 12296 | tf_op jit(solution)/shard_map/ppermute | solution.py:220
  34.3 26.5 %collective-permute-start.10 = (bf16[128,1536]{1,0:T(8,128)(2,1)}, bf16[128,1536]{1,0:T(8,128)(2,1)}, u32[]{:S(2)}, u32[]{:S(2)}) collective-permute-start(bf16[128,1536]{1,0:T(8,128)(2,1)} %get-tuple-element.27), channel_id=1, source_target_pairs={{0,1},{1,0},{2,3},{3,2},{4,5},{5,4},{6,7},{7,6},{8,9},{9,8},{10,11... | collective-permute-start | bytes 1179656 | tf_op jit(solution)/shard_map/ppermute | solution.py:214
  36.8 15.0 %collective-permute-start.16 = (bf16[512,512]{1,0:T(8,128)(2,1)S(1)}, bf16[512,512]{1,0:T(8,128)(2,1)S(1)}, u32[]{:S(2)}, u32[]{:S(2)}) collective-permute-start(bf16[512,512]{1,0:T(8,128)(2,1)S(1)} %get-tuple-element.23), channel_id=1, source_target_pairs={{0,4},{2,6},{4,0},{6,2},{1,5},{3,7},{5,1},{7,3},{8,12},{10,14},{12... | collective-permute-start | bytes 1572872 | tf_op jit(solution)/shard_map/ppermute | solution.py:208
  37.4 23.2 %collective-permute-start.17 = (bf16[512,512]{1,0:T(8,128)(2,1)S(1)}, bf16[512,512]{1,0:T(8,128)(2,1)S(1)}, u32[]{:S(2)}, u32[]{:S(2)}) collective-permute-start(bf16[512,512]{1,0:T(8,128)(2,1)S(1)} %get-tuple-element.22), channel_id=1, source_target_pairs={{0,6},{2,0},{4,2},{6,4},{1,7},{3,1},{5,3},{7,5},{8,14},{10,8},{12,... | collective-permute-start | bytes 1572872 | tf_op jit(solution)/shard_map/ppermute | solution.py:208
  60.8 1.4 copy-start.3
  90.7 24.1 %copy-start.1 = (bf16[256,1536]{1,0:T(8,128)(2,1)S(1)}, bf16[256,1536]{1,0:T(8,128)(2,1)}, u32[]{:S(2)}) copy-start(bf16[256,1536]{1,0:T(8,128)(2,1)} %get-tuple-element.8) | copy-start | bytes 2359300
  90.7 25.3 %copy-start = (bf16[256,1536]{1,0:T(8,128)(2,1)S(1)}, bf16[256,1536]{1,0:T(8,128)(2,1)}, u32[]{:S(2)}) copy-start(bf16[256,1536]{1,0:T(8,128)(2,1)} %get-tuple-element.7) | copy-start | bytes 2359300
  90.7 44.7 %collective-permute-start.20 = (bf16[512,512]{1,0:T(8,128)(2,1)S(1)}, bf16[512,512]{1,0:T(8,128)(2,1)S(1)}, u32[]{:S(2)}, u32[]{:S(2)}) collective-permute-start(bf16[512,512]{1,0:T(8,128)(2,1)S(1)} %pad_maximum_fusion.1), channel_id=1, source_target_pairs={{0,6},{2,0},{4,2},{6,4},{1,7},{3,1},{5,3},{7,5},{8,14},{10,8},{12,... | collective-permute-start | bytes 1572872 | tf_op jit(solution)/shard_map/ppermute | solution.py:227
  113.4 25.2 %collective-permute-start.21 = (bf16[512,512]{1,0:T(8,128)(2,1)S(1)}, bf16[512,512]{1,0:T(8,128)(2,1)S(1)}, u32[]{:S(2)}, u32[]{:S(2)}) collective-permute-start(bf16[512,512]{1,0:T(8,128)(2,1)S(1)} %pad_maximum_fusion.2), channel_id=1, source_target_pairs={{0,2},{2,4},{4,6},{6,0},{1,3},{3,5},{5,7},{7,1},{8,10},{10,12},{12... | collective-permute-start | bytes 1572872 | tf_op jit(solution)/shard_map/ppermute | solution.py:227
  113.5 25.2 %collective-permute-start.22 = (bf16[512,512]{1,0:T(8,128)(2,1)S(1)}, bf16[512,512]{1,0:T(8,128)(2,1)S(1)}, u32[]{:S(2)}, u32[]{:S(2)}) collective-permute-start(bf16[512,512]{1,0:T(8,128)(2,1)S(1)} %pad_maximum_fusion.3), channel_id=1, source_target_pairs={{0,4},{2,6},{4,0},{6,2},{1,5},{3,7},{5,1},{7,3},{8,12},{10,14},{12... | collective-permute-start | bytes 1572872 | tf_op jit(solution)/shard_map/ppermute | solution.py:227
  114.9 2.5 %collective-permute-start.19 = (bf16[128,1536]{1,0:T(8,128)(2,1)S(1)}, bf16[128,1536]{1,0:T(8,128)(2,1)S(1)}, u32[]{:S(2)}, u32[]{:S(2)}) collective-permute-start(bf16[128,1536]{1,0:T(8,128)(2,1)S(1)} %get-tuple-element.19), channel_id=1, source_target_pairs={{0,1},{1,0},{2,3},{3,2},{4,5},{5,4},{6,7},{7,6},{8,9},{9,8},{10,11... | collective-permute-start | bytes 1179656 | tf_op jit(solution)/shard_map/ppermute | solution.py:238
  116.0 27.6 %collective-permute-start.18 = (bf16[128,1536]{1,0:T(8,128)(2,1)S(1)}, bf16[128,1536]{1,0:T(8,128)(2,1)S(1)}, u32[]{:S(2)}, u32[]{:S(2)}) collective-permute-start(bf16[128,1536]{1,0:T(8,128)(2,1)S(1)} %get-tuple-element.21), channel_id=1, source_target_pairs={{0,1},{1,0},{2,3},{3,2},{4,5},{5,4},{6,7},{7,6},{8,9},{9,8},{10,11... | collective-permute-start | bytes 1179656 | tf_op jit(solution)/shard_map/ppermute | solution.py:238
  140.4 28.6 %collective-permute-start.23 = (bf16[256,512]{1,0:T(8,128)(2,1)S(1)}, bf16[256,512]{1,0:T(8,128)(2,1)S(1)}, u32[]{:S(2)}, u32[]{:S(2)}) collective-permute-start(bf16[256,512]{1,0:T(8,128)(2,1)S(1)} %get-tuple-element.10), channel_id=1, source_target_pairs={{8,0},{16,8},{24,16},{9,1},{17,9},{25,17},{10,2},{18,10},{26,18},{... | collective-permute-start | bytes 786440 | tf_op jit(solution)/shard_map/ppermute | solution.py:233
  142.3 33.1 %collective-permute-start.24 = (bf16[256,512]{1,0:T(8,128)(2,1)S(1)}, bf16[256,512]{1,0:T(8,128)(2,1)S(1)}, u32[]{:S(2)}, u32[]{:S(2)}) collective-permute-start(bf16[256,512]{1,0:T(8,128)(2,1)S(1)} %get-tuple-element.11), channel_id=1, source_target_pairs={{16,0},{24,8},{17,1},{25,9},{18,2},{26,10},{19,3},{27,11},{20,4},{... | collective-permute-start | bytes 786440 | tf_op jit(solution)/shard_map/ppermute | solution.py:234
  176.7 3.9 %collective-permute-start.25 = (bf16[128,512]{1,0:T(8,128)(2,1)S(1)}, bf16[128,512]{1,0:T(8,128)(2,1)S(1)}, u32[]{:S(2)}, u32[]{:S(2)}) collective-permute-start(bf16[128,512]{1,0:T(8,128)(2,1)S(1)} %slice.140), channel_id=1, source_target_pairs={{0,1},{1,0},{2,3},{3,2},{4,5},{5,4},{6,7},{7,6},{8,9},{9,8},{10,11... | collective-permute-start | bytes 393224 | tf_op jit(solution)/shard_map/ppermute | solution.py:245

commit v2 on v1

v2 whole, which is shorter than its diff:
```python
import functools
import math

import jax
import jax.numpy as jnp
from jax import lax
from jax.experimental import pallas as pl
from jax.experimental.pallas import tpu as pltpu
from jax.sharding import Mesh, PartitionSpec as P

QH = 24
KVH = 4
HD = 128
CAP = 30.0
NEAR = 2
GROUP = QH // KVH
ROWS = 256
HALF = 128
WIDE = GROUP * ROWS
TILE = 2 * ROWS
SLOTS = 9
BF = jnp.bfloat16
F32 = jnp.float32
SCALE = HD ** (-0.5)


def dot(a, b, over=(1, 0)):
    return lax.dot_general(a, b, (((over[0],), (over[1],)), ((), ())), preferred_element_type=F32)


def place_x_first(y):
    places = [(0, 0, 0), (1, 0, 4), (2, 0, 8)]
    for at, k in enumerate((1, 3, 2)):
        places += [(3 + at, 0, k), (3 + at, ROWS, 4 + k)]
    return places


def place_y_first(y):
    places = []
    for m in range(3):
        for at, k in enumerate((0, 1, 3, 2)):
            slot = 4 * m + k - jnp.where(y < k, 4, 0)
            places.append((m, at * ROWS, slot))
    return places


def attention_kernel(head, places_of, pieces, at_ref, len_ref, *refs):
    qm_ref, qo_ref, gm_ref, go_ref = refs[:4]
    piece_refs = refs[4:4 + pieces]
    att_ref, dq_ref, dkv_ref = refs[4 + pieces:7 + pieces]
    kv, qs, gs, expo, slope, out_s, dq_s, den, row_dot, ds_buf = refs[7 + pieces:]
    chip = at_ref[0]
    core = at_ref[1]
    row = lax.broadcasted_iota(jnp.int32, (TILE, 1), 0) % ROWS
    row_pos = chip * ROWS + row + jnp.where(row < HALF, core * HALF, (1 - core) * HALF - HALF)
    sub = lax.broadcasted_iota(jnp.int32, (1, ROWS), 1)
    key_off = sub + jnp.where(sub < HALF, core * HALF, (1 - core) * HALF - HALF)

    start = jnp.zeros((TILE, 1), jnp.int32)
    low = jnp.int32(0)
    high = jnp.int32(0)
    edge = jnp.int32(0)
    for j in range(8):
        edge = edge + len_ref[j]
        start = jnp.maximum(start, jnp.where(row_pos >= edge, edge, 0))
        low = jnp.maximum(low, jnp.where(chip * ROWS >= edge, edge, 0))
        high = jnp.maximum(high, jnp.where(chip * ROWS + ROWS - 1 >= edge, edge, 0))

    def needed(slot):
        return (slot <= chip) & ((chip - slot + 1) * ROWS > low)

    for piece, first, slot in places_of(lax.rem(chip, 4)):
        if isinstance(slot, int):
            kv[slot] = piece_refs[piece][first:first + ROWS, :]
        else:
            @pl.when((slot >= 0) & (slot < SLOTS))
            def _():
                kv[jnp.clip(slot, 0, SLOTS - 1)] = piece_refs[piece][first:first + ROWS, :]

    for j in range(GROUP):
        cols = slice((head * GROUP + j) * HD, (head * GROUP + j + 1) * HD)
        for part, (q_in, g_in) in enumerate(((qm_ref, gm_ref), (qo_ref, go_ref))):
            rows = slice(j * ROWS + part * HALF, j * ROWS + (part + 1) * HALF)
            qs[rows, :] = q_in[:, cols]
            gs[rows, :] = g_in[:, cols]
    out_s[...] = jnp.zeros_like(out_s)
    dq_s[...] = jnp.zeros_like(dq_s)
    den[...] = jnp.zeros_like(den)

    def forward(slot, masked):
        keys = kv[slot, :, :HD]
        values = kv[slot, :, HD:]
        for j in range(WIDE // TILE):
            rows = slice(j * TILE, (j + 1) * TILE)
            sq = jnp.tanh(dot(qs[rows, :], keys, (1, 1)) * (SCALE / CAP))
            e = jnp.exp2(sq * (CAP / math.log(2.0)))
            if masked:
                key_pos = (chip - slot) * ROWS + key_off
                e = jnp.where((key_pos >= start) & (key_pos <= row_pos), e, 0.0)
            eb = e.astype(BF)
            expo[slot, rows, :] = eb
            slope[slot, rows, :] = (e * (1.0 - sq * sq)).astype(BF)
            den[rows, :] += e[:, :HD] + e[:, HD:]
            out_s[rows, :] += dot(eb, values)

    def forward_step(slot, carry):
        plain = (slot > 0) & ((chip - slot) * ROWS >= high)

        @pl.when(needed(slot) & plain)
        def _():
            forward(slot, False)

        @pl.when(needed(slot) & jnp.logical_not(plain))
        def _():
            forward(slot, True)

        return carry

    lax.fori_loop(0, SLOTS, forward_step, 0)

    for j in range(GROUP):
        rows = slice(j * ROWS, (j + 1) * ROWS)
        inv = 1.0 / jnp.sum(den[rows, :], axis=1, keepdims=True)
        out = (out_s[rows, :] * inv).astype(BF)
        att_ref[:, j * HD:(j + 1) * HD] = out
        g = (gs[rows, :].astype(F32) * inv).astype(BF)
        gs[rows, :] = g
        row_dot[rows, :] = jnp.broadcast_to(
            jnp.sum(g.astype(F32) * out.astype(F32), axis=1, keepdims=True), (ROWS, HD)
        )

    def backward(slot):
        keys = kv[slot, :, :HD]
        values = kv[slot, :, HD:]
        for j in range(WIDE // TILE):
            rows = slice(j * TILE, (j + 1) * TILE)
            dp = dot(gs[rows, :], values, (1, 1))
            rd = row_dot[rows, :]
            ds = slope[slot, rows, :].astype(F32) * (dp - jnp.concatenate([rd, rd], axis=1))
            ds = ds.astype(BF)
            ds_buf[rows, :] = ds
            dq_s[rows, :] += dot(ds, keys)
        dkv_ref[slot, :, :HD] = (dot(ds_buf[...], qs[...], (0, 0)) * SCALE).astype(BF)
        dkv_ref[slot, :, HD:] = dot(expo[slot], gs[...], (0, 0)).astype(BF)

    def backward_step(slot, carry):
        @pl.when(needed(slot))
        def _():
            backward(slot)

        @pl.when(jnp.logical_not(needed(slot)))
        def _():
            dkv_ref[slot] = jnp.zeros((ROWS, 2 * HD), BF)

        return carry

    lax.fori_loop(0, SLOTS, backward_step, 0)

    for j in range(GROUP):
        rows = slice(j * ROWS, (j + 1) * ROWS)
        dq_ref[:, j * HD:(j + 1) * HD] = (dq_s[rows, :] * SCALE).astype(BF)


def attention(head, places_of, at, lengths, qm, qo, gm, go, *pieces):
    smem = pl.BlockSpec(memory_space=pltpu.SMEM)
    vmem = pl.BlockSpec(memory_space=pltpu.VMEM)
    return pl.pallas_call(
        functools.partial(attention_kernel, head, places_of, len(pieces)),
        out_shape=(
            jax.ShapeDtypeStruct((ROWS, GROUP * HD), BF),
            jax.ShapeDtypeStruct((ROWS, GROUP * HD), BF),
            jax.ShapeDtypeStruct((SLOTS, ROWS, 2 * HD), BF),
        ),
        in_specs=[smem] * 2 + [vmem] * (4 + len(pieces)),
        out_specs=(vmem,) * 3,
        scratch_shapes=[
            pltpu.VMEM((SLOTS, ROWS, 2 * HD), BF),
            pltpu.VMEM((WIDE, HD), BF),
            pltpu.VMEM((WIDE, HD), BF),
            pltpu.VMEM((SLOTS, WIDE, ROWS), BF),
            pltpu.VMEM((SLOTS, WIDE, ROWS), BF),
            pltpu.VMEM((WIDE, HD), F32),
            pltpu.VMEM((WIDE, HD), F32),
            pltpu.VMEM((WIDE, HD), F32),
            pltpu.VMEM((WIDE, HD), F32),
            pltpu.VMEM((WIDE, ROWS), BF),
        ],
        compiler_params=pltpu.CompilerParams(vmem_limit_bytes=40 * 1024 * 1024),
        cost_estimate=pl.CostEstimate(
            flops=12 * WIDE * HD * ROWS * SLOTS * 4, bytes_accessed=6_000_000, transcendentals=7_000_000
        ),
    )(at, lengths, qm, qo, gm, go, *pieces)


SWAP = [(0, 1), (1, 0)]


def ring(k):
    return [(i, (i + k) % 4) for i in range(4)]


def gather_x_first(own, y):
    r1 = lax.ppermute(own, "x", ring(1))
    r2 = lax.ppermute(own, "x", ring(2))
    three = jnp.concatenate([own, r1, r2], axis=0)
    pieces = [own, r1, r2]
    for k in (1, 3, 2):
        pair = lax.dynamic_slice_in_dim(three, jnp.where(y + k >= 4, ROWS, 0), 2 * ROWS, 0)
        pieces.append(lax.ppermute(pair, "y", ring(k)))
    return pieces


def gather_y_first(own):
    near = jnp.concatenate([own] + [lax.ppermute(own, "y", ring(k)) for k in (1, 3, 2)], axis=0)
    return [near, lax.ppermute(near, "x", ring(1)), lax.ppermute(near, "x", ring(2))]


def after(value, token):
    return lax.optimization_barrier((value, token))[0]


def send_y(dkv):
    return [
        lax.ppermute(jnp.concatenate([dkv[k], dkv[4 + k]], axis=0), "y", ring(4 - k)) for k in (1, 3, 2)
    ]


def scatter_y(dkv, received, y):
    sums = [dkv[0].astype(F32), dkv[4].astype(F32), dkv[8].astype(F32)]
    for k, got in zip((1, 3, 2), received):
        got = got.astype(F32)
        over = y + k >= 4
        first, second = got[:ROWS], got[ROWS:]
        sums[0] = sums[0] + jnp.where(over, 0.0, first)
        sums[1] = sums[1] + jnp.where(over, first, second)
        sums[2] = sums[2] + jnp.where(over, second, 0.0)
    return sums[0], sums[1].astype(BF), sums[2].astype(BF)


def scatter_x(sums):
    t1 = lax.ppermute(sums[1], "x", ring(3))
    t2 = lax.ppermute(sums[2], "x", ring(2))
    return sums[0] + t1.astype(F32) + t2.astype(F32)


def body(queries, key_rows, value_rows, upstream, loss_weight, doc_lengths):
    x, y, core = lax.axis_index("x"), lax.axis_index("y"), lax.axis_index("core")
    weights_row = loss_weight[0]
    mine_at, other_at = core, 1 - core

    def half(array, at):
        size = array.shape[1] // 2
        return lax.dynamic_slice_in_dim(array, at * size, size, 1)

    def heads(at):
        k, v = half(key_rows[0], at), half(value_rows[0], at)
        return jnp.concatenate([k[:, :HD], v[:, :HD], k[:, HD:], v[:, HD:]], axis=1)

    kv_other = lax.ppermute(heads(other_at), "core", SWAP)
    own = jnp.concatenate([heads(mine_at), kv_other], axis=0)
    first, second = own[:, :2 * HD], own[:, 2 * HD:]
    first_pieces = gather_x_first(first, y)
    second_pieces = gather_y_first(second)

    weighted = (upstream[0].astype(F32) * weights_row[:, None]).astype(BF)
    qm, gm = half(queries[0], mine_at), half(weighted, mine_at)
    qo = lax.ppermute(half(queries[0], other_at), "core", SWAP)
    go = lax.ppermute(half(weighted, other_at), "core", SWAP)

    at = jnp.stack([4 * x + y, core]).astype(jnp.int32)
    lengths = doc_lengths[0]
    att0, dq0, dkv0 = attention(0, place_x_first, at, lengths, qm, qo, gm, go, *first_pieces)
    att1, dq1, dkv1 = attention(1, place_y_first, at, lengths, qm, qo, gm, go, *second_pieces)

    sent0 = send_y(dkv0)
    sent0 = after(sent0, dkv1)
    sent1 = send_y(dkv1)
    sums0 = scatter_y(dkv0, sent0, y)

    total = jnp.full((8, 128), jnp.sum(weights_row))
    total = total + lax.ppermute(total, "core", SWAP)
    for axis, token in (("y", second_pieces[0]), ("x", att0), ("dp", att1)):
        total = after(total, token)
        total = total + sum(lax.ppermute(total, axis, ring(k)) for k in (1, 2, 3))
    inv = 1.0 / total[0, 0]

    grad0 = scatter_x(sums0)
    grad1 = scatter_x(scatter_y(dkv1, sent1, y))
    own_grad = jnp.concatenate([grad0, grad1], axis=1).astype(BF)

    def join(a, b, scale):
        got_a = lax.ppermute(a[HALF:], "core", SWAP)
        got_b = lax.ppermute(b[HALF:], "core", SWAP)
        a, b = a[:HALF], b[:HALF]
        low = jnp.concatenate([a, b, got_a, got_b], axis=1)
        high = jnp.concatenate([got_a, got_b, a, b], axis=1)
        both = jnp.where(core == 0, low, high)
        return both if scale is None else (both.astype(F32) * scale).astype(BF)

    out_rows = join(att0, att1, None)
    dq_rows = join(dq0, dq1, inv)
    got = lax.ppermute(own_grad[HALF:], "core", SWAP)
    mine = own_grad[:HALF]

    def side(at):
        a = [mine[:, at:at + HD], mine[:, at + 2 * HD:at + 3 * HD]]
        b = [got[:, at:at + HD], got[:, at + 2 * HD:at + 3 * HD]]
        both = jnp.where(core == 0, jnp.concatenate(a + b, axis=1), jnp.concatenate(b + a, axis=1))
        return (both.astype(F32) * inv).astype(BF)

    return (out_rows[None], dq_rows[None], side(0)[None], side(HD)[None])


def solution(mesh):
    split = Mesh(mesh.devices.reshape(4, 4, 4, 2), ("dp", "x", "y", "core"))
    ctx = ("x", "y", "core")
    rows = P("dp", ctx, None)
    return jax.shard_map(
        body,
        mesh=split,
        in_specs=(rows, rows, rows, rows, P("dp", ctx), P("dp", None)),
        out_specs=(rows, rows, rows, rows),
        check_vma=False,
    )
```

time: 183 us -> 134 us (0.73)
  the two profiles are of different devices: /device:TPU:3 before, /device:TPU:1 now
where the time goes in v2:
time: 134 us; the launch traced here: 135 us
  starting transfers between devices  78.2 us (58%)
  waiting for transfers between devices  32.9 us (25%)
  Pallas kernels  9.04 us (7%)
  other arithmetic  7.58 us (6%)
  local copies, waits for them, and re-layouts  5.96 us (4%)
  between operations  1.73 us (1%)
    ppermute x9, starting transfers between devices, body(): total = total + sum((lax.ppermute(total, axis, ring(k)) for k in (1, 2, 3)))  27.6 us
    ppermute x6, waiting for transfers between devices, send_y(): lax.ppermute(jnp.concatenate([dkv[k], dkv[4 + k]], axis=0), 'y', ring(4 -...  17.4 us
    ppermute x2, starting transfers between devices, scatter_x(): t1 = lax.ppermute(sums[1], 'x', ring(3))  13 us
    pallas_call x2, Pallas kernels, attention(): pl.pallas_call(functools.partial(attention_kernel, head, places_of, len(p...  9.04 us
    ppermute x2, waiting for transfers between devices, scatter_x(): t1 = lax.ppermute(sums[1], 'x', ring(3))  6.81 us
    ppermute x3, waiting for transfers between devices, gather_x_first(): pieces.append(lax.ppermute(pair, 'y', ring(k)))  5.97 us
    ppermute x2, starting transfers between devices, join(): got_a = lax.ppermute(a[HALF:], 'core', SWAP)  4.93 us
    ppermute x3, starting transfers between devices, gather_y_first(): lax.ppermute(own, 'y', ring(k))  4.38 us
  transfers between devices with their start and end apart: 38, of which 15 were waited for; matrix products, arithmetic and copies ran while one was open for 7% of the time, Pallas kernels for 7%

profile of v2, /device:TPU:1, one launch (start us, length us, event | category | flops | bytes accessed | tf_op | source)
XLA Modules:
  0.0 135.4 jit_solution(14592200559752131093)
XLA Ops:
  0.7 1.3 reduce_sum.9
  2.6 1.5 %collective-permute-start.17 = (f32[8,128]{1,0:T(8,128)S(1)}, f32[8,128]{1,0:T(8,128)S(1)}, u32[]{:S(2)}, u32[]{:S(2)}) collective-permute-start(f32[8,128]{1,0:T(8,128)S(1)} %broadcast_in_dim.23), channel_id=1, source_target_pairs={{0,1},{1,0},{2,3},{3,2},{4,5},{5,4},{6,7},{7,6},{8,9},{9,8},{10,11... | collective-permute-start | bytes 12296 | tf_op jit(solution)/shard_map/ppermute | solution.py:281
  7.7 2.9 %collective-permute-start.4 = (bf16[256,256]{1,0:T(8,128)(2,1)S(1)}, bf16[256,256]{1,0:T(8,128)(2,1)S(1)}, u32[]{:S(2)}, u32[]{:S(2)}) collective-permute-start(bf16[256,256]{1,0:T(8,128)(2,1)S(1)} %get-tuple-element.59.refs_4_), channel_id=1, source_target_pairs={{0,16},{8,24},{16,0},{24,8},{1,17},{9,25},{17,1},{25,9},{2,18},{10... | collective-permute-start | bytes 393224 | tf_op jit(solution)/shard_map/ppermute | solution.py:204
  10.9 2.9 %collective-permute-start.10 = (bf16[256,256]{1,0:T(8,128)(2,1)S(1)}, bf16[256,256]{1,0:T(8,128)(2,1)S(1)}, u32[]{:S(2)}, u32[]{:S(2)}) collective-permute-start(bf16[256,256]{1,0:T(8,128)(2,1)S(1)} %get-tuple-element.60), channel_id=1, source_target_pairs={{0,4},{2,6},{4,0},{6,2},{1,5},{3,7},{5,1},{7,3},{8,12},{10,14},{12... | collective-permute-start | bytes 393224 | tf_op jit(solution)/shard_map/ppermute | solution.py:214
  16.2 3.0 %collective-permute-start.1 = (bf16[128,1536]{1,0:T(8,128)(2,1)}, bf16[128,1536]{1,0:T(8,128)(2,1)S(1)}, u32[]{:S(2)}, u32[]{:S(2)}) collective-permute-start(bf16[128,1536]{1,0:T(8,128)(2,1)} %get-tuple-element.44), channel_id=1, source_target_pairs={{0,1},{1,0},{2,3},{3,2},{4,5},{5,4},{6,7},{7,6},{8,9},{9,8},{10,11... | collective-permute-start | bytes 1179656 | tf_op jit(solution)/shard_map/ppermute | solution.py:268
  19.3 2.2 %collective-permute-start = (bf16[128,1536]{1,0:T(8,128)(2,1)}, bf16[128,1536]{1,0:T(8,128)(2,1)S(1)}, u32[]{:S(2)}, u32[]{:S(2)}) collective-permute-start(bf16[128,1536]{1,0:T(8,128)(2,1)} %get-tuple-element.46), channel_id=1, source_target_pairs={{0,1},{1,0},{2,3},{3,2},{4,5},{5,4},{6,7},{7,6},{8,9},{9,8},{10,11... | collective-permute-start | bytes 1179656 | tf_op jit(solution)/shard_map/ppermute | solution.py:267
  21.5 2.5 %collective-permute-start.20 = (f32[8,128]{1,0:T(8,128)S(1)}, f32[8,128]{1,0:T(8,128)S(1)}, u32[]{:S(2)}, u32[]{:S(2)}) collective-permute-start(f32[8,128]{1,0:T(8,128)S(1)} %broadcast_add_fusion), channel_id=1, source_target_pairs={{0,6},{2,0},{4,2},{6,4},{1,7},{3,1},{5,3},{7,5},{8,14},{10,8},{12,... | collective-permute-start | bytes 12296 | tf_op jit(solution)/shard_map/ppermute | solution.py:284
  25.6 2.3 %collective-permute-start.7 = (bf16[512,256]{1,0:T(8,128)(2,1)}, bf16[512,256]{1,0:T(8,128)(2,1)S(1)}, u32[]{:S(2)}, u32[]{:S(2)}) collective-permute-start(bf16[512,256]{1,0:T(8,128)(2,1)} %get-tuple-element.56), channel_id=1, source_target_pairs={{0,4},{2,6},{4,0},{6,2},{1,5},{3,7},{5,1},{7,3},{8,12},{10,14},{12... | collective-permute-start | bytes 786440 | tf_op jit(solution)/shard_map/ppermute | solution.py:209
  27.9 2.0 %collective-permute-start.6 = (bf16[512,256]{1,0:T(8,128)(2,1)}, bf16[512,256]{1,0:T(8,128)(2,1)S(1)}, u32[]{:S(2)}, u32[]{:S(2)}) collective-permute-start(bf16[512,256]{1,0:T(8,128)(2,1)} %get-tuple-element.57), channel_id=1, source_target_pairs={{0,6},{2,0},{4,2},{6,4},{1,7},{3,1},{5,3},{7,5},{8,14},{10,8},{12,... | collective-permute-start | bytes 786440 | tf_op jit(solution)/shard_map/ppermute | solution.py:209
  31.3 1.7 %collective-permute-start.12 = (bf16[1024,256]{1,0:T(8,128)(2,1)S(1)}, bf16[1024,256]{1,0:T(8,128)(2,1)S(1)}, u32[]{:S(2)}, u32[]{:S(2)}) collective-permute-start(bf16[1024,256]{1,0:T(8,128)(2,1)S(1)} %pad_maximum_fusion.refs_4_), channel_id=1, source_target_pairs={{0,16},{8,24},{16,0},{24,8},{1,17},{9,25},{17,1},{25,9},{2,18},{10... | collective-permute-start | bytes 1572872 | tf_op jit(solution)/shard_map/ppermute | solution.py:215
  34.3 5.9 %collective-permute-done.6.refs_8_ = bf16[512,256]{1,0:T(8,128)(2,1)S(1)} collective-permute-done((bf16[512,256]{1,0:T(8,128)(2,1)}, bf16[512,256]{1,0:T(8,128)(2,1)S(1)}, u32[]{:S(2)}, u32[]{:S(2)}) %collective-permute-start.6) | collective-permute-done | bytes 262176 | tf_op jit(solution)/shard_map/ppermute | solution.py:209
  40.3 4.5 %shard_map.93 = (bf16[256,768]{1,0:T(8,128)(2,1)S(1)}, bf16[256,768]{1,0:T(8,128)(2,1)S(1)}, bf16[9,256,256]{2,1,0:T(8,128)(2,1)S(1)}) custom-call(s32[2]{0:T(128)S(1)} %pad_add_fusion.at_ref, s32[8]{0:T(128)S(1)} %bitcast.90, bf16[128,1536]{1,0:T(8,128)(2,1)S(1)} %get-tuple-element.47.refs_0_, bf16[128,1536]{1,0:T(8,128)(2,1)S(1)} %collective-permute-done.refs_1_, ...), custom_call_target="tpu_custom_call" | custom-call | flops 21743271936 | bytes 6000000 | tf_op jit(solution)/shard_map/pallas_call | solution.py:167
  44.7 18.7 %collective-permute-start.23 = (f32[8,128]{1,0:T(8,128)S(1)}, f32[8,128]{1,0:T(8,128)S(1)}, u32[]{:S(2)}, u32[]{:S(2)}) collective-permute-start(f32[8,128]{1,0:T(8,128)S(1)} %add_add_fusion.2), channel_id=1, source_target_pairs={{0,24},{8,0},{16,8},{24,16},{1,25},{9,1},{17,9},{25,17},{2,26},{10... | collective-permute-start | bytes 12296 | tf_op jit(solution)/shard_map/ppermute | solution.py:284
  64.3 2.1 %collective-permute-start.15 = (bf16[128,768]{1,0:T(8,128)(2,1)S(1)}, bf16[128,768]{1,0:T(8,128)(2,1)S(1)}, u32[]{:S(2)}, u32[]{:S(2)}) collective-permute-start(bf16[128,768]{1,0:T(8,128)(2,1)S(1)} %get-tuple-element.49), channel_id=1, source_target_pairs={{0,1},{1,0},{2,3},{3,2},{4,5},{5,4},{6,7},{7,6},{8,9},{9,8},{10,11... | collective-permute-start | bytes 589832 | tf_op jit(solution)/shard_map/ppermute | solution.py:292
  67.4 2.8 %collective-permute-start.13 = (bf16[128,768]{1,0:T(8,128)(2,1)S(1)}, bf16[128,768]{1,0:T(8,128)(2,1)S(1)}, u32[]{:S(2)}, u32[]{:S(2)}) collective-permute-start(bf16[128,768]{1,0:T(8,128)(2,1)S(1)} %get-tuple-element.53), channel_id=1, source_target_pairs={{0,1},{1,0},{2,3},{3,2},{4,5},{5,4},{6,7},{7,6},{8,9},{9,8},{10,11... | collective-permute-start | bytes 589832 | tf_op jit(solution)/shard_map/ppermute | solution.py:292
  70.2 1.5 %collective-permute-start.28 = (bf16[512,256]{1,0:T(8,128)(2,1)S(1)}, bf16[512,256]{1,0:T(8,128)(2,1)S(1)}, u32[]{:S(2)}, u32[]{:S(2)}) collective-permute-start(bf16[512,256]{1,0:T(8,128)(2,1)S(1)} %pad_maximum_fusion.4), channel_id=1, source_target_pairs={{0,2},{2,4},{4,6},{6,0},{1,3},{3,5},{5,7},{7,1},{8,10},{10,12},{12... | collective-permute-start | bytes 786440 | tf_op jit(solution)/shard_map/ppermute | solution.py:224
  71.7 4.6 %shard_map.94 = (bf16[256,768]{1,0:T(8,128)(2,1)S(1)}, bf16[256,768]{1,0:T(8,128)(2,1)S(1)}, bf16[9,256,256]{2,1,0:T(8,128)(2,1)S(1)}) custom-call(s32[2]{0:T(128)S(1)} %pad_add_fusion.at_ref, s32[8]{0:T(128)S(1)} %bitcast.91, bf16[128,1536]{1,0:T(8,128)(2,1)S(1)} %get-tuple-element.47.refs_0_, bf16[128,1536]{1,0:T(8,128)(2,1)S(1)} %collective-permute-done.refs_1_, ...), custom_call_target="tpu_custom_call" | custom-call | flops 21743271936 | bytes 6000000 | tf_op jit(solution)/shard_map/pallas_call | solution.py:167
  76.5 1.7 %collective-permute-done.27 = bf16[512,256]{1,0:T(8,128)(2,1)S(1)} collective-permute-done((bf16[512,256]{1,0:T(8,128)(2,1)S(1)}, bf16[512,256]{1,0:T(8,128)(2,1)S(1)}, u32[]{:S(2)}, u32[]{:S(2)}) %collective-permute-start.27) | collective-permute-done | bytes 262176 | tf_op jit(solution)/shard_map/ppermute | solution.py:224
  78.1 1.5 %collective-permute-start.26 = (f32[8,128]{1,0:T(8,128)S(1)}, f32[8,128]{1,0:T(8,128)S(1)}, u32[]{:S(2)}, u32[]{:S(2)}) collective-permute-start(f32[8,128]{1,0:T(8,128)S(1)} %add_add_fusion.1), channel_id=1, source_target_pairs={{0,96},{32,0},{64,32},{96,64},{1,97},{33,1},{65,33},{97,65},{2,98}... | collective-permute-start | bytes 12296 | tf_op jit(solution)/shard_map/ppermute | solution.py:284
  79.6 5.4 %collective-permute-done.28 = bf16[512,256]{1,0:T(8,128)(2,1)S(1)} collective-permute-done((bf16[512,256]{1,0:T(8,128)(2,1)S(1)}, bf16[512,256]{1,0:T(8,128)(2,1)S(1)}, u32[]{:S(2)}, u32[]{:S(2)}) %collective-permute-start.28) | collective-permute-done | bytes 262176 | tf_op jit(solution)/shard_map/ppermute | solution.py:224
  85.0 3.6 %collective-permute-start.25 = (f32[8,128]{1,0:T(8,128)S(1)}, f32[8,128]{1,0:T(8,128)S(1)}, u32[]{:S(2)}, u32[]{:S(2)}) collective-permute-start(f32[8,128]{1,0:T(8,128)S(1)} %add_add_fusion.1), channel_id=1, source_target_pairs={{0,64},{32,96},{64,0},{96,32},{1,65},{33,97},{65,1},{97,33},{2,66}... | collective-permute-start | bytes 12296 | tf_op jit(solution)/shard_map/ppermute | solution.py:284
  89.0 1.7 %collective-permute-start.16 = (bf16[128,768]{1,0:T(8,128)(2,1)S(1)}, bf16[128,768]{1,0:T(8,128)(2,1)S(1)}, u32[]{:S(2)}, u32[]{:S(2)}) collective-permute-start(bf16[128,768]{1,0:T(8,128)(2,1)S(1)} %get-tuple-element.51), channel_id=1, source_target_pairs={{0,1},{1,0},{2,3},{3,2},{4,5},{5,4},{6,7},{7,6},{8,9},{9,8},{10,11... | collective-permute-start | bytes 589832 | tf_op jit(solution)/shard_map/ppermute | solution.py:293
  90.8 8.7 %collective-permute-start.30 = (bf16[256,256]{1,0:T(8,128)(2,1)S(1)}, bf16[256,256]{1,0:T(8,128)(2,1)S(1)}, u32[]{:S(2)}, u32[]{:S(2)}) collective-permute-start(bf16[256,256]{1,0:T(8,128)(2,1)S(1)} %get-tuple-element.28), channel_id=1, source_target_pairs={{0,24},{8,0},{16,8},{24,16},{1,25},{9,1},{17,9},{25,17},{2,26},{10... | collective-permute-start | bytes 393224 | tf_op jit(solution)/shard_map/ppermute | solution.py:241
  100.6 2.9 %collective-permute-done.30 = bf16[256,256]{1,0:T(8,128)(2,1)S(1)} collective-permute-done((bf16[256,256]{1,0:T(8,128)(2,1)S(1)}, bf16[256,256]{1,0:T(8,128)(2,1)S(1)}, u32[]{:S(2)}, u32[]{:S(2)}) %collective-permute-start.30) | collective-permute-done | bytes 131104 | tf_op jit(solution)/shard_map/ppermute | solution.py:241
  103.5 2.4 %collective-permute-start.14 = (bf16[128,768]{1,0:T(8,128)(2,1)S(1)}, bf16[128,768]{1,0:T(8,128)(2,1)S(1)}, u32[]{:S(2)}, u32[]{:S(2)}) collective-permute-start(bf16[128,768]{1,0:T(8,128)(2,1)S(1)} %get-tuple-element.55), channel_id=1, source_target_pairs={{0,1},{1,0},{2,3},{3,2},{4,5},{5,4},{6,7},{7,6},{8,9},{9,8},{10,11... | collective-permute-start | bytes 589832 | tf_op jit(solution)/shard_map/ppermute | solution.py:293
  106.1 2.1 %collective-permute-start.34 = (bf16[512,256]{1,0:T(8,128)(2,1)S(1)}, bf16[512,256]{1,0:T(8,128)(2,1)S(1)}, u32[]{:S(2)}, u32[]{:S(2)}) collective-permute-start(bf16[512,256]{1,0:T(8,128)(2,1)S(1)} %pad_maximum_fusion.8), channel_id=1, source_target_pairs={{0,4},{2,6},{4,0},{6,2},{1,5},{3,7},{5,1},{7,3},{8,12},{10,14},{12... | collective-permute-start | bytes 786440 | tf_op jit(solution)/shard_map/ppermute | solution.py:224
  110.0 5.6 %collective-permute-done.33 = bf16[512,256]{1,0:T(8,128)(2,1)S(1)} collective-permute-done((bf16[512,256]{1,0:T(8,128)(2,1)S(1)}, bf16[512,256]{1,0:T(8,128)(2,1)S(1)}, u32[]{:S(2)}, u32[]{:S(2)}) %collective-permute-start.33) | collective-permute-done | bytes 262176 | tf_op jit(solution)/shard_map/ppermute | solution.py:224
  115.6 2.7 %collective-permute-done.34 = bf16[512,256]{1,0:T(8,128)(2,1)S(1)} collective-permute-done((bf16[512,256]{1,0:T(8,128)(2,1)S(1)}, bf16[512,256]{1,0:T(8,128)(2,1)S(1)}, u32[]{:S(2)}, u32[]{:S(2)}) %collective-permute-start.34) | collective-permute-done | bytes 262176 | tf_op jit(solution)/shard_map/ppermute | solution.py:224
  118.4 2.0 %collective-permute-done.32 = bf16[512,256]{1,0:T(8,128)(2,1)S(1)} collective-permute-done((bf16[512,256]{1,0:T(8,128)(2,1)S(1)}, bf16[512,256]{1,0:T(8,128)(2,1)S(1)}, u32[]{:S(2)}, u32[]{:S(2)}) %collective-permute-start.32) | collective-permute-done | bytes 262176 | tf_op jit(solution)/shard_map/ppermute | solution.py:224
  120.6 4.3 %collective-permute-start.35 = (bf16[256,256]{1,0:T(8,128)(2,1)S(1)}, bf16[256,256]{1,0:T(8,128)(2,1)S(1)}, u32[]{:S(2)}, u32[]{:S(2)}) collective-permute-start(bf16[256,256]{1,0:T(8,128)(2,1)S(1)} %get-tuple-element.30), channel_id=1, source_target_pairs={{0,24},{8,0},{16,8},{24,16},{1,25},{9,1},{17,9},{25,17},{2,26},{10... | collective-permute-start | bytes 393224 | tf_op jit(solution)/shard_map/ppermute | solution.py:241
  126.1 3.9 %collective-permute-done.35 = bf16[256,256]{1,0:T(8,128)(2,1)S(1)} collective-permute-done((bf16[256,256]{1,0:T(8,128)(2,1)S(1)}, bf16[256,256]{1,0:T(8,128)(2,1)S(1)}, u32[]{:S(2)}, u32[]{:S(2)}) %collective-permute-start.35) | collective-permute-done | bytes 131104 | tf_op jit(solution)/shard_map/ppermute | solution.py:241
  130.4 2.6 %collective-permute-start.37 = (bf16[128,512]{1,0:T(8,128)(2,1)S(1)}, bf16[128,512]{1,0:T(8,128)(2,1)S(1)}, u32[]{:S(2)}, u32[]{:S(2)}) collective-permute-start(bf16[128,512]{1,0:T(8,128)(2,1)S(1)} %pad_maximum_fusion.9), channel_id=1, source_target_pairs={{0,1},{1,0},{2,3},{3,2},{4,5},{5,4},{6,7},{7,6},{8,9},{9,8},{10,11... | collective-permute-start | bytes 393224 | tf_op jit(solution)/shard_map/ppermute | solution.py:302
  (110 shorter events, 20.2 us)
Async XLA Ops:
  2.6 11.9 %collective-permute-start.17 = (f32[8,128]{1,0:T(8,128)S(1)}, f32[8,128]{1,0:T(8,128)S(1)}, u32[]{:S(2)}, u32[]{:S(2)}) collective-permute-start(f32[8,128]{1,0:T(8,128)S(1)} %broadcast_in_dim.23), channel_id=1, source_target_pairs={{0,1},{1,0},{2,3},{3,2},{4,5},{5,4},{6,7},{7,6},{8,9},{9,8},{10,11... | collective-permute-start | bytes 12296 | tf_op jit(solution)/shard_map/ppermute | solution.py:281
  7.7 16.3 %collective-permute-start.4 = (bf16[256,256]{1,0:T(8,128)(2,1)S(1)}, bf16[256,256]{1,0:T(8,128)(2,1)S(1)}, u32[]{:S(2)}, u32[]{:S(2)}) collective-permute-start(bf16[256,256]{1,0:T(8,128)(2,1)S(1)} %get-tuple-element.59.refs_4_), channel_id=1, source_target_pairs={{0,16},{8,24},{16,0},{24,8},{1,17},{9,25},{17,1},{25,9},{2,18},{10... | collective-permute-start | bytes 393224 | tf_op jit(solution)/shard_map/ppermute | solution.py:204
  10.6 13.8 %collective-permute-start.3 = (bf16[256,256]{1,0:T(8,128)(2,1)S(1)}, bf16[256,256]{1,0:T(8,128)(2,1)S(1)}, u32[]{:S(2)}, u32[]{:S(2)}) collective-permute-start(bf16[256,256]{1,0:T(8,128)(2,1)S(1)} %get-tuple-element.59.refs_4_), channel_id=1, source_target_pairs={{0,8},{8,16},{16,24},{24,0},{1,9},{9,17},{17,25},{25,1},{2,10},{10... | collective-permute-start | bytes 393224 | tf_op jit(solution)/shard_map/ppermute | solution.py:203
  10.9 5.3 %collective-permute-start.10 = (bf16[256,256]{1,0:T(8,128)(2,1)S(1)}, bf16[256,256]{1,0:T(8,128)(2,1)S(1)}, u32[]{:S(2)}, u32[]{:S(2)}) collective-permute-start(bf16[256,256]{1,0:T(8,128)(2,1)S(1)} %get-tuple-element.60), channel_id=1, source_target_pairs={{0,4},{2,6},{4,0},{6,2},{1,5},{3,7},{5,1},{7,3},{8,12},{10,14},{12... | collective-permute-start | bytes 393224 | tf_op jit(solution)/shard_map/ppermute | solution.py:214
  13.8 5.5 %collective-permute-start.9 = (bf16[256,256]{1,0:T(8,128)(2,1)S(1)}, bf16[256,256]{1,0:T(8,128)(2,1)S(1)}, u32[]{:S(2)}, u32[]{:S(2)}) collective-permute-start(bf16[256,256]{1,0:T(8,128)(2,1)S(1)} %get-tuple-element.60), channel_id=1, source_target_pairs={{0,6},{2,0},{4,2},{6,4},{1,7},{3,1},{5,3},{7,5},{8,14},{10,8},{12,... | collective-permute-start | bytes 393224 | tf_op jit(solution)/shard_map/ppermute | solution.py:214
  14.6 6.9 %collective-permute-start.8 = (bf16[256,256]{1,0:T(8,128)(2,1)S(1)}, bf16[256,256]{1,0:T(8,128)(2,1)S(1)}, u32[]{:S(2)}, u32[]{:S(2)}) collective-permute-start(bf16[256,256]{1,0:T(8,128)(2,1)S(1)} %get-tuple-element.60), channel_id=1, source_target_pairs={{0,2},{2,4},{4,6},{6,0},{1,3},{3,5},{5,7},{7,1},{8,10},{10,12},{12... | collective-permute-start | bytes 393224 | tf_op jit(solution)/shard_map/ppermute | solution.py:214
  16.2 15.1 %collective-permute-start.1 = (bf16[128,1536]{1,0:T(8,128)(2,1)}, bf16[128,1536]{1,0:T(8,128)(2,1)S(1)}, u32[]{:S(2)}, u32[]{:S(2)}) collective-permute-start(bf16[128,1536]{1,0:T(8,128)(2,1)} %get-tuple-element.44), channel_id=1, source_target_pairs={{0,1},{1,0},{2,3},{3,2},{4,5},{5,4},{6,7},{7,6},{8,9},{9,8},{10,11... | collective-permute-start | bytes 1179656 | tf_op jit(solution)/shard_map/ppermute | solution.py:268
  19.3 13.8 %collective-permute-start = (bf16[128,1536]{1,0:T(8,128)(2,1)}, bf16[128,1536]{1,0:T(8,128)(2,1)S(1)}, u32[]{:S(2)}, u32[]{:S(2)}) collective-permute-start(bf16[128,1536]{1,0:T(8,128)(2,1)} %get-tuple-element.46), channel_id=1, source_target_pairs={{0,1},{1,0},{2,3},{3,2},{4,5},{5,4},{6,7},{7,6},{8,9},{9,8},{10,11... | collective-permute-start | bytes 1179656 | tf_op jit(solution)/shard_map/ppermute | solution.py:267
  24.3 5.6 %collective-permute-start.18 = (f32[8,128]{1,0:T(8,128)S(1)}, f32[8,128]{1,0:T(8,128)S(1)}, u32[]{:S(2)}, u32[]{:S(2)}) collective-permute-start(f32[8,128]{1,0:T(8,128)S(1)} %broadcast_add_fusion), channel_id=1, source_target_pairs={{0,2},{2,4},{4,6},{6,0},{1,3},{3,5},{5,7},{7,1},{8,10},{10,12},{12... | collective-permute-start | bytes 12296 | tf_op jit(solution)/shard_map/ppermute | solution.py:284
  25.6 8.7 %collective-permute-start.7 = (bf16[512,256]{1,0:T(8,128)(2,1)}, bf16[512,256]{1,0:T(8,128)(2,1)S(1)}, u32[]{:S(2)}, u32[]{:S(2)}) collective-permute-start(bf16[512,256]{1,0:T(8,128)(2,1)} %get-tuple-element.56), channel_id=1, source_target_pairs={{0,4},{2,6},{4,0},{6,2},{1,5},{3,7},{5,1},{7,3},{8,12},{10,14},{12... | collective-permute-start | bytes 786440 | tf_op jit(solution)/shard_map/ppermute | solution.py:209
  27.9 12.2 %collective-permute-start.6 = (bf16[512,256]{1,0:T(8,128)(2,1)}, bf16[512,256]{1,0:T(8,128)(2,1)S(1)}, u32[]{:S(2)}, u32[]{:S(2)}) collective-permute-start(bf16[512,256]{1,0:T(8,128)(2,1)} %get-tuple-element.57), channel_id=1, source_target_pairs={{0,6},{2,0},{4,2},{6,4},{1,7},{3,1},{5,3},{7,5},{8,14},{10,8},{12,... | collective-permute-start | bytes 786440 | tf_op jit(solution)/shard_map/ppermute | solution.py:209
  30.0 10.3 %collective-permute-start.5 = (bf16[512,256]{1,0:T(8,128)(2,1)S(1)}, bf16[512,256]{1,0:T(8,128)(2,1)S(1)}, u32[]{:S(2)}, u32[]{:S(2)}) collective-permute-start(bf16[512,256]{1,0:T(8,128)(2,1)S(1)} %get-tuple-element.58), channel_id=1, source_target_pairs={{0,2},{2,4},{4,6},{6,0},{1,3},{3,5},{5,7},{7,1},{8,10},{10,12},{12... | collective-permute-start | bytes 786440 | tf_op jit(solution)/shard_map/ppermute | solution.py:209
  31.3 38.9 %collective-permute-start.12 = (bf16[1024,256]{1,0:T(8,128)(2,1)S(1)}, bf16[1024,256]{1,0:T(8,128)(2,1)S(1)}, u32[]{:S(2)}, u32[]{:S(2)}) collective-permute-start(bf16[1024,256]{1,0:T(8,128)(2,1)S(1)} %pad_maximum_fusion.refs_4_), channel_id=1, source_target_pairs={{0,16},{8,24},{16,0},{24,8},{1,17},{9,25},{17,1},{25,9},{2,18},{10... | collective-permute-start | bytes 1572872 | tf_op jit(solution)/shard_map/ppermute | solution.py:215
  33.1 38.7 %collective-permute-start.11 = (bf16[1024,256]{1,0:T(8,128)(2,1)S(1)}, bf16[1024,256]{1,0:T(8,128)(2,1)S(1)}, u32[]{:S(2)}, u32[]{:S(2)}) collective-permute-start(bf16[1024,256]{1,0:T(8,128)(2,1)S(1)} %pad_maximum_fusion.refs_4_), channel_id=1, source_target_pairs={{0,8},{8,16},{16,24},{24,0},{1,9},{9,17},{17,25},{25,1},{2,10},{10... | collective-permute-start | bytes 1572872 | tf_op jit(solution)/shard_map/ppermute | solution.py:215
  44.7 19.6 %collective-permute-start.23 = (f32[8,128]{1,0:T(8,128)S(1)}, f32[8,128]{1,0:T(8,128)S(1)}, u32[]{:S(2)}, u32[]{:S(2)}) collective-permute-start(f32[8,128]{1,0:T(8,128)S(1)} %add_add_fusion.2), channel_id=1, source_target_pairs={{0,24},{8,0},{16,8},{24,16},{1,25},{9,1},{17,9},{25,17},{2,26},{10... | collective-permute-start | bytes 12296 | tf_op jit(solution)/shard_map/ppermute | solution.py:284
  63.4 6.8 %collective-permute-start.21 = (f32[8,128]{1,0:T(8,128)S(1)}, f32[8,128]{1,0:T(8,128)S(1)}, u32[]{:S(2)}, u32[]{:S(2)}) collective-permute-start(f32[8,128]{1,0:T(8,128)S(1)} %add_add_fusion.2), channel_id=1, source_target_pairs={{0,8},{8,16},{16,24},{24,0},{1,9},{9,17},{17,25},{25,1},{2,10},{10... | collective-permute-start | bytes 12296 | tf_op jit(solution)/shard_map/ppermute | solution.py:284
  64.3 60.7 %collective-permute-start.15 = (bf16[128,768]{1,0:T(8,128)(2,1)S(1)}, bf16[128,768]{1,0:T(8,128)(2,1)S(1)}, u32[]{:S(2)}, u32[]{:S(2)}) collective-permute-start(bf16[128,768]{1,0:T(8,128)(2,1)S(1)} %get-tuple-element.49), channel_id=1, source_target_pairs={{0,1},{1,0},{2,3},{3,2},{4,5},{5,4},{6,7},{7,6},{8,9},{9,8},{10,11... | collective-permute-start | bytes 589832 | tf_op jit(solution)/shard_map/ppermute | solution.py:292
  67.4 38.7 %collective-permute-start.13 = (bf16[128,768]{1,0:T(8,128)(2,1)S(1)}, bf16[128,768]{1,0:T(8,128)(2,1)S(1)}, u32[]{:S(2)}, u32[]{:S(2)}) collective-permute-start(bf16[128,768]{1,0:T(8,128)(2,1)S(1)} %get-tuple-element.53), channel_id=1, source_target_pairs={{0,1},{1,0},{2,3},{3,2},{4,5},{5,4},{6,7},{7,6},{8,9},{9,8},{10,11... | collective-permute-start | bytes 589832 | tf_op jit(solution)/shard_map/ppermute | solution.py:292
  70.2 7.9 %collective-permute-start.27 = (bf16[512,256]{1,0:T(8,128)(2,1)S(1)}, bf16[512,256]{1,0:T(8,128)(2,1)S(1)}, u32[]{:S(2)}, u32[]{:S(2)}) collective-permute-start(bf16[512,256]{1,0:T(8,128)(2,1)S(1)} %pad_maximum_fusion.3), channel_id=1, source_target_pairs={{0,6},{2,0},{4,2},{6,4},{1,7},{3,1},{5,3},{7,5},{8,14},{10,8},{12,... | collective-permute-start | bytes 786440 | tf_op jit(solution)/shard_map/ppermute | solution.py:224
  70.2 14.8 %collective-permute-start.28 = (bf16[512,256]{1,0:T(8,128)(2,1)S(1)}, bf16[512,256]{1,0:T(8,128)(2,1)S(1)}, u32[]{:S(2)}, u32[]{:S(2)}) collective-permute-start(bf16[512,256]{1,0:T(8,128)(2,1)S(1)} %pad_maximum_fusion.4), channel_id=1, source_target_pairs={{0,2},{2,4},{4,6},{6,0},{1,3},{3,5},{5,7},{7,1},{8,10},{10,12},{12... | collective-permute-start | bytes 786440 | tf_op jit(solution)/shard_map/ppermute | solution.py:224
  71.7 16.9 %collective-permute-start.29 = (bf16[512,256]{1,0:T(8,128)(2,1)S(1)}, bf16[512,256]{1,0:T(8,128)(2,1)S(1)}, u32[]{:S(2)}, u32[]{:S(2)}) collective-permute-start(bf16[512,256]{1,0:T(8,128)(2,1)S(1)} %pad_maximum_fusion.5), channel_id=1, source_target_pairs={{0,4},{2,6},{4,0},{6,2},{1,5},{3,7},{5,1},{7,3},{8,12},{10,14},{12... | collective-permute-start | bytes 786440 | tf_op jit(solution)/shard_map/ppermute | solution.py:224
  78.1 10.9 %collective-permute-start.26 = (f32[8,128]{1,0:T(8,128)S(1)}, f32[8,128]{1,0:T(8,128)S(1)}, u32[]{:S(2)}, u32[]{:S(2)}) collective-permute-start(f32[8,128]{1,0:T(8,128)S(1)} %add_add_fusion.1), channel_id=1, source_target_pairs={{0,96},{32,0},{64,32},{96,64},{1,97},{33,1},{65,33},{97,65},{2,98}... | collective-permute-start | bytes 12296 | tf_op jit(solution)/shard_map/ppermute | solution.py:284
  85.0 5.7 %collective-permute-start.25 = (f32[8,128]{1,0:T(8,128)S(1)}, f32[8,128]{1,0:T(8,128)S(1)}, u32[]{:S(2)}, u32[]{:S(2)}) collective-permute-start(f32[8,128]{1,0:T(8,128)S(1)} %add_add_fusion.1), channel_id=1, source_target_pairs={{0,64},{32,96},{64,0},{96,32},{1,65},{33,97},{65,1},{97,33},{2,66}... | collective-permute-start | bytes 12296 | tf_op jit(solution)/shard_map/ppermute | solution.py:284
  88.6 10.8 %collective-permute-start.24 = (f32[8,128]{1,0:T(8,128)S(1)}, f32[8,128]{1,0:T(8,128)S(1)}, u32[]{:S(2)}, u32[]{:S(2)}) collective-permute-start(f32[8,128]{1,0:T(8,128)S(1)} %add_add_fusion.1), channel_id=1, source_target_pairs={{0,32},{32,64},{64,96},{96,0},{1,33},{33,65},{65,97},{97,1},{2,34}... | collective-permute-start | bytes 12296 | tf_op jit(solution)/shard_map/ppermute | solution.py:284
  89.0 35.9 %collective-permute-start.16 = (bf16[128,768]{1,0:T(8,128)(2,1)S(1)}, bf16[128,768]{1,0:T(8,128)(2,1)S(1)}, u32[]{:S(2)}, u32[]{:S(2)}) collective-permute-start(bf16[128,768]{1,0:T(8,128)(2,1)S(1)} %get-tuple-element.51), channel_id=1, source_target_pairs={{0,1},{1,0},{2,3},{3,2},{4,5},{5,4},{6,7},{7,6},{8,9},{9,8},{10,11... | collective-permute-start | bytes 589832 | tf_op jit(solution)/shard_map/ppermute | solution.py:293
  90.8 12.8 %collective-permute-start.30 = (bf16[256,256]{1,0:T(8,128)(2,1)S(1)}, bf16[256,256]{1,0:T(8,128)(2,1)S(1)}, u32[]{:S(2)}, u32[]{:S(2)}) collective-permute-start(bf16[256,256]{1,0:T(8,128)(2,1)S(1)} %get-tuple-element.28), channel_id=1, source_target_pairs={{0,24},{8,0},{16,8},{24,16},{1,25},{9,1},{17,9},{25,17},{2,26},{10... | collective-permute-start | bytes 393224 | tf_op jit(solution)/shard_map/ppermute | solution.py:241
  99.4 6.6 %collective-permute-start.31 = (bf16[256,256]{1,0:T(8,128)(2,1)S(1)}, bf16[256,256]{1,0:T(8,128)(2,1)S(1)}, u32[]{:S(2)}, u32[]{:S(2)}) collective-permute-start(bf16[256,256]{1,0:T(8,128)(2,1)S(1)} %get-tuple-element.29), channel_id=1, source_target_pairs={{0,16},{8,24},{16,0},{24,8},{1,17},{9,25},{17,1},{25,9},{2,18},{10... | collective-permute-start | bytes 393224 | tf_op jit(solution)/shard_map/ppermute | solution.py:242
  106.0 9.6 %collective-permute-start.33 = (bf16[512,256]{1,0:T(8,128)(2,1)S(1)}, bf16[512,256]{1,0:T(8,128)(2,1)S(1)}, u32[]{:S(2)}, u32[]{:S(2)}) collective-permute-start(bf16[512,256]{1,0:T(8,128)(2,1)S(1)} %pad_maximum_fusion.7), channel_id=1, source_target_pairs={{0,2},{2,4},{4,6},{6,0},{1,3},{3,5},{5,7},{7,1},{8,10},{10,12},{12... | collective-permute-start | bytes 786440 | tf_op jit(solution)/shard_map/ppermute | solution.py:224
  106.1 12.2 %collective-permute-start.34 = (bf16[512,256]{1,0:T(8,128)(2,1)S(1)}, bf16[512,256]{1,0:T(8,128)(2,1)S(1)}, u32[]{:S(2)}, u32[]{:S(2)}) collective-permute-start(bf16[512,256]{1,0:T(8,128)(2,1)S(1)} %pad_maximum_fusion.8), channel_id=1, source_target_pairs={{0,4},{2,6},{4,0},{6,2},{1,5},{3,7},{5,1},{7,3},{8,12},{10,14},{12... | collective-permute-start | bytes 786440 | tf_op jit(solution)/shard_map/ppermute | solution.py:224
  108.2 12.2 %collective-permute-start.32 = (bf16[512,256]{1,0:T(8,128)(2,1)S(1)}, bf16[512,256]{1,0:T(8,128)(2,1)S(1)}, u32[]{:S(2)}, u32[]{:S(2)}) collective-permute-start(bf16[512,256]{1,0:T(8,128)(2,1)S(1)} %pad_maximum_fusion.6), channel_id=1, source_target_pairs={{0,6},{2,0},{4,2},{6,4},{1,7},{3,1},{5,3},{7,5},{8,14},{10,8},{12,... | collective-permute-start | bytes 786440 | tf_op jit(solution)/shard_map/ppermute | solution.py:224
  120.6 9.4 %collective-permute-start.35 = (bf16[256,256]{1,0:T(8,128)(2,1)S(1)}, bf16[256,256]{1,0:T(8,128)(2,1)S(1)}, u32[]{:S(2)}, u32[]{:S(2)}) collective-permute-start(bf16[256,256]{1,0:T(8,128)(2,1)S(1)} %get-tuple-element.30), channel_id=1, source_target_pairs={{0,24},{8,0},{16,8},{24,16},{1,25},{9,1},{17,9},{25,17},{2,26},{10... | collective-permute-start | bytes 393224 | tf_op jit(solution)/shard_map/ppermute | solution.py:241
  125.0 5.3 %collective-permute-start.36 = (bf16[256,256]{1,0:T(8,128)(2,1)S(1)}, bf16[256,256]{1,0:T(8,128)(2,1)S(1)}, u32[]{:S(2)}, u32[]{:S(2)}) collective-permute-start(bf16[256,256]{1,0:T(8,128)(2,1)S(1)} %get-tuple-element.31), channel_id=1, source_target_pairs={{0,16},{8,24},{16,0},{24,8},{1,17},{9,25},{17,1},{25,9},{2,18},{10... | collective-permute-start | bytes 393224 | tf_op jit(solution)/shard_map/ppermute | solution.py:242
  (12 other events, 54.7 us)

commit v3 on v2

--- a/solution.py
+++ b/solution.py
@@ -18,6 +18,7 @@
 HALF = 128
 WIDE = GROUP * ROWS
 TILE = 2 * ROWS
+NOTE = 16
 SLOTS = 9
 BF = jnp.bfloat16
 F32 = jnp.float32
@@ -40,7 +41,7 @@
     for m in range(3):
         for at, k in enumerate((0, 1, 3, 2)):
             slot = 4 * m + k - jnp.where(y < k, 4, 0)
-            places.append((m, at * ROWS, slot))
+            places.append((m, at * (ROWS + NOTE), slot))
     return places
 
 
@@ -199,20 +200,17 @@
     return [(i, (i + k) % 4) for i in range(4)]
 
 
-def gather_x_first(own, y):
-    r1 = lax.ppermute(own, "x", ring(1))
-    r2 = lax.ppermute(own, "x", ring(2))
-    three = jnp.concatenate([own, r1, r2], axis=0)
-    pieces = [own, r1, r2]
-    for k in (1, 3, 2):
-        pair = lax.dynamic_slice_in_dim(three, jnp.where(y + k >= 4, ROWS, 0), 2 * ROWS, 0)
-        pieces.append(lax.ppermute(pair, "y", ring(k)))
-    return pieces
-
-
-def gather_y_first(own):
-    near = jnp.concatenate([own] + [lax.ppermute(own, "y", ring(k)) for k in (1, 3, 2)], axis=0)
-    return [near, lax.ppermute(near, "x", ring(1)), lax.ppermute(near, "x", ring(2))]
+def note(value, width):
+    high = lax.reduce_precision(value, 8, 7)
+    middle = lax.reduce_precision(value - high, 8, 7)
+    column = lax.broadcasted_iota(jnp.int32, (NOTE, width), 1)
+    rest = value - high - middle
+    parts = jnp.where(column == 0, high, jnp.where(column == 1, middle, jnp.where(column == 2, rest, 0.0)))
+    return parts.astype(BF)
+
+
+def noted(array, row):
+    return jnp.sum(array[row, :3].astype(F32))
 
 
 def after(value, token):
@@ -256,49 +254,67 @@
         k, v = half(key_rows[0], at), half(value_rows[0], at)
         return jnp.concatenate([k[:, :HD], v[:, :HD], k[:, HD:], v[:, HD:]], axis=1)
 
-    kv_other = lax.ppermute(heads(other_at), "core", SWAP)
-    own = jnp.concatenate([heads(mine_at), kv_other], axis=0)
-    first, second = own[:, :2 * HD], own[:, 2 * HD:]
-    first_pieces = gather_x_first(first, y)
-    second_pieces = gather_y_first(second)
+    part = jnp.sum(weights_row)
+    kv_other = lax.ppermute(jnp.concatenate([heads(other_at), note(part, 4 * HD)], axis=0), "core", SWAP)
+    chip_total = part + noted(kv_other, HALF)
+    own = jnp.concatenate([heads(mine_at), kv_other[:HALF]], axis=0)
+    first = own[:, :2 * HD]
+    second = jnp.concatenate([own[:, 2 * HD:], note(chip_total, 2 * HD)], axis=0)
+    r1 = lax.ppermute(first, "x", ring(1))
+    r2 = lax.ppermute(first, "x", ring(2))
+    near = jnp.concatenate([second] + [lax.ppermute(second, "y", ring(k)) for k in (1, 3, 2)], axis=0)
 
     weighted = (upstream[0].astype(F32) * weights_row[:, None]).astype(BF)
     qm, gm = half(queries[0], mine_at), half(weighted, mine_at)
-    qo = lax.ppermute(half(queries[0], other_at), "core", SWAP)
-    go = lax.ppermute(half(weighted, other_at), "core", SWAP)
+    q_send, g_send = after((half(queries[0], other_at), half(weighted, other_at)), first)
+    qo = lax.ppermute(q_send, "core", SWAP)
+    go = lax.ppermute(g_send, "core", SWAP)
+
+    three = jnp.concatenate([first, r1, r2], axis=0)
+    three, near = after((three, near), (qo, go))
+    first_pieces = [first, r1, r2]
+    for k in (1, 3, 2):
+        pair = lax.dynamic_slice_in_dim(three, jnp.where(y + k >= 4, ROWS, 0), 2 * ROWS, 0)
+        first_pieces.append(lax.ppermute(pair, "y", ring(k)))
+    second_pieces = [near, lax.ppermute(near, "x", ring(1)), lax.ppermute(near, "x", ring(2))]
 
     at = jnp.stack([4 * x + y, core]).astype(jnp.int32)
     lengths = doc_lengths[0]
     att0, dq0, dkv0 = attention(0, place_x_first, at, lengths, qm, qo, gm, go, *first_pieces)
-    att1, dq1, dkv1 = attention(1, place_y_first, at, lengths, qm, qo, gm, go, *second_pieces)
+    att1, dq1, dkv1 = attention(1, place_y_first, after(at, att0), lengths, qm, qo, gm, go, *second_pieces)
 
     sent0 = send_y(dkv0)
-    sent0 = after(sent0, dkv1)
-    sent1 = send_y(dkv1)
-    sums0 = scatter_y(dkv0, sent0, y)
-
-    total = jnp.full((8, 128), jnp.sum(weights_row))
-    total = total + lax.ppermute(total, "core", SWAP)
-    for axis, token in (("y", second_pieces[0]), ("x", att0), ("dp", att1)):
-        total = after(total, token)
-        total = total + sum(lax.ppermute(total, axis, ring(k)) for k in (1, 2, 3))
+    sums0 = scatter_y(dkv0, after(sent0, dkv1), y)
+    sent1 = send_y(after(dkv1, sums0))
+    sums1 = scatter_y(dkv1, sent1, y)
+    grad0 = scatter_x(after(sums0, sent1[0]))
+    grad1 = scatter_x(sums1)
+
+    rows_total = sum(noted(near, at * (ROWS + NOTE) + ROWS) for at in range(4))
+    total = jnp.full((8, 128), after(rows_total, att0))
+    total = total + lax.ppermute(total, "x", ring(3))
+    for piece in second_pieces[1:]:
+        total = total + sum(noted(piece, at * (ROWS + NOTE) + ROWS) for at in range(4))
+    total = after(total, grad0)
+    total = total + sum(lax.ppermute(total, "dp", ring(k)) for k in (1, 2, 3))
     inv = 1.0 / total[0, 0]
 
-    grad0 = scatter_x(sums0)
-    grad1 = scatter_x(scatter_y(dkv1, sent1, y))
     own_grad = jnp.concatenate([grad0, grad1], axis=1).astype(BF)
 
-    def join(a, b, scale):
-        got_a = lax.ppermute(a[HALF:], "core", SWAP)
-        got_b = lax.ppermute(b[HALF:], "core", SWAP)
-        a, b = a[:HALF], b[:HALF]
-        low = jnp.concatenate([a, b, got_a, got_b], axis=1)
-        high = jnp.concatenate([got_a, got_b, a, b], axis=1)
-        both = jnp.where(core == 0, low, high)
-        return both if scale is None else (both.astype(F32) * scale).astype(BF)
-
-    out_rows = join(att0, att1, None)
-    dq_rows = join(dq0, dq1, inv)
+    width = GROUP * HD
+    parts = [att0, att1, dq0, dq1]
+    others = jnp.concatenate([part[HALF:] for part in parts], axis=1)
+    others = lax.ppermute(after(others, sums1[1]), "core", SWAP)
+
+    def join(at):
+        ours = jnp.concatenate([parts[at][:HALF], parts[at + 1][:HALF]], axis=1)
+        theirs = others[:, at * width:(at + 2) * width]
+        low = jnp.concatenate([ours, theirs], axis=1)
+        high = jnp.concatenate([theirs, ours], axis=1)
+        return jnp.where(core == 0, low, high)
+
+    out_rows = join(0)
+    dq_rows = (join(2).astype(F32) * inv).astype(BF)
     got = lax.ppermute(own_grad[HALF:], "core", SWAP)
     mine = own_grad[:HALF]
 

time: 134 us -> 139 us (1.037); the launches traced: 135 us -> 136 us
  waiting for transfers between devices: 32.9 us -> 15.6 us
  between operations: 1.73 us -> 16.7 us
  starting transfers between devices: 78.2 us -> 67.6 us
  other arithmetic: 7.58 us -> 17 us
  local copies, waits for them, and re-layouts: 5.96 us -> 9.64 us
    ppermute x27 -> x18, starting transfers between devices: 58.3 us -> 32.4 us  [the longest x1 6.49 us: body(): total = total + lax.ppermute(total, 'x', ring(3))]
    ppermute x2, starting transfers between devices: 0.01 us -> 15.5 us  [scatter_x(): t2 = lax.ppermute(sums[2], 'x', ring(2))]
    ppermute x6, waiting for transfers between devices: 17.4 us -> 6.82 us  [send_y(): lax.ppermute(jnp.concatenate([dkv[k], dkv[4 + k]], axis=0), 'y', ring(4 -...]
    ppermute x2, waiting for transfers between devices: 6.81 us -> 0.01 us  [scatter_x(): t1 = lax.ppermute(sums[1], 'x', ring(3))]
    ppermute x6, starting transfers between devices: 4.37 us -> 10.1 us  [send_y(): lax.ppermute(jnp.concatenate([dkv[k], dkv[4 + k]], axis=0), 'y', ring(4 -...]
    ppermute x2, starting transfers between devices: 13 us -> 7.73 us  [scatter_x(): t1 = lax.ppermute(sums[1], 'x', ring(3))]
    convert_element_type x6, other arithmetic: 0.22 us -> 3.07 us  [scatter_y(): got = got.astype(F32)]
    unnamed x12 -> x24, local copies, waits for them, and re-layouts: 1.06 us -> 3.83 us
  transfers between devices with their start and end apart: 38 -> 29, of which waited for: 15 -> 6; matrix products, arithmetic and copies ran while one was open for 7% -> 12% of each run, Pallas kernels for 7% -> 7%
where the time goes in v3:
time: 139 us; the launch traced here: 136 us
  starting transfers between devices  67.6 us (49%)
  other arithmetic  17 us (12%)
  between operations  16.7 us (12%)
  waiting for transfers between devices  15.6 us (11%)
  Pallas kernels  9.78 us (7%)
  local copies, waits for them, and re-layouts  9.64 us (7%)
    ppermute x2, starting transfers between devices, scatter_x(): t2 = lax.ppermute(sums[2], 'x', ring(2))  15.5 us
    ppermute x6, starting transfers between devices, send_y(): lax.ppermute(jnp.concatenate([dkv[k], dkv[4 + k]], axis=0), 'y', ring(4 -...  10.1 us
    pallas_call x2, Pallas kernels, attention(): pl.pallas_call(functools.partial(attention_kernel, head, places_of, len(p...  9.78 us
    ppermute x2, starting transfers between devices, scatter_x(): t1 = lax.ppermute(sums[1], 'x', ring(3))  7.73 us
    ppermute x6, waiting for transfers between devices, send_y(): lax.ppermute(jnp.concatenate([dkv[k], dkv[4 + k]], axis=0), 'y', ring(4 -...  6.82 us
    ppermute x1, starting transfers between devices, body(): total = total + lax.ppermute(total, 'x', ring(3))  6.49 us
    ppermute x3, starting transfers between devices, body(): total = total + sum((lax.ppermute(total, 'dp', ring(k)) for k in (1, 2, 3)))  5.26 us
    ppermute x3, starting transfers between devices, body(): lax.ppermute(second, 'y', ring(k))  4.99 us
  transfers between devices with their start and end apart: 29, of which 6 were waited for; matrix products, arithmetic and copies ran while one was open for 12% of the time, Pallas kernels for 7%

profile of v3, /device:TPU:1, one launch (start us, length us, event | category | flops | bytes accessed | tf_op | source)
XLA Modules:
  0.0 136.3 jit_solution(13800606807130880449)
XLA Ops:
  0.7 1.3 reduce_sum.126
  6.6 1.3 select_convert_fusion
  8.0 1.5 %collective-permute-start = (bf16[144,512]{1,0:T(8,128)(2,1)S(1)}, bf16[144,512]{1,0:T(8,128)(2,1)S(1)}, u32[]{:S(2)}, u32[]{:S(2)}) collective-permute-start(bf16[144,512]{1,0:T(8,128)(2,1)S(1)} %pad_maximum_fusion.9), channel_id=1, source_target_pairs={{0,1},{1,0},{2,3},{3,2},{4,5},{5,4},{6,7},{7,6},{8,9},{9,8},{10,11... | collective-permute-start | bytes 442376 | tf_op jit(solution)/shard_map/ppermute | solution.py:258
  10.6 2.9 %collective-permute-start.4 = (bf16[256,256]{1,0:T(8,128)(2,1)S(1)}, bf16[256,256]{1,0:T(8,128)(2,1)S(1)}, u32[]{:S(2)}, u32[]{:S(2)}) collective-permute-start(bf16[256,256]{1,0:T(8,128)(2,1)S(1)} %get-tuple-element.94.refs_4_), channel_id=1, source_target_pairs={{0,16},{8,24},{16,0},{24,8},{1,17},{9,25},{17,1},{25,9},{2,18},{10... | collective-permute-start | bytes 393224 | tf_op jit(solution)/shard_map/ppermute | solution.py:264
  18.1 1.3 select_convert_fusion.1
  20.1 1.3 collective-permute-start.5
  22.2 2.6 %collective-permute-start.7 = (bf16[272,256]{1,0:T(8,128)(2,1)}, bf16[272,256]{1,0:T(8,128)(2,1)S(1)}, u32[]{:S(2)}, u32[]{:S(2)}) collective-permute-start(bf16[272,256]{1,0:T(8,128)(2,1)} %pad_maximum_fusion.10), channel_id=1, source_target_pairs={{0,4},{2,6},{4,0},{6,2},{1,5},{3,7},{5,1},{7,3},{8,12},{10,14},{12... | collective-permute-start | bytes 417800 | tf_op jit(solution)/shard_map/ppermute | solution.py:265
  24.8 1.1 collective-permute-start.6
  25.9 1.7 %collective-permute-start.1 = (bf16[128,1536]{1,0:T(8,128)(2,1)}, bf16[128,1536]{1,0:T(8,128)(2,1)S(1)}, u32[]{:S(2)}, u32[]{:S(2)}) collective-permute-start(bf16[128,1536]{1,0:T(8,128)(2,1)} %get-tuple-element.25), channel_id=1, source_target_pairs={{0,1},{1,0},{2,3},{3,2},{4,5},{5,4},{6,7},{7,6},{8,9},{9,8},{10,11... | collective-permute-start | bytes 1179656 | tf_op jit(solution)/shard_map/ppermute | solution.py:270
  28.6 2.0 %collective-permute-done.6 = bf16[272,256]{1,0:T(8,128)(2,1)S(1)} collective-permute-done((bf16[272,256]{1,0:T(8,128)(2,1)}, bf16[272,256]{1,0:T(8,128)(2,1)S(1)}, u32[]{:S(2)}, u32[]{:S(2)}) %collective-permute-start.6) | collective-permute-done | bytes 139296 | tf_op jit(solution)/shard_map/ppermute | solution.py:265
  31.7 2.0 %collective-permute-start.10 = (bf16[512,256]{1,0:T(8,128)(2,1)}, bf16[512,256]{1,0:T(8,128)(2,1)}, u32[]{:S(2)}, u32[]{:S(2)}) collective-permute-start(bf16[512,256]{1,0:T(8,128)(2,1)} %get-tuple-element.89), channel_id=1, source_target_pairs={{0,4},{2,6},{4,0},{6,2},{1,5},{3,7},{5,1},{7,3},{8,12},{10,14},{12... | collective-permute-start | bytes 786440 | tf_op jit(solution)/shard_map/ppermute | solution.py:278
  33.7 1.5 %collective-permute-start.9 = (bf16[512,256]{1,0:T(8,128)(2,1)}, bf16[512,256]{1,0:T(8,128)(2,1)}, u32[]{:S(2)}, u32[]{:S(2)}) collective-permute-start(bf16[512,256]{1,0:T(8,128)(2,1)} %get-tuple-element.90), channel_id=1, source_target_pairs={{0,6},{2,0},{4,2},{6,4},{1,7},{3,1},{5,3},{7,5},{8,14},{10,8},{12,... | collective-permute-start | bytes 786440 | tf_op jit(solution)/shard_map/ppermute | solution.py:278
  35.3 1.8 %collective-permute-start.12 = (bf16[1088,256]{1,0:T(8,128)(2,1)S(1)}, bf16[1088,256]{1,0:T(8,128)(2,1)S(1)}, u32[]{:S(2)}, u32[]{:S(2)}) collective-permute-start(bf16[1088,256]{1,0:T(8,128)(2,1)S(1)} %constant_dynamic-update-slice_fusion.refs_4_), channel_id=1, source_target_pairs={{0,16},{8,24},{16,0},{24,8},{1,17},{9,25},{17,1},{25,9},{2,18},{10... | collective-permute-start | bytes 1671176 | tf_op jit(solution)/shard_map/ppermute | solution.py:279
  37.0 1.2 collective-permute-start.11
  41.4 4.9 %collective-permute-done.9.refs_8_ = bf16[512,256]{1,0:T(8,128)(2,1)} collective-permute-done((bf16[512,256]{1,0:T(8,128)(2,1)}, bf16[512,256]{1,0:T(8,128)(2,1)}, u32[]{:S(2)}, u32[]{:S(2)}) %collective-permute-start.9) | collective-permute-done | bytes 262176 | tf_op jit(solution)/shard_map/ppermute | solution.py:278
  47.4 5.0 %shard_map.93 = (bf16[256,768]{1,0:T(8,128)(2,1)S(1)}, bf16[256,768]{1,0:T(8,128)(2,1)S(1)}, bf16[9,256,256]{2,1,0:T(8,128)(2,1)S(1)}) custom-call(s32[2]{0:T(128)S(1)} %pad_add_fusion.at_ref, s32[8]{0:T(128)S(1)} %bitcast.90, bf16[128,1536]{1,0:T(8,128)(2,1)S(1)} %get-tuple-element.80.refs_0_, bf16[128,1536]{1,0:T(8,128)(2,1)S(1)} %collective-permute-done.1.refs_1_, ...), custom_call_target="tpu_custom_call" | custom-call | flops 21743271936 | bytes 6000000 | tf_op jit(solution)/shard_map/pallas_call | solution.py:168
  52.4 6.5 %collective-permute-start.20 = (f32[8,128]{1,0:T(8,128)S(1)}, f32[8,128]{1,0:T(8,128)S(1)}, u32[]{:S(2)}, u32[]{:S(2)}) collective-permute-start(f32[8,128]{1,0:T(8,128)S(1)} %broadcast_in_dim.62), channel_id=1, source_target_pairs={{0,24},{8,0},{16,8},{24,16},{1,25},{9,1},{17,9},{25,17},{2,26},{10... | collective-permute-start | bytes 12296 | tf_op jit(solution)/shard_map/ppermute | solution.py:295
  59.0 3.5 %collective-permute-start.13 = (bf16[512,256]{1,0:T(8,128)(2,1)S(1)}, bf16[512,256]{1,0:T(8,128)(2,1)S(1)}, u32[]{:S(2)}, u32[]{:S(2)}) collective-permute-start(bf16[512,256]{1,0:T(8,128)(2,1)S(1)} %pad_maximum_fusion.3), channel_id=1, source_target_pairs={{0,6},{2,0},{4,2},{6,4},{1,7},{3,1},{5,3},{7,5},{8,14},{10,8},{12,... | collective-permute-start | bytes 786440 | tf_op jit(solution)/shard_map/ppermute | solution.py:222
  64.9 1.2 collective-permute-start.15
  67.1 4.7 %shard_map.94 = (bf16[256,768]{1,0:T(8,128)(2,1)S(1)}, bf16[256,768]{1,0:T(8,128)(2,1)S(1)}, bf16[9,256,256]{2,1,0:T(8,128)(2,1)S(1)}) custom-call(s32[2]{0:T(128)S(1)} %pad_add_fusion.at_ref, s32[8]{0:T(128)S(1)} %bitcast.91, bf16[128,1536]{1,0:T(8,128)(2,1)S(1)} %get-tuple-element.80.refs_0_, bf16[128,1536]{1,0:T(8,128)(2,1)S(1)} %collective-permute-done.1.refs_1_, ...), custom_call_target="tpu_custom_call" | custom-call | flops 21743271936 | bytes 6000000 | tf_op jit(solution)/shard_map/pallas_call | solution.py:168
  72.0 3.1 %collective-permute-done.15 = bf16[512,256]{1,0:T(8,128)(2,1)S(1)} collective-permute-done((bf16[512,256]{1,0:T(8,128)(2,1)S(1)}, bf16[512,256]{1,0:T(8,128)(2,1)S(1)}, u32[]{:S(2)}, u32[]{:S(2)}) %collective-permute-start.15) | collective-permute-done | bytes 262176 | tf_op jit(solution)/shard_map/ppermute | solution.py:222
  77.9 4.3 %collective-permute-start.18 = (bf16[512,256]{1,0:T(8,128)(2,1)}, bf16[512,256]{1,0:T(8,128)(2,1)}, u32[]{:S(2)}, u32[]{:S(2)}) collective-permute-start(bf16[512,256]{1,0:T(8,128)(2,1)} %pad_maximum_fusion.8), channel_id=1, source_target_pairs={{0,4},{2,6},{4,0},{6,2},{1,5},{3,7},{5,1},{7,3},{8,12},{10,14},{12... | collective-permute-start | bytes 786440 | tf_op jit(solution)/shard_map/ppermute | solution.py:222
  89.4 3.7 %collective-permute-done.16 = bf16[512,256]{1,0:T(8,128)(2,1)} collective-permute-done((bf16[512,256]{1,0:T(8,128)(2,1)}, bf16[512,256]{1,0:T(8,128)(2,1)}, u32[]{:S(2)}, u32[]{:S(2)}) %collective-permute-start.16) | collective-permute-done | bytes 262176 | tf_op jit(solution)/shard_map/ppermute | solution.py:222
  93.1 7.4 %collective-permute-start.21 = (bf16[256,256]{1,0:T(8,128)(2,1)S(1)}, bf16[256,256]{1,0:T(8,128)(2,1)S(1)}, u32[]{:S(2)}, u32[]{:S(2)}) collective-permute-start(bf16[256,256]{1,0:T(8,128)(2,1)S(1)} %get-tuple-element.43), channel_id=1, source_target_pairs={{0,24},{8,0},{16,8},{24,16},{1,25},{9,1},{17,9},{25,17},{2,26},{10... | collective-permute-start | bytes 393224 | tf_op jit(solution)/shard_map/ppermute | solution.py:239
  100.5 13.2 %collective-permute-start.22 = (bf16[256,256]{1,0:T(8,128)(2,1)S(1)}, bf16[256,256]{1,0:T(8,128)(2,1)S(1)}, u32[]{:S(2)}, u32[]{:S(2)}) collective-permute-start(bf16[256,256]{1,0:T(8,128)(2,1)S(1)} %get-tuple-element.44), channel_id=1, source_target_pairs={{0,16},{8,24},{16,0},{24,8},{1,17},{9,25},{17,1},{25,9},{2,18},{10... | collective-permute-start | bytes 393224 | tf_op jit(solution)/shard_map/ppermute | solution.py:240
  117.1 2.4 %collective-permute-start.27 = (bf16[256,256]{1,0:T(8,128)(2,1)S(1)}, bf16[256,256]{1,0:T(8,128)(2,1)S(1)}, u32[]{:S(2)}, u32[]{:S(2)}) collective-permute-start(bf16[256,256]{1,0:T(8,128)(2,1)S(1)} %get-tuple-element.58), channel_id=1, source_target_pairs={{0,16},{8,24},{16,0},{24,8},{1,17},{9,25},{17,1},{25,9},{2,18},{10... | collective-permute-start | bytes 393224 | tf_op jit(solution)/shard_map/ppermute | solution.py:240
  119.5 2.7 %collective-permute-start.19 = (bf16[128,3072]{1,0:T(8,128)(2,1)S(1)}, bf16[128,3072]{1,0:T(8,128)(2,1)S(1)}, u32[]{:S(2)}, u32[]{:S(2)}) collective-permute-start(bf16[128,3072]{1,0:T(8,128)(2,1)S(1)} %pad_maximum_fusion), channel_id=1, source_target_pairs={{0,1},{1,0},{2,3},{3,2},{4,5},{5,4},{6,7},{7,6},{8,9},{9,8},{10,11... | collective-permute-start | bytes 2359304 | tf_op jit(solution)/shard_map/ppermute | solution.py:307
  122.2 3.7 %collective-permute-start.25 = (f32[8,128]{1,0:T(8,128)S(1)}, f32[8,128]{1,0:T(8,128)S(1)}, u32[]{:S(2)}, u32[]{:S(2)}) collective-permute-start(f32[8,128]{1,0:T(8,128)S(1)} %add_add_fusion.1), channel_id=1, source_target_pairs={{0,96},{32,0},{64,32},{96,64},{1,97},{33,1},{65,33},{97,65},{2,98}... | collective-permute-start | bytes 12296 | tf_op jit(solution)/shard_map/ppermute | solution.py:299
  125.9 1.5 %collective-permute-start.24 = (f32[8,128]{1,0:T(8,128)S(1)}, f32[8,128]{1,0:T(8,128)S(1)}, u32[]{:S(2)}, u32[]{:S(2)}) collective-permute-start(f32[8,128]{1,0:T(8,128)S(1)} %add_add_fusion.1), channel_id=1, source_target_pairs={{0,64},{32,96},{64,0},{96,32},{1,65},{33,97},{65,1},{97,33},{2,66}... | collective-permute-start | bytes 12296 | tf_op jit(solution)/shard_map/ppermute | solution.py:299
  127.7 1.9 %collective-permute-start.28 = (bf16[128,512]{1,0:T(8,128)(2,1)S(1)}, bf16[128,512]{1,0:T(8,128)(2,1)S(1)}, u32[]{:S(2)}, u32[]{:S(2)}) collective-permute-start(bf16[128,512]{1,0:T(8,128)(2,1)S(1)} %pad_maximum_fusion.11), channel_id=1, source_target_pairs={{0,1},{1,0},{2,3},{3,2},{4,5},{5,4},{6,7},{7,6},{8,9},{9,8},{10,11... | collective-permute-start | bytes 393224 | tf_op jit(solution)/shard_map/ppermute | solution.py:318
  129.8 1.5 %collective-permute-done.23 = f32[8,128]{1,0:T(8,128)S(1)} collective-permute-done((f32[8,128]{1,0:T(8,128)S(1)}, f32[8,128]{1,0:T(8,128)S(1)}, u32[]{:S(2)}, u32[]{:S(2)}) %collective-permute-start.23) | collective-permute-done | bytes 4128 | tf_op jit(solution)/shard_map/ppermute | solution.py:299
  134.1 1.1 multiply_convert_fusion
  (116 shorter events, 23.8 us)
Async XLA Ops:
  0.6 8.8 %copy-start.10 = (f32[1,128]{1,0:T(1,128)S(1)}, f32[1,128]{1,0:T(1,128)}, u32[]{:S(2)}) copy-start(f32[1,128]{1,0:T(1,128)} %param.10) | copy-start | bytes 1540
  8.0 2.6 %collective-permute-start = (bf16[144,512]{1,0:T(8,128)(2,1)S(1)}, bf16[144,512]{1,0:T(8,128)(2,1)S(1)}, u32[]{:S(2)}, u32[]{:S(2)}) collective-permute-start(bf16[144,512]{1,0:T(8,128)(2,1)S(1)} %pad_maximum_fusion.9), channel_id=1, source_target_pairs={{0,1},{1,0},{2,3},{3,2},{4,5},{5,4},{6,7},{7,6},{8,9},{9,8},{10,11... | collective-permute-start | bytes 442376 | tf_op jit(solution)/shard_map/ppermute | solution.py:258
  10.5 10.9 %copy-start.7 = (bf16[1,128,3072]{2,1,0:T(8,128)(2,1)S(1)}, bf16[1,128,3072]{2,1,0:T(8,128)(2,1)}, u32[]{:S(2)}) copy-start(bf16[1,128,3072]{2,1,0:T(8,128)(2,1)} %param.6) | copy-start | bytes 2359300
  10.6 15.2 %collective-permute-start.4 = (bf16[256,256]{1,0:T(8,128)(2,1)S(1)}, bf16[256,256]{1,0:T(8,128)(2,1)S(1)}, u32[]{:S(2)}, u32[]{:S(2)}) collective-permute-start(bf16[256,256]{1,0:T(8,128)(2,1)S(1)} %get-tuple-element.94.refs_4_), channel_id=1, source_target_pairs={{0,16},{8,24},{16,0},{24,8},{1,17},{9,25},{17,1},{25,9},{2,18},{10... | collective-permute-start | bytes 393224 | tf_op jit(solution)/shard_map/ppermute | solution.py:264
  13.5 14.0 %collective-permute-start.3 = (bf16[256,256]{1,0:T(8,128)(2,1)S(1)}, bf16[256,256]{1,0:T(8,128)(2,1)S(1)}, u32[]{:S(2)}, u32[]{:S(2)}) collective-permute-start(bf16[256,256]{1,0:T(8,128)(2,1)S(1)} %get-tuple-element.94.refs_4_), channel_id=1, source_target_pairs={{0,8},{8,16},{16,24},{24,0},{1,9},{9,17},{17,25},{25,1},{2,10},{10... | collective-permute-start | bytes 393224 | tf_op jit(solution)/shard_map/ppermute | solution.py:263
  20.1 7.6 %collective-permute-start.5 = (bf16[272,256]{1,0:T(8,128)(2,1)}, bf16[272,256]{1,0:T(8,128)(2,1)}, u32[]{:S(2)}, u32[]{:S(2)}) collective-permute-start(bf16[272,256]{1,0:T(8,128)(2,1)} %pad_maximum_fusion.10), channel_id=1, source_target_pairs={{0,2},{2,4},{4,6},{6,0},{1,3},{3,5},{5,7},{7,1},{8,10},{10,12},{12... | collective-permute-start | bytes 417800 | tf_op jit(solution)/shard_map/ppermute | solution.py:265
  22.2 8.5 %collective-permute-start.7 = (bf16[272,256]{1,0:T(8,128)(2,1)}, bf16[272,256]{1,0:T(8,128)(2,1)S(1)}, u32[]{:S(2)}, u32[]{:S(2)}) collective-permute-start(bf16[272,256]{1,0:T(8,128)(2,1)} %pad_maximum_fusion.10), channel_id=1, source_target_pairs={{0,4},{2,6},{4,0},{6,2},{1,5},{3,7},{5,1},{7,3},{8,12},{10,14},{12... | collective-permute-start | bytes 417800 | tf_op jit(solution)/shard_map/ppermute | solution.py:265
  24.8 5.8 %collective-permute-start.6 = (bf16[272,256]{1,0:T(8,128)(2,1)}, bf16[272,256]{1,0:T(8,128)(2,1)S(1)}, u32[]{:S(2)}, u32[]{:S(2)}) collective-permute-start(bf16[272,256]{1,0:T(8,128)(2,1)} %pad_maximum_fusion.10), channel_id=1, source_target_pairs={{0,6},{2,0},{4,2},{6,4},{1,7},{3,1},{5,3},{7,5},{8,14},{10,8},{12,... | collective-permute-start | bytes 417800 | tf_op jit(solution)/shard_map/ppermute | solution.py:265
  25.9 4.8 %collective-permute-start.1 = (bf16[128,1536]{1,0:T(8,128)(2,1)}, bf16[128,1536]{1,0:T(8,128)(2,1)S(1)}, u32[]{:S(2)}, u32[]{:S(2)}) collective-permute-start(bf16[128,1536]{1,0:T(8,128)(2,1)} %get-tuple-element.25), channel_id=1, source_target_pairs={{0,1},{1,0},{2,3},{3,2},{4,5},{5,4},{6,7},{7,6},{8,9},{9,8},{10,11... | collective-permute-start | bytes 1179656 | tf_op jit(solution)/shard_map/ppermute | solution.py:270
  27.6 3.1 %collective-permute-start.2 = (bf16[128,1536]{1,0:T(8,128)(2,1)}, bf16[128,1536]{1,0:T(8,128)(2,1)S(1)}, u32[]{:S(2)}, u32[]{:S(2)}) collective-permute-start(bf16[128,1536]{1,0:T(8,128)(2,1)} %get-tuple-element.26), channel_id=1, source_target_pairs={{0,1},{1,0},{2,3},{3,2},{4,5},{5,4},{6,7},{7,6},{8,9},{9,8},{10,11... | collective-permute-start | bytes 1179656 | tf_op jit(solution)/shard_map/ppermute | solution.py:271
  27.7 18.7 %copy-start.5 = (s32[1,8]{1,0:T(1,128)S(1)}, s32[1,8]{1,0:T(1,128)}, u32[]{:S(2)}) copy-start(s32[1,8]{1,0:T(1,128)} %param.11) | copy-start | bytes 100
  31.7 9.7 %collective-permute-start.10 = (bf16[512,256]{1,0:T(8,128)(2,1)}, bf16[512,256]{1,0:T(8,128)(2,1)}, u32[]{:S(2)}, u32[]{:S(2)}) collective-permute-start(bf16[512,256]{1,0:T(8,128)(2,1)} %get-tuple-element.89), channel_id=1, source_target_pairs={{0,4},{2,6},{4,0},{6,2},{1,5},{3,7},{5,1},{7,3},{8,12},{10,14},{12... | collective-permute-start | bytes 786440 | tf_op jit(solution)/shard_map/ppermute | solution.py:278
  33.7 12.7 %collective-permute-start.9 = (bf16[512,256]{1,0:T(8,128)(2,1)}, bf16[512,256]{1,0:T(8,128)(2,1)}, u32[]{:S(2)}, u32[]{:S(2)}) collective-permute-start(bf16[512,256]{1,0:T(8,128)(2,1)} %get-tuple-element.90), channel_id=1, source_target_pairs={{0,6},{2,0},{4,2},{6,4},{1,7},{3,1},{5,3},{7,5},{8,14},{10,8},{12,... | collective-permute-start | bytes 786440 | tf_op jit(solution)/shard_map/ppermute | solution.py:278
  35.2 11.2 %collective-permute-start.8 = (bf16[512,256]{1,0:T(8,128)(2,1)}, bf16[512,256]{1,0:T(8,128)(2,1)}, u32[]{:S(2)}, u32[]{:S(2)}) collective-permute-start(bf16[512,256]{1,0:T(8,128)(2,1)} %get-tuple-element.91), channel_id=1, source_target_pairs={{0,2},{2,4},{4,6},{6,0},{1,3},{3,5},{5,7},{7,1},{8,10},{10,12},{12... | collective-permute-start | bytes 786440 | tf_op jit(solution)/shard_map/ppermute | solution.py:278
  35.3 28.8 %collective-permute-start.12 = (bf16[1088,256]{1,0:T(8,128)(2,1)S(1)}, bf16[1088,256]{1,0:T(8,128)(2,1)S(1)}, u32[]{:S(2)}, u32[]{:S(2)}) collective-permute-start(bf16[1088,256]{1,0:T(8,128)(2,1)S(1)} %constant_dynamic-update-slice_fusion.refs_4_), channel_id=1, source_target_pairs={{0,16},{8,24},{16,0},{24,8},{1,17},{9,25},{17,1},{25,9},{2,18},{10... | collective-permute-start | bytes 1671176 | tf_op jit(solution)/shard_map/ppermute | solution.py:279
  37.0 29.0 %collective-permute-start.11 = (bf16[1088,256]{1,0:T(8,128)(2,1)S(1)}, bf16[1088,256]{1,0:T(8,128)(2,1)S(1)}, u32[]{:S(2)}, u32[]{:S(2)}) collective-permute-start(bf16[1088,256]{1,0:T(8,128)(2,1)S(1)} %constant_dynamic-update-slice_fusion.refs_4_), channel_id=1, source_target_pairs={{0,8},{8,16},{16,24},{24,0},{1,9},{9,17},{17,25},{25,1},{2,10},{10... | collective-permute-start | bytes 1671176 | tf_op jit(solution)/shard_map/ppermute | solution.py:279
  52.4 36.9 %collective-permute-start.20 = (f32[8,128]{1,0:T(8,128)S(1)}, f32[8,128]{1,0:T(8,128)S(1)}, u32[]{:S(2)}, u32[]{:S(2)}) collective-permute-start(f32[8,128]{1,0:T(8,128)S(1)} %broadcast_in_dim.62), channel_id=1, source_target_pairs={{0,24},{8,0},{16,8},{24,16},{1,25},{9,1},{17,9},{25,17},{2,26},{10... | collective-permute-start | bytes 12296 | tf_op jit(solution)/shard_map/ppermute | solution.py:295
  59.0 12.9 %collective-permute-start.13 = (bf16[512,256]{1,0:T(8,128)(2,1)S(1)}, bf16[512,256]{1,0:T(8,128)(2,1)S(1)}, u32[]{:S(2)}, u32[]{:S(2)}) collective-permute-start(bf16[512,256]{1,0:T(8,128)(2,1)S(1)} %pad_maximum_fusion.3), channel_id=1, source_target_pairs={{0,6},{2,0},{4,2},{6,4},{1,7},{3,1},{5,3},{7,5},{8,14},{10,8},{12,... | collective-permute-start | bytes 786440 | tf_op jit(solution)/shard_map/ppermute | solution.py:222
  62.5 9.4 %collective-permute-start.14 = (bf16[512,256]{1,0:T(8,128)(2,1)S(1)}, bf16[512,256]{1,0:T(8,128)(2,1)S(1)}, u32[]{:S(2)}, u32[]{:S(2)}) collective-permute-start(bf16[512,256]{1,0:T(8,128)(2,1)S(1)} %pad_maximum_fusion.4), channel_id=1, source_target_pairs={{0,2},{2,4},{4,6},{6,0},{1,3},{3,5},{5,7},{7,1},{8,10},{10,12},{12... | collective-permute-start | bytes 786440 | tf_op jit(solution)/shard_map/ppermute | solution.py:222
  64.9 10.2 %collective-permute-start.15 = (bf16[512,256]{1,0:T(8,128)(2,1)S(1)}, bf16[512,256]{1,0:T(8,128)(2,1)S(1)}, u32[]{:S(2)}, u32[]{:S(2)}) collective-permute-start(bf16[512,256]{1,0:T(8,128)(2,1)S(1)} %pad_maximum_fusion.5), channel_id=1, source_target_pairs={{0,4},{2,6},{4,0},{6,2},{1,5},{3,7},{5,1},{7,3},{8,12},{10,14},{12... | collective-permute-start | bytes 786440 | tf_op jit(solution)/shard_map/ppermute | solution.py:222
  76.2 38.5 %collective-permute-start.17 = (bf16[512,256]{1,0:T(8,128)(2,1)}, bf16[512,256]{1,0:T(8,128)(2,1)}, u32[]{:S(2)}, u32[]{:S(2)}) collective-permute-start(bf16[512,256]{1,0:T(8,128)(2,1)} %pad_maximum_fusion.7), channel_id=1, source_target_pairs={{0,2},{2,4},{4,6},{6,0},{1,3},{3,5},{5,7},{7,1},{8,10},{10,12},{12... | collective-permute-start | bytes 786440 | tf_op jit(solution)/shard_map/ppermute | solution.py:222
  77.9 37.8 %collective-permute-start.18 = (bf16[512,256]{1,0:T(8,128)(2,1)}, bf16[512,256]{1,0:T(8,128)(2,1)}, u32[]{:S(2)}, u32[]{:S(2)}) collective-permute-start(bf16[512,256]{1,0:T(8,128)(2,1)} %pad_maximum_fusion.8), channel_id=1, source_target_pairs={{0,4},{2,6},{4,0},{6,2},{1,5},{3,7},{5,1},{7,3},{8,12},{10,14},{12... | collective-permute-start | bytes 786440 | tf_op jit(solution)/shard_map/ppermute | solution.py:222
  82.9 10.2 %collective-permute-start.16 = (bf16[512,256]{1,0:T(8,128)(2,1)}, bf16[512,256]{1,0:T(8,128)(2,1)}, u32[]{:S(2)}, u32[]{:S(2)}) collective-permute-start(bf16[512,256]{1,0:T(8,128)(2,1)} %pad_maximum_fusion.6), channel_id=1, source_target_pairs={{0,6},{2,0},{4,2},{6,4},{1,7},{3,1},{5,3},{7,5},{8,14},{10,8},{12,... | collective-permute-start | bytes 786440 | tf_op jit(solution)/shard_map/ppermute | solution.py:222
  93.1 29.1 %collective-permute-start.21 = (bf16[256,256]{1,0:T(8,128)(2,1)S(1)}, bf16[256,256]{1,0:T(8,128)(2,1)S(1)}, u32[]{:S(2)}, u32[]{:S(2)}) collective-permute-start(bf16[256,256]{1,0:T(8,128)(2,1)S(1)} %get-tuple-element.43), channel_id=1, source_target_pairs={{0,24},{8,0},{16,8},{24,16},{1,25},{9,1},{17,9},{25,17},{2,26},{10... | collective-permute-start | bytes 393224 | tf_op jit(solution)/shard_map/ppermute | solution.py:239
  100.5 21.7 %collective-permute-start.22 = (bf16[256,256]{1,0:T(8,128)(2,1)S(1)}, bf16[256,256]{1,0:T(8,128)(2,1)S(1)}, u32[]{:S(2)}, u32[]{:S(2)}) collective-permute-start(bf16[256,256]{1,0:T(8,128)(2,1)S(1)} %get-tuple-element.44), channel_id=1, source_target_pairs={{0,16},{8,24},{16,0},{24,8},{1,17},{9,25},{17,1},{25,9},{2,18},{10... | collective-permute-start | bytes 393224 | tf_op jit(solution)/shard_map/ppermute | solution.py:240
  116.8 10.7 %collective-permute-start.26 = (bf16[256,256]{1,0:T(8,128)(2,1)S(1)}, bf16[256,256]{1,0:T(8,128)(2,1)S(1)}, u32[]{:S(2)}, u32[]{:S(2)}) collective-permute-start(bf16[256,256]{1,0:T(8,128)(2,1)S(1)} %get-tuple-element.59), channel_id=1, source_target_pairs={{0,24},{8,0},{16,8},{24,16},{1,25},{9,1},{17,9},{25,17},{2,26},{10... | collective-permute-start | bytes 393224 | tf_op jit(solution)/shard_map/ppermute | solution.py:239
  117.1 10.3 %collective-permute-start.27 = (bf16[256,256]{1,0:T(8,128)(2,1)S(1)}, bf16[256,256]{1,0:T(8,128)(2,1)S(1)}, u32[]{:S(2)}, u32[]{:S(2)}) collective-permute-start(bf16[256,256]{1,0:T(8,128)(2,1)S(1)} %get-tuple-element.58), channel_id=1, source_target_pairs={{0,16},{8,24},{16,0},{24,8},{1,17},{9,25},{17,1},{25,9},{2,18},{10... | collective-permute-start | bytes 393224 | tf_op jit(solution)/shard_map/ppermute | solution.py:240
  119.5 14.5 %collective-permute-start.19 = (bf16[128,3072]{1,0:T(8,128)(2,1)S(1)}, bf16[128,3072]{1,0:T(8,128)(2,1)S(1)}, u32[]{:S(2)}, u32[]{:S(2)}) collective-permute-start(bf16[128,3072]{1,0:T(8,128)(2,1)S(1)} %pad_maximum_fusion), channel_id=1, source_target_pairs={{0,1},{1,0},{2,3},{3,2},{4,5},{5,4},{6,7},{7,6},{8,9},{9,8},{10,11... | collective-permute-start | bytes 2359304 | tf_op jit(solution)/shard_map/ppermute | solution.py:307
  122.2 7.3 %collective-permute-start.25 = (f32[8,128]{1,0:T(8,128)S(1)}, f32[8,128]{1,0:T(8,128)S(1)}, u32[]{:S(2)}, u32[]{:S(2)}) collective-permute-start(f32[8,128]{1,0:T(8,128)S(1)} %add_add_fusion.1), channel_id=1, source_target_pairs={{0,96},{32,0},{64,32},{96,64},{1,97},{33,1},{65,33},{97,65},{2,98}... | collective-permute-start | bytes 12296 | tf_op jit(solution)/shard_map/ppermute | solution.py:299
  125.9 4.0 %collective-permute-start.24 = (f32[8,128]{1,0:T(8,128)S(1)}, f32[8,128]{1,0:T(8,128)S(1)}, u32[]{:S(2)}, u32[]{:S(2)}) collective-permute-start(f32[8,128]{1,0:T(8,128)S(1)} %add_add_fusion.1), channel_id=1, source_target_pairs={{0,64},{32,96},{64,0},{96,32},{1,65},{33,97},{65,1},{97,33},{2,66}... | collective-permute-start | bytes 12296 | tf_op jit(solution)/shard_map/ppermute | solution.py:299
  127.4 3.9 %collective-permute-start.23 = (f32[8,128]{1,0:T(8,128)S(1)}, f32[8,128]{1,0:T(8,128)S(1)}, u32[]{:S(2)}, u32[]{:S(2)}) collective-permute-start(f32[8,128]{1,0:T(8,128)S(1)} %add_add_fusion.1), channel_id=1, source_target_pairs={{0,32},{32,64},{64,96},{96,0},{1,33},{33,65},{65,97},{97,1},{2,34}... | collective-permute-start | bytes 12296 | tf_op jit(solution)/shard_map/ppermute | solution.py:299
  127.7 4.9 %collective-permute-start.28 = (bf16[128,512]{1,0:T(8,128)(2,1)S(1)}, bf16[128,512]{1,0:T(8,128)(2,1)S(1)}, u32[]{:S(2)}, u32[]{:S(2)}) collective-permute-start(bf16[128,512]{1,0:T(8,128)(2,1)S(1)} %pad_maximum_fusion.11), channel_id=1, source_target_pairs={{0,1},{1,0},{2,3},{3,2},{4,5},{5,4},{6,7},{7,6},{8,9},{9,8},{10,11... | collective-permute-start | bytes 393224 | tf_op jit(solution)/shard_map/ppermute | solution.py:318
  (8 other events, 22.5 us)

commit v4 on v3

v4 whole, which is shorter than its diff:
```python
import functools
import math

import jax
import jax.numpy as jnp
from jax import lax
from jax.experimental import pallas as pl
from jax.experimental.pallas import tpu as pltpu
from jax.sharding import Mesh, PartitionSpec as P

QH = 24
KVH = 4
HD = 128
CAP = 30.0
NEAR = 2
GROUP = QH // KVH
ROWS = 256
HALF = 128
WIDE = GROUP * ROWS
TILE = HALF
NOTE = 16
SLOTS = 9
BF = jnp.bfloat16
F32 = jnp.float32
SCALE = HD ** (-0.5)


def dot(a, b, over=(1, 0)):
    return lax.dot_general(a, b, (((over[0],), (over[1],)), ((), ())), preferred_element_type=F32)


def place_x_first(y):
    places = [(0, 0, 0), (1, 0, 4), (2, 0, 8)]
    for at, k in enumerate((1, 3, 2)):
        places += [(3 + at, 0, k), (3 + at, ROWS, 4 + k)]
    return places


def place_y_first(y):
    places = []
    for m in range(3):
        for at, k in enumerate((0, 1, 3, 2)):
            slot = 4 * m + k - jnp.where(y < k, 4, 0)
            places.append((m, at * (ROWS + NOTE), slot))
    return places


def attention_kernel(head, places_of, pieces, at_ref, len_ref, *refs):
    qm_ref, qo_ref, gm_ref, go_ref = refs[:4]
    piece_refs = refs[4:4 + pieces]
    att_ref, dq_ref, self_ref, *pair_refs = refs[4 + pieces:10 + pieces]
    keys, values, qs, gs, expo, slope, row_dot, dkv = refs[10 + pieces:]
    chip = at_ref[0]
    core = at_ref[1]
    row = lax.broadcasted_iota(jnp.int32, (HALF, 1), 0) + chip * ROWS
    row_pos = [row + core * HALF, row + (1 - core) * HALF]
    sub = lax.broadcasted_iota(jnp.int32, (1, ROWS), 1)
    key_off = sub + jnp.where(sub < HALF, core * HALF, (1 - core) * HALF - HALF)

    start = [jnp.zeros((HALF, 1), jnp.int32)] * 2
    low = jnp.int32(0)
    high = jnp.int32(0)
    edge = jnp.int32(0)
    for j in range(8):
        edge = edge + len_ref[j]
        start = [jnp.maximum(s, jnp.where(p >= edge, edge, 0)) for s, p in zip(start, row_pos)]
        low = jnp.maximum(low, jnp.where(chip * ROWS >= edge, edge, 0))
        high = jnp.maximum(high, jnp.where(chip * ROWS + ROWS - 1 >= edge, edge, 0))

    def needed(slot):
        return (slot <= chip) & ((chip - slot + 1) * ROWS > low)

    def block(slot):
        return pl.ds(pl.multiple_of(slot * ROWS, ROWS), ROWS)

    values[:, HD:] = jnp.ones((SLOTS * ROWS, HD), BF)
    for piece, first, slot in places_of(lax.rem(chip, 4)):
        @pl.when((slot >= 0) & (slot < SLOTS))
        def _():
            to = block(jnp.clip(slot, 0, SLOTS - 1))
            keys[to, :] = piece_refs[piece][first:first + ROWS, :HD]
            values[to, :HD] = piece_refs[piece][first:first + ROWS, HD:]

    for j in range(GROUP):
        cols = slice((head * GROUP + j) * HD, (head * GROUP + j + 1) * HD)
        for part, (q_in, g_in) in enumerate(((qm_ref, gm_ref), (qo_ref, go_ref))):
            rows = slice(j * ROWS + part * HALF, j * ROWS + (part + 1) * HALF)
            qs[rows, :] = q_in[:, cols]
            gs[rows, :] = g_in[:, cols]

    def forward(slot, masked):
        block_keys = keys[block(slot), :]
        for j in range(WIDE // TILE):
            rows = slice(j * TILE, (j + 1) * TILE)
            sq = jnp.tanh(dot(qs[rows, :], block_keys, (1, 1)) * (SCALE / CAP))
            e = jnp.exp2(sq * (CAP / math.log(2.0)))
            if masked:
                key_pos = (chip - slot) * ROWS + key_off
                e = jnp.where((key_pos >= start[j % 2]) & (key_pos <= row_pos[j % 2]), e, 0.0)
            expo[rows, block(slot)] = e.astype(BF)
            slope[rows, block(slot)] = (e * (1.0 - sq * sq)).astype(BF)

    def forward_step(slot, carry):
        plain = (slot > 0) & ((chip - slot) * ROWS >= high)

        @pl.when(needed(slot) & plain)
        def _():
            forward(slot, False)

        @pl.when(needed(slot) & jnp.logical_not(plain))
        def _():
            forward(slot, True)

        @pl.when(jnp.logical_not(needed(slot)))
        def _():
            expo[:, block(slot)] = jnp.zeros((WIDE, ROWS), BF)
            slope[:, block(slot)] = jnp.zeros((WIDE, ROWS), BF)

        return carry

    lax.fori_loop(0, SLOTS, forward_step, 0)

    for j in range(GROUP):
        rows = slice(j * ROWS, (j + 1) * ROWS)
        mixed = dot(expo[rows, :], values[...])
        inv = 1.0 / mixed[:, HD:]
        out = (mixed[:, :HD] * inv).astype(BF)
        att_ref[:, j * HD:(j + 1) * HD] = out
        g = (gs[rows, :].astype(F32) * inv).astype(BF)
        gs[rows, :] = g
        row_dot[rows, :] = jnp.broadcast_to(
            jnp.sum(g.astype(F32) * out.astype(F32), axis=1, keepdims=True), (ROWS, HD)
        )

    def backward(slot):
        block_values = values[block(slot), :HD]
        for j in range(WIDE // TILE):
            rows = slice(j * TILE, (j + 1) * TILE)
            dp = dot(gs[rows, :], block_values, (1, 1))
            rd = row_dot[rows, :]
            ds = slope[rows, block(slot)].astype(F32) * (dp - jnp.concatenate([rd, rd], axis=1))
            slope[rows, block(slot)] = ds.astype(BF)
        dkv[slot, :, :HD] = (dot(slope[:, block(slot)], qs[...], (0, 0)) * SCALE).astype(BF)
        dkv[slot, :, HD:] = dot(expo[:, block(slot)], gs[...], (0, 0)).astype(BF)

    def backward_step(slot, carry):
        @pl.when(needed(slot))
        def _():
            backward(slot)

        @pl.when(jnp.logical_not(needed(slot)))
        def _():
            dkv[slot] = jnp.zeros((ROWS, 2 * HD), BF)

        return carry

    lax.fori_loop(0, SLOTS, backward_step, 0)

    for j in range(GROUP):
        rows = slice(j * ROWS, (j + 1) * ROWS)
        dq_ref[:, j * HD:(j + 1) * HD] = (dot(slope[rows, :], keys[...]) * SCALE).astype(BF)
    for m in range(3):
        self_ref[m] = dkv[4 * m]
    for pair_ref, k in zip(pair_refs, (1, 3, 2)):
        pair_ref[:ROWS, :] = dkv[k]
        pair_ref[ROWS:, :] = dkv[4 + k]


def attention(head, places_of, at, lengths, qm, qo, gm, go, *pieces):
    smem = pl.BlockSpec(memory_space=pltpu.SMEM)
    vmem = pl.BlockSpec(memory_space=pltpu.VMEM)
    return pl.pallas_call(
        functools.partial(attention_kernel, head, places_of, len(pieces)),
        out_shape=(
            jax.ShapeDtypeStruct((ROWS, GROUP * HD), BF),
            jax.ShapeDtypeStruct((ROWS, GROUP * HD), BF),
            jax.ShapeDtypeStruct((3, ROWS, 2 * HD), BF),
        ) + (jax.ShapeDtypeStruct((2 * ROWS, 2 * HD), BF),) * 3,
        in_specs=[smem] * 2 + [vmem] * (4 + len(pieces)),
        out_specs=(vmem,) * 6,
        scratch_shapes=[
            pltpu.VMEM((SLOTS * ROWS, HD), BF),
            pltpu.VMEM((SLOTS * ROWS, 2 * HD), BF),
            pltpu.VMEM((WIDE, HD), BF),
            pltpu.VMEM((WIDE, HD), BF),
            pltpu.VMEM((WIDE, SLOTS * ROWS), BF),
            pltpu.VMEM((WIDE, SLOTS * ROWS), BF),
            pltpu.VMEM((WIDE, HD), F32),
            pltpu.VMEM((SLOTS, ROWS, 2 * HD), BF),
        ],
        compiler_params=pltpu.CompilerParams(vmem_limit_bytes=40 * 1024 * 1024),
        cost_estimate=pl.CostEstimate(
            flops=12 * WIDE * HD * ROWS * SLOTS * 4, bytes_accessed=6_000_000, transcendentals=7_000_000
        ),
    )(at, lengths, qm, qo, gm, go, *pieces)


def inverse(total_ref):
    total = jnp.sum(total_ref[...], axis=0, keepdims=True)
    return 1.0 / jnp.sum(total, axis=1, keepdims=True)


def finish_rows(core_ref, total_ref, att0, att1, dq0, dq1, others, out_ref, dq_ref):
    inv = inverse(total_ref)
    width = GROUP * HD
    for at, pair in ((0, (att0, att1)), (2, (dq0, dq1))):
        for to, mine in ((0, core_ref[0] == 0), (2 * width, core_ref[0] != 0)):
            for j, part in enumerate(pair):
                theirs = others[:, (at + j) * width:(at + j + 1) * width]
                rows = jnp.where(mine, part[:HALF, :], theirs)
                cols = slice(to + j * width, to + (j + 1) * width)
                if at == 0:
                    out_ref[:, cols] = rows
                else:
                    dq_ref[:, cols] = (rows.astype(F32) * inv).astype(BF)


def finish_keys(core_ref, total_ref, own, got, key_ref, value_ref):
    inv = inverse(total_ref)
    for to, mine in ((0, core_ref[0] == 0), (NEAR * HD, core_ref[0] != 0)):
        for h in range(NEAR):
            cols = slice(to + h * HD, to + (h + 1) * HD)
            for at, ref in ((2 * h * HD, key_ref), ((2 * h + 1) * HD, value_ref)):
                rows = jnp.where(mine, own[:HALF, at:at + HD], got[:, at:at + HD])
                ref[:, cols] = (rows.astype(F32) * inv).astype(BF)


def finish(kernel, core, *arrays, outs, width):
    vmem = pl.BlockSpec(memory_space=pltpu.VMEM)
    return pl.pallas_call(
        kernel,
        out_shape=(jax.ShapeDtypeStruct((HALF, width), BF),) * outs,
        in_specs=[pl.BlockSpec(memory_space=pltpu.SMEM)] + [vmem] * len(arrays),
        out_specs=(vmem,) * outs,
        compiler_params=pltpu.CompilerParams(vmem_limit_bytes=16 * 1024 * 1024),
    )(core.astype(jnp.int32).reshape(1), *arrays)


SWAP = [(0, 1), (1, 0)]


def ring(k):
    return [(i, (i + k) % 4) for i in range(4)]


def note(values):
    high = lax.reduce_precision(values, 8, 7)
    middle = lax.reduce_precision(values - high, 8, 7)
    rest = values - high - middle
    row = lax.broadcasted_iota(jnp.int32, (NOTE, HD), 0)
    parts = jnp.where(row == 0, high, jnp.where(row == 1, middle, jnp.where(row == 2, rest, 0.0)))
    return jnp.concatenate([parts, parts], axis=1).astype(BF)


def noted(array):
    return sum(array[at + ROWS:at + ROWS + 3, :HD].astype(F32) for at in range(0, 4 * (ROWS + NOTE), ROWS + NOTE))


def after(value, token):
    return lax.optimization_barrier((value, token))[0]


def send_y(pairs):
    return [lax.ppermute(pair, "y", ring(4 - k)) for pair, k in zip(pairs, (1, 3, 2))]


def scatter_y(selves, received, y):
    sums = [selves[m].astype(F32) for m in range(3)]
    for k, got in zip((1, 3, 2), received):
        got = got.astype(F32)
        over = y + k >= 4
        first, second = got[:ROWS], got[ROWS:]
        sums[0] = sums[0] + jnp.where(over, 0.0, first)
        sums[1] = sums[1] + jnp.where(over, first, second)
        sums[2] = sums[2] + jnp.where(over, second, 0.0)
    return sums[0], sums[1].astype(BF), sums[2].astype(BF)


def scatter_x(sums):
    t1 = lax.ppermute(sums[1], "x", ring(3))
    t2 = lax.ppermute(sums[2], "x", ring(2))
    return sums[0] + t1.astype(F32) + t2.astype(F32)


def body(queries, key_rows, value_rows, upstream, loss_weight, doc_lengths):
    x, y, core = lax.axis_index("x"), lax.axis_index("y"), lax.axis_index("core")
    weights_row = loss_weight[0]
    mine_at, other_at = core, 1 - core

    def half(array, at):
        size = array.shape[1] // 2
        return lax.dynamic_slice_in_dim(array, at * size, size, 1)

    def heads(at):
        k, v = half(key_rows[0], at), half(value_rows[0], at)
        return jnp.concatenate([k[:, :HD], v[:, :HD], k[:, HD:], v[:, HD:]], axis=1)

    weights = jnp.broadcast_to(weights_row[None], (8, HD))
    weights = weights + lax.ppermute(weights, "core", SWAP)
    kv_other = lax.ppermute(heads(other_at), "core", SWAP)
    own = jnp.concatenate([heads(mine_at), kv_other], axis=0)
    first = own[:, :2 * HD]
    second = jnp.concatenate([own[:, 2 * HD:], note(weights[:1])], axis=0)
    r1 = lax.ppermute(first, "x", ring(1))
    r2 = lax.ppermute(first, "x", ring(2))
    near = jnp.concatenate([second] + [lax.ppermute(second, "y", ring(k)) for k in (1, 3, 2)], axis=0)

    weighted = (upstream[0].astype(F32) * weights_row[:, None]).astype(BF)
    qm, gm = half(queries[0], mine_at), half(weighted, mine_at)
    q_send, g_send = after((half(queries[0], other_at), half(weighted, other_at)), first)
    qo = lax.ppermute(q_send, "core", SWAP)
    go = lax.ppermute(g_send, "core", SWAP)

    three = jnp.concatenate([first, r1, r2], axis=0)
    three = after(three, (qo, go))
    first_pieces = [first, r1, r2]
    for k in (1, 3, 2):
        pair = lax.dynamic_slice_in_dim(three, jnp.where(y + k >= 4, ROWS, 0), 2 * ROWS, 0)
        first_pieces.append(lax.ppermute(pair, "y", ring(k)))
    second_pieces = [near, lax.ppermute(near, "x", ring(1)), lax.ppermute(near, "x", ring(2))]

    at = jnp.stack([4 * x + y, core]).astype(jnp.int32)
    lengths = doc_lengths[0]
    att0, dq0, self0, *pairs0 = attention(0, place_x_first, at, lengths, qm, qo, gm, go, *first_pieces)
    att1, dq1, self1, *pairs1 = attention(1, place_y_first, after(at, att0), lengths, qm, qo, gm, go, *second_pieces)

    sent0 = send_y(pairs0)
    sums0 = scatter_y(self0, after(sent0, self1), y)
    grad0 = scatter_x(sums0)
    sent1 = send_y(pairs1)
    sums1 = scatter_y(self1, sent1, y)
    grad1 = scatter_x(sums1)

    total = noted(near)
    total = total + lax.ppermute(after(total, att0), "x", ring(3))
    total = after(total + noted(second_pieces[1]) + noted(second_pieces[2]), sums1[1])
    pieces = [total] + [lax.ppermute(total, "dp", ring(k)) for k in (1, 2, 3)]
    total = jnp.concatenate(pieces, axis=0)

    own_grad = jnp.concatenate([grad0, grad1], axis=1).astype(BF)

    parts = [att0, att1, dq0, dq1]
    others = jnp.concatenate([part[HALF:] for part in parts], axis=1)
    others = lax.ppermute(after(others, sums1[1]), "core", SWAP)
    out_rows, dq_rows = finish(finish_rows, core, total, *parts, others, outs=2, width=QH * HD)
    got = lax.ppermute(own_grad[HALF:], "core", SWAP)
    key_grad, value_grad = finish(finish_keys, core, total, own_grad, got, outs=2, width=KVH * HD)
    return (out_rows[None], dq_rows[None], key_grad[None], value_grad[None])


def solution(mesh):
    split = Mesh(mesh.devices.reshape(4, 4, 4, 2), ("dp", "x", "y", "core"))
    ctx = ("x", "y", "core")
    rows = P("dp", ctx, None)
    return jax.shard_map(
        body,
        mesh=split,
        in_specs=(rows, rows, rows, rows, P("dp", ctx), P("dp", None)),
        out_specs=(rows, rows, rows, rows),
        check_vma=False,
    )
```

time: 139 us -> 113 us (0.81); the launches traced: 136 us -> 112 us
  between operations: 16.7 us -> 1.06 us
  other arithmetic: 17 us -> 1.4 us
  Pallas kernels: 9.78 us -> 17.9 us
  local copies, waits for them, and re-layouts: 9.64 us -> 3.08 us
  waiting for transfers between devices: 15.6 us -> 21.3 us
    ppermute x2, starting transfers between devices: 15.5 us -> 0.01 us  [scatter_x(): t2 = lax.ppermute(sums[2], 'x', ring(2))]
    ppermute x2, starting transfers between devices: 7.73 us -> 14.8 us  [scatter_x(): t1 = lax.ppermute(sums[1], 'x', ring(3))]
    ppermute x11 -> x12, waiting for transfers between devices: 8.61 us -> 2.53 us  [the longest x6 2.52 us: send_y(): lax.ppermute(pair, 'y', ring(4 - k))]
    pallas_call x2, Pallas kernels: 9.78 us -> 15.7 us  [attention(): pl.pallas_call(functools.partial(attention_kernel, head, places_of, len(p...]
    ppermute x3, waiting for transfers between devices: 4.95 us -> 10.1 us  [body(): first_pieces.append(lax.ppermute(pair, 'y', ring(k)))]
    convert_element_type x5 -> x0, other arithmetic: 5.12 us -> none  [the longest x2 2.6 us: note(): return parts.astype(BF)]
    ppermute x11 -> x12, starting transfers between devices: 23.3 us -> 27.8 us  [the longest x6 11.8 us: send_y(): lax.ppermute(pair, 'y', ring(4 - k))]
    reduce_sum x5 -> x0, other arithmetic: 3.93 us -> none  [the longest x4 2.6 us: noted(): return jnp.sum(array[row, :3].astype(F32))]
  transfers between devices with their start and end apart: 29 -> 30, of which waited for: 6 -> 8; matrix products, arithmetic and copies ran while one was open for 12% -> 2% of each run, Pallas kernels for 7% -> 15%
where the time goes in v4:
time: 113 us; the launch traced here: 112 us
  starting transfers between devices  67 us (59%)
  waiting for transfers between devices  21.3 us (19%)
  Pallas kernels  17.9 us (16%)
  local copies, waits for them, and re-layouts  3.08 us (3%)
  other arithmetic  1.4 us (1%)
    pallas_call x2, Pallas kernels, attention(): pl.pallas_call(functools.partial(attention_kernel, head, places_of, len(p...  15.7 us
    ppermute x2, starting transfers between devices, scatter_x(): t1 = lax.ppermute(sums[1], 'x', ring(3))  14.8 us
    ppermute x6, starting transfers between devices, send_y(): lax.ppermute(pair, 'y', ring(4 - k))  11.8 us
    ppermute x3, waiting for transfers between devices, body(): first_pieces.append(lax.ppermute(pair, 'y', ring(k)))  10.1 us
    ppermute x1, starting transfers between devices, body(): total = total + lax.ppermute(after(total, att0), 'x', ring(3))  9.59 us
    ppermute x3, starting transfers between devices, body(): lax.ppermute(second, 'y', ring(k))  7.16 us
    ppermute x3, starting transfers between devices, body(): pieces = [total] + [lax.ppermute(total, 'dp', ring(k)) for k in (1, 2, 3)]  4.93 us
    ppermute x3, waiting for transfers between devices, body(): lax.ppermute(second, 'y', ring(k))  4.61 us
  transfers between devices with their start and end apart: 30, of which 8 were waited for; matrix products, arithmetic and copies ran while one was open for 2% of the time, Pallas kernels for 15%

profile of v4, /device:TPU:1, one launch (start us, length us, event | category | flops | bytes accessed | tf_op | source)
XLA Modules:
  0.0 111.8 jit_solution(13104352189793190003)
XLA Ops:
  1.4 1.4 %collective-permute-start = (f32[8,128]{1,0:T(8,128)S(1)}, f32[8,128]{1,0:T(8,128)S(1)}, u32[]{:S(2)}, u32[]{:S(2)}) collective-permute-start(f32[8,128]{1,0:T(8,128)S(1)} %broadcast_in_dim.67), channel_id=1, source_target_pairs={{0,1},{1,0},{2,3},{3,2},{4,5},{5,4},{6,7},{7,6},{8,9},{9,8},{10,11... | collective-permute-start | bytes 12296 | tf_op jit(solution)/shard_map/ppermute | solution.py:299
  2.8 1.0 dynamic-slice_bitcast_fusion.4
  4.3 1.1 copy-done.2
  5.7 2.9 %collective-permute-start.8 = (bf16[256,256]{1,0:T(8,128)(2,1)S(1)}, bf16[256,256]{1,0:T(8,128)(2,1)S(1)}, u32[]{:S(2)}, u32[]{:S(2)}) collective-permute-start(bf16[256,256]{1,0:T(8,128)(2,1)S(1)} %get-tuple-element.68.refs_4_), channel_id=1, source_target_pairs={{0,16},{8,24},{16,0},{24,8},{1,17},{9,25},{17,1},{25,9},{2,18},{10... | collective-permute-start | bytes 393224 | tf_op jit(solution)/shard_map/ppermute | solution.py:305
  8.9 1.4 %collective-permute-start.2 = (bf16[272,256]{1,0:T(8,128)(2,1)S(1)}, bf16[272,256]{1,0:T(8,128)(2,1)S(1)}, u32[]{:S(2)}, u32[]{:S(2)}) collective-permute-start(bf16[272,256]{1,0:T(8,128)(2,1)S(1)} %maximum_maximum_fusion), channel_id=1, source_target_pairs={{0,2},{2,4},{4,6},{6,0},{1,3},{3,5},{5,7},{7,1},{8,10},{10,12},{12... | collective-permute-start | bytes 417800 | tf_op jit(solution)/shard_map/ppermute | solution.py:306
  10.3 1.3 %collective-permute-start.5 = (bf16[128,1536]{1,0:T(8,128)(2,1)S(1)}, bf16[128,1536]{1,0:T(8,128)(2,1)S(1)}, u32[]{:S(2)}, u32[]{:S(2)}) collective-permute-start(bf16[128,1536]{1,0:T(8,128)(2,1)S(1)} %get-tuple-element.30), channel_id=1, source_target_pairs={{0,1},{1,0},{2,3},{3,2},{4,5},{5,4},{6,7},{7,6},{8,9},{9,8},{10,11... | collective-permute-start | bytes 1179656 | tf_op jit(solution)/shard_map/ppermute | solution.py:311
  11.8 3.0 %collective-permute-start.4 = (bf16[272,256]{1,0:T(8,128)(2,1)S(1)}, bf16[272,256]{1,0:T(8,128)(2,1)S(1)}, u32[]{:S(2)}, u32[]{:S(2)}) collective-permute-start(bf16[272,256]{1,0:T(8,128)(2,1)S(1)} %maximum_maximum_fusion), channel_id=1, source_target_pairs={{0,4},{2,6},{4,0},{6,2},{1,5},{3,7},{5,1},{7,3},{8,12},{10,14},{12... | collective-permute-start | bytes 417800 | tf_op jit(solution)/shard_map/ppermute | solution.py:306
  15.2 2.8 %collective-permute-start.3 = (bf16[272,256]{1,0:T(8,128)(2,1)S(1)}, bf16[272,256]{1,0:T(8,128)(2,1)S(1)}, u32[]{:S(2)}, u32[]{:S(2)}) collective-permute-start(bf16[272,256]{1,0:T(8,128)(2,1)S(1)} %maximum_maximum_fusion), channel_id=1, source_target_pairs={{0,6},{2,0},{4,2},{6,4},{1,7},{3,1},{5,3},{7,5},{8,14},{10,8},{12,... | collective-permute-start | bytes 417800 | tf_op jit(solution)/shard_map/ppermute | solution.py:306
  18.1 4.6 %collective-permute-done.3 = bf16[272,256]{1,0:T(8,128)(2,1)S(1)} collective-permute-done((bf16[272,256]{1,0:T(8,128)(2,1)S(1)}, bf16[272,256]{1,0:T(8,128)(2,1)S(1)}, u32[]{:S(2)}, u32[]{:S(2)}) %collective-permute-start.3) | collective-permute-done | bytes 139296 | tf_op jit(solution)/shard_map/ppermute | solution.py:306
  22.8 1.3 %collective-permute-start.11 = (bf16[512,256]{1,0:T(8,128)(2,1)S(1)}, bf16[512,256]{1,0:T(8,128)(2,1)S(1)}, u32[]{:S(2)}, u32[]{:S(2)}) collective-permute-start(bf16[512,256]{1,0:T(8,128)(2,1)S(1)} %get-tuple-element.64), channel_id=1, source_target_pairs={{0,4},{2,6},{4,0},{6,2},{1,5},{3,7},{5,1},{7,3},{8,12},{10,14},{12... | collective-permute-start | bytes 786440 | tf_op jit(solution)/shard_map/ppermute | solution.py:319
  24.1 2.3 %collective-permute-start.10 = (bf16[512,256]{1,0:T(8,128)(2,1)S(1)}, bf16[512,256]{1,0:T(8,128)(2,1)S(1)}, u32[]{:S(2)}, u32[]{:S(2)}) collective-permute-start(bf16[512,256]{1,0:T(8,128)(2,1)S(1)} %get-tuple-element.65), channel_id=1, source_target_pairs={{0,6},{2,0},{4,2},{6,4},{1,7},{3,1},{5,3},{7,5},{8,14},{10,8},{12,... | collective-permute-start | bytes 786440 | tf_op jit(solution)/shard_map/ppermute | solution.py:319
  27.1 1.3 %collective-permute-start.13 = (bf16[1088,256]{1,0:T(8,128)(2,1)S(1)}, bf16[1088,256]{1,0:T(8,128)(2,1)S(1)}, u32[]{:S(2)}, u32[]{:S(2)}) collective-permute-start(bf16[1088,256]{1,0:T(8,128)(2,1)S(1)} %constant_dynamic-update-slice_fusion.refs_4_), channel_id=1, source_target_pairs={{0,8},{8,16},{16,24},{24,0},{1,9},{9,17},{17,25},{25,1},{2,10},{10... | collective-permute-start | bytes 1671176 | tf_op jit(solution)/shard_map/ppermute | solution.py:320
  28.4 3.4 %collective-permute-done.11.refs_9_ = bf16[512,256]{1,0:T(8,128)(2,1)S(1)} collective-permute-done((bf16[512,256]{1,0:T(8,128)(2,1)S(1)}, bf16[512,256]{1,0:T(8,128)(2,1)S(1)}, u32[]{:S(2)}, u32[]{:S(2)}) %collective-permute-start.11) | collective-permute-done | bytes 262176 | tf_op jit(solution)/shard_map/ppermute | solution.py:319
  31.7 6.7 %collective-permute-done.10.refs_8_ = bf16[512,256]{1,0:T(8,128)(2,1)S(1)} collective-permute-done((bf16[512,256]{1,0:T(8,128)(2,1)S(1)}, bf16[512,256]{1,0:T(8,128)(2,1)S(1)}, u32[]{:S(2)}, u32[]{:S(2)}) %collective-permute-start.10) | collective-permute-done | bytes 262176 | tf_op jit(solution)/shard_map/ppermute | solution.py:319
  38.5 7.8 %shard_map.93 = (bf16[256,768]{1,0:T(8,128)(2,1)S(1)}, bf16[256,768]{1,0:T(8,128)(2,1)S(1)}, bf16[3,256,256]{2,1,0:T(8,128)(2,1)S(1)}, bf16[512,256]{1,0:T(8,128...) custom-call(s32[2]{0:T(128)S(1)} %pad_add_fusion.at_ref, s32[8]{0:T(128)S(1)} %bitcast.47, ...), custom_call_target="tpu_custom_call" | custom-call | flops 21743271936 | bytes 6000000 | tf_op jit(solution)/shard_map/pallas_call | solution.py:172
  46.3 9.6 %collective-permute-start.12 = (f32[3,128]{1,0:T(4,128)S(1)}, f32[3,128]{1,0:T(4,128)S(1)}, u32[]{:S(2)}, u32[]{:S(2)}) collective-permute-start(f32[3,128]{1,0:T(4,128)S(1)} %convert_add_fusion.6), channel_id=1, source_target_pairs={{0,24},{8,0},{16,8},{24,16},{1,25},{9,1},{17,9},{25,17},{2,26},{10... | collective-permute-start | bytes 4616 | tf_op jit(solution)/shard_map/ppermute | solution.py:335
  56.2 4.1 %collective-permute-start.23 = (bf16[512,256]{1,0:T(8,128)(2,1)S(1)}, bf16[512,256]{1,0:T(8,128)(2,1)S(1)}, u32[]{:S(2)}, u32[]{:S(2)}) collective-permute-start(bf16[512,256]{1,0:T(8,128)(2,1)S(1)} %get-tuple-element.49), channel_id=1, source_target_pairs={{0,2},{2,4},{4,6},{6,0},{1,3},{3,5},{5,7},{7,1},{8,10},{10,12},{12... | collective-permute-start | bytes 786440 | tf_op jit(solution)/shard_map/ppermute | solution.py:264
  60.3 1.7 %collective-permute-start.24 = (bf16[512,256]{1,0:T(8,128)(2,1)S(1)}, bf16[512,256]{1,0:T(8,128)(2,1)S(1)}, u32[]{:S(2)}, u32[]{:S(2)}) collective-permute-start(bf16[512,256]{1,0:T(8,128)(2,1)S(1)} %get-tuple-element.50), channel_id=1, source_target_pairs={{0,4},{2,6},{4,0},{6,2},{1,5},{3,7},{5,1},{7,3},{8,12},{10,14},{12... | collective-permute-start | bytes 786440 | tf_op jit(solution)/shard_map/ppermute | solution.py:264
  62.0 7.9 %shard_map.94 = (bf16[256,768]{1,0:T(8,128)(2,1)S(1)}, bf16[256,768]{1,0:T(8,128)(2,1)S(1)}, bf16[3,256,256]{2,1,0:T(8,128)(2,1)S(1)}, bf16[512,256]{1,0:T(8,128...) custom-call(s32[2]{0:T(128)S(1)} %pad_add_fusion.at_ref, s32[8]{0:T(128)S(1)} %bitcast.48, ...), custom_call_target="tpu_custom_call" | custom-call | flops 21743271936 | bytes 6000000 | tf_op jit(solution)/shard_map/pallas_call | solution.py:172
  70.0 3.6 %collective-permute-start.15 = (bf16[512,256]{1,0:T(8,128)(2,1)S(1)}, bf16[512,256]{1,0:T(8,128)(2,1)S(1)}, u32[]{:S(2)}, u32[]{:S(2)}) collective-permute-start(bf16[512,256]{1,0:T(8,128)(2,1)S(1)} %get-tuple-element.37), channel_id=1, source_target_pairs={{0,6},{2,0},{4,2},{6,4},{1,7},{3,1},{5,3},{7,5},{8,14},{10,8},{12,... | collective-permute-start | bytes 786440 | tf_op jit(solution)/shard_map/ppermute | solution.py:264
  73.7 2.1 %collective-permute-start.17 = (bf16[512,256]{1,0:T(8,128)(2,1)S(1)}, bf16[512,256]{1,0:T(8,128)(2,1)S(1)}, u32[]{:S(2)}, u32[]{:S(2)}) collective-permute-start(bf16[512,256]{1,0:T(8,128)(2,1)S(1)} %get-tuple-element.39), channel_id=1, source_target_pairs={{0,4},{2,6},{4,0},{6,2},{1,5},{3,7},{5,1},{7,3},{8,12},{10,14},{12... | collective-permute-start | bytes 786440 | tf_op jit(solution)/shard_map/ppermute | solution.py:264
  76.1 7.5 %collective-permute-start.25 = (bf16[256,256]{1,0:T(8,128)(2,1)S(1)}, bf16[256,256]{1,0:T(8,128)(2,1)S(1)}, u32[]{:S(2)}, u32[]{:S(2)}) collective-permute-start(bf16[256,256]{1,0:T(8,128)(2,1)S(1)} %get-tuple-element.56), channel_id=1, source_target_pairs={{0,24},{8,0},{16,8},{24,16},{1,25},{9,1},{17,9},{25,17},{2,26},{10... | collective-permute-start | bytes 393224 | tf_op jit(solution)/shard_map/ppermute | solution.py:280
  83.7 2.5 %collective-permute-done.17 = bf16[512,256]{1,0:T(8,128)(2,1)S(1)} collective-permute-done((bf16[512,256]{1,0:T(8,128)(2,1)S(1)}, bf16[512,256]{1,0:T(8,128)(2,1)S(1)}, u32[]{:S(2)}, u32[]{:S(2)}) %collective-permute-start.17) | collective-permute-done | bytes 262176 | tf_op jit(solution)/shard_map/ppermute | solution.py:264
  86.4 2.6 %collective-permute-start.20 = (f32[3,128]{1,0:T(4,128)S(1)}, f32[3,128]{1,0:T(4,128)S(1)}, u32[]{:S(2)}, u32[]{:S(2)}) collective-permute-start(f32[3,128]{1,0:T(4,128)S(1)} %add_add_fusion), channel_id=1, source_target_pairs={{0,96},{32,0},{64,32},{96,64},{1,97},{33,1},{65,33},{97,65},{2,98}... | collective-permute-start | bytes 4616 | tf_op jit(solution)/shard_map/ppermute | solution.py:337
  89.1 1.5 %collective-permute-start.19 = (f32[3,128]{1,0:T(4,128)S(1)}, f32[3,128]{1,0:T(4,128)S(1)}, u32[]{:S(2)}, u32[]{:S(2)}) collective-permute-start(f32[3,128]{1,0:T(4,128)S(1)} %add_add_fusion), channel_id=1, source_target_pairs={{0,64},{32,96},{64,0},{96,32},{1,65},{33,97},{65,1},{97,33},{2,66}... | collective-permute-start | bytes 4616 | tf_op jit(solution)/shard_map/ppermute | solution.py:337
  90.6 7.3 %collective-permute-start.27 = (bf16[256,256]{1,0:T(8,128)(2,1)S(1)}, bf16[256,256]{1,0:T(8,128)(2,1)S(1)}, u32[]{:S(2)}, u32[]{:S(2)}) collective-permute-start(bf16[256,256]{1,0:T(8,128)(2,1)S(1)} %get-tuple-element.59), channel_id=1, source_target_pairs={{0,24},{8,0},{16,8},{24,16},{1,25},{9,1},{17,9},{25,17},{2,26},{10... | collective-permute-start | bytes 393224 | tf_op jit(solution)/shard_map/ppermute | solution.py:280
  97.9 2.7 %collective-permute-start.21 = (bf16[128,3072]{1,0:T(8,128)(2,1)S(1)}, bf16[128,3072]{1,0:T(8,128)(2,1)S(1)}, u32[]{:S(2)}, u32[]{:S(2)}) collective-permute-start(bf16[128,3072]{1,0:T(8,128)(2,1)S(1)} %pad_maximum_fusion), channel_id=1, source_target_pairs={{0,1},{1,0},{2,3},{3,2},{4,5},{5,4},{6,7},{7,6},{8,9},{9,8},{10,11... | collective-permute-start | bytes 2359304 | tf_op jit(solution)/shard_map/ppermute | solution.py:344
  100.8 2.4 %collective-permute-done.28 = bf16[256,256]{1,0:T(8,128)(2,1)S(1)} collective-permute-done((bf16[256,256]{1,0:T(8,128)(2,1)S(1)}, bf16[256,256]{1,0:T(8,128)(2,1)S(1)}, u32[]{:S(2)}, u32[]{:S(2)}) %collective-permute-start.28) | collective-permute-done | bytes 131104 | tf_op jit(solution)/shard_map/ppermute | solution.py:281
  104.1 4.5 %collective-permute-start.29 = (bf16[128,512]{1,0:T(8,128)(2,1)S(1)}, bf16[128,512]{1,0:T(8,128)(2,1)S(1)}, u32[]{:S(2)}, u32[]{:S(2)}) collective-permute-start(bf16[128,512]{1,0:T(8,128)(2,1)S(1)} %fusion.23), channel_id=1, source_target_pairs={{0,1},{1,0},{2,3},{3,2},{4,5},{5,4},{6,7},{7,6},{8,9},{9,8},{10,11... | collective-permute-start | bytes 393224 | tf_op jit(solution)/shard_map/ppermute | solution.py:346
  108.7 0.9 collective-permute-done.29.got
  109.6 0.8 shard_map.96
  110.4 1.4 %shard_map.95 = (bf16[128,3072]{1,0:T(8,128)(2,1)}, bf16[128,3072]{1,0:T(8,128)(2,1)}) custom-call(s32[1]{0:T(128)} %bitcast.core_ref, f32[12,128]{1,0:T(8,128)S(1)} %pad_maximum_fusion.5.total_ref, bf16[256,768]{1,0:T(8,128)(2,1)S(1)} %get-tuple-element.33.att0, bf16[256,768]{1,0:T(8,128)(2,1)S(1)} %get-tuple-element.41.att1, ...), custom_call_target="tpu_custom_call" | custom-call | tf_op jit(solution)/shard_map/pallas_call | solution.py:230
  (85 shorter events, 5.3 us)
Async XLA Ops:
  0.6 3.3 %copy-start.3 = (f32[1,128]{1,0:T(1,128)S(1)}, f32[1,128]{1,0:T(1,128)}, u32[]{:S(2)}) copy-start(f32[1,128]{1,0:T(1,128)} %param.10) | copy-start | bytes 1540
  1.4 4.1 %collective-permute-start = (f32[8,128]{1,0:T(8,128)S(1)}, f32[8,128]{1,0:T(8,128)S(1)}, u32[]{:S(2)}, u32[]{:S(2)}) collective-permute-start(f32[8,128]{1,0:T(8,128)S(1)} %broadcast_in_dim.67), channel_id=1, source_target_pairs={{0,1},{1,0},{2,3},{3,2},{4,5},{5,4},{6,7},{7,6},{8,9},{9,8},{10,11... | collective-permute-start | bytes 12296 | tf_op jit(solution)/shard_map/ppermute | solution.py:299
  3.8 1.8 %collective-permute-start.1 = (bf16[128,512]{1,0:T(8,128)(2,1)S(1)}, bf16[128,512]{1,0:T(8,128)(2,1)S(1)}, u32[]{:S(2)}, u32[]{:S(2)}) collective-permute-start(bf16[128,512]{1,0:T(8,128)(2,1)S(1)} %pad_maximum_fusion.4), channel_id=1, source_target_pairs={{0,1},{1,0},{2,3},{3,2},{4,5},{5,4},{6,7},{7,6},{8,9},{9,8},{10,11... | collective-permute-start | bytes 393224 | tf_op jit(solution)/shard_map/ppermute | solution.py:300
  5.7 6.2 %collective-permute-start.8 = (bf16[256,256]{1,0:T(8,128)(2,1)S(1)}, bf16[256,256]{1,0:T(8,128)(2,1)S(1)}, u32[]{:S(2)}, u32[]{:S(2)}) collective-permute-start(bf16[256,256]{1,0:T(8,128)(2,1)S(1)} %get-tuple-element.68.refs_4_), channel_id=1, source_target_pairs={{0,16},{8,24},{16,0},{24,8},{1,17},{9,25},{17,1},{25,9},{2,18},{10... | collective-permute-start | bytes 393224 | tf_op jit(solution)/shard_map/ppermute | solution.py:305
  8.6 6.7 %collective-permute-start.7 = (bf16[256,256]{1,0:T(8,128)(2,1)S(1)}, bf16[256,256]{1,0:T(8,128)(2,1)S(1)}, u32[]{:S(2)}, u32[]{:S(2)}) collective-permute-start(bf16[256,256]{1,0:T(8,128)(2,1)S(1)} %get-tuple-element.68.refs_4_), channel_id=1, source_target_pairs={{0,8},{8,16},{16,24},{24,0},{1,9},{9,17},{17,25},{25,1},{2,10},{10... | collective-permute-start | bytes 393224 | tf_op jit(solution)/shard_map/ppermute | solution.py:304
  8.9 9.2 %collective-permute-start.2 = (bf16[272,256]{1,0:T(8,128)(2,1)S(1)}, bf16[272,256]{1,0:T(8,128)(2,1)S(1)}, u32[]{:S(2)}, u32[]{:S(2)}) collective-permute-start(bf16[272,256]{1,0:T(8,128)(2,1)S(1)} %maximum_maximum_fusion), channel_id=1, source_target_pairs={{0,2},{2,4},{4,6},{6,0},{1,3},{3,5},{5,7},{7,1},{8,10},{10,12},{12... | collective-permute-start | bytes 417800 | tf_op jit(solution)/shard_map/ppermute | solution.py:306
  10.3 12.5 %collective-permute-start.5 = (bf16[128,1536]{1,0:T(8,128)(2,1)S(1)}, bf16[128,1536]{1,0:T(8,128)(2,1)S(1)}, u32[]{:S(2)}, u32[]{:S(2)}) collective-permute-start(bf16[128,1536]{1,0:T(8,128)(2,1)S(1)} %get-tuple-element.30), channel_id=1, source_target_pairs={{0,1},{1,0},{2,3},{3,2},{4,5},{5,4},{6,7},{7,6},{8,9},{9,8},{10,11... | collective-permute-start | bytes 1179656 | tf_op jit(solution)/shard_map/ppermute | solution.py:311
  11.6 11.2 %collective-permute-start.6 = (bf16[128,1536]{1,0:T(8,128)(2,1)S(1)}, bf16[128,1536]{1,0:T(8,128)(2,1)S(1)}, u32[]{:S(2)}, u32[]{:S(2)}) collective-permute-start(bf16[128,1536]{1,0:T(8,128)(2,1)S(1)} %get-tuple-element.31), channel_id=1, source_target_pairs={{0,1},{1,0},{2,3},{3,2},{4,5},{5,4},{6,7},{7,6},{8,9},{9,8},{10,11... | collective-permute-start | bytes 1179656 | tf_op jit(solution)/shard_map/ppermute | solution.py:312
  11.8 15.1 %collective-permute-start.4 = (bf16[272,256]{1,0:T(8,128)(2,1)S(1)}, bf16[272,256]{1,0:T(8,128)(2,1)S(1)}, u32[]{:S(2)}, u32[]{:S(2)}) collective-permute-start(bf16[272,256]{1,0:T(8,128)(2,1)S(1)} %maximum_maximum_fusion), channel_id=1, source_target_pairs={{0,4},{2,6},{4,0},{6,2},{1,5},{3,7},{5,1},{7,3},{8,12},{10,14},{12... | collective-permute-start | bytes 417800 | tf_op jit(solution)/shard_map/ppermute | solution.py:306
  15.2 7.5 %collective-permute-start.3 = (bf16[272,256]{1,0:T(8,128)(2,1)S(1)}, bf16[272,256]{1,0:T(8,128)(2,1)S(1)}, u32[]{:S(2)}, u32[]{:S(2)}) collective-permute-start(bf16[272,256]{1,0:T(8,128)(2,1)S(1)} %maximum_maximum_fusion), channel_id=1, source_target_pairs={{0,6},{2,0},{4,2},{6,4},{1,7},{3,1},{5,3},{7,5},{8,14},{10,8},{12,... | collective-permute-start | bytes 417800 | tf_op jit(solution)/shard_map/ppermute | solution.py:306
  22.7 15.7 %copy-start = (s32[1,8]{1,0:T(1,128)S(1)}, s32[1,8]{1,0:T(1,128)}, u32[]{:S(2)}) copy-start(s32[1,8]{1,0:T(1,128)} %param.11) | copy-start | bytes 100
  22.8 8.9 %collective-permute-start.11 = (bf16[512,256]{1,0:T(8,128)(2,1)S(1)}, bf16[512,256]{1,0:T(8,128)(2,1)S(1)}, u32[]{:S(2)}, u32[]{:S(2)}) collective-permute-start(bf16[512,256]{1,0:T(8,128)(2,1)S(1)} %get-tuple-element.64), channel_id=1, source_target_pairs={{0,4},{2,6},{4,0},{6,2},{1,5},{3,7},{5,1},{7,3},{8,12},{10,14},{12... | collective-permute-start | bytes 786440 | tf_op jit(solution)/shard_map/ppermute | solution.py:319
  24.1 14.3 %collective-permute-start.10 = (bf16[512,256]{1,0:T(8,128)(2,1)S(1)}, bf16[512,256]{1,0:T(8,128)(2,1)S(1)}, u32[]{:S(2)}, u32[]{:S(2)}) collective-permute-start(bf16[512,256]{1,0:T(8,128)(2,1)S(1)} %get-tuple-element.65), channel_id=1, source_target_pairs={{0,6},{2,0},{4,2},{6,4},{1,7},{3,1},{5,3},{7,5},{8,14},{10,8},{12,... | collective-permute-start | bytes 786440 | tf_op jit(solution)/shard_map/ppermute | solution.py:319
  26.4 12.1 %collective-permute-start.9 = (bf16[512,256]{1,0:T(8,128)(2,1)S(1)}, bf16[512,256]{1,0:T(8,128)(2,1)S(1)}, u32[]{:S(2)}, u32[]{:S(2)}) collective-permute-start(bf16[512,256]{1,0:T(8,128)(2,1)S(1)} %get-tuple-element.66), channel_id=1, source_target_pairs={{0,2},{2,4},{4,6},{6,0},{1,3},{3,5},{5,7},{7,1},{8,10},{10,12},{12... | collective-permute-start | bytes 786440 | tf_op jit(solution)/shard_map/ppermute | solution.py:319
  26.9 33.4 %collective-permute-start.14 = (bf16[1088,256]{1,0:T(8,128)(2,1)S(1)}, bf16[1088,256]{1,0:T(8,128)(2,1)S(1)}, u32[]{:S(2)}, u32[]{:S(2)}) collective-permute-start(bf16[1088,256]{1,0:T(8,128)(2,1)S(1)} %constant_dynamic-update-slice_fusion.refs_4_), channel_id=1, source_target_pairs={{0,16},{8,24},{16,0},{24,8},{1,17},{9,25},{17,1},{25,9},{2,18},{10... | collective-permute-start | bytes 1671176 | tf_op jit(solution)/shard_map/ppermute | solution.py:320
  27.1 35.0 %collective-permute-start.13 = (bf16[1088,256]{1,0:T(8,128)(2,1)S(1)}, bf16[1088,256]{1,0:T(8,128)(2,1)S(1)}, u32[]{:S(2)}, u32[]{:S(2)}) collective-permute-start(bf16[1088,256]{1,0:T(8,128)(2,1)S(1)} %constant_dynamic-update-slice_fusion.refs_4_), channel_id=1, source_target_pairs={{0,8},{8,16},{16,24},{24,0},{1,9},{9,17},{17,25},{25,1},{2,10},{10... | collective-permute-start | bytes 1671176 | tf_op jit(solution)/shard_map/ppermute | solution.py:320
  46.3 27.3 %collective-permute-start.12 = (f32[3,128]{1,0:T(4,128)S(1)}, f32[3,128]{1,0:T(4,128)S(1)}, u32[]{:S(2)}, u32[]{:S(2)}) collective-permute-start(f32[3,128]{1,0:T(4,128)S(1)} %convert_add_fusion.6), channel_id=1, source_target_pairs={{0,24},{8,0},{16,8},{24,16},{1,25},{9,1},{17,9},{25,17},{2,26},{10... | collective-permute-start | bytes 4616 | tf_op jit(solution)/shard_map/ppermute | solution.py:335
  55.9 17.8 %collective-permute-start.22 = (bf16[512,256]{1,0:T(8,128)(2,1)S(1)}, bf16[512,256]{1,0:T(8,128)(2,1)S(1)}, u32[]{:S(2)}, u32[]{:S(2)}) collective-permute-start(bf16[512,256]{1,0:T(8,128)(2,1)S(1)} %get-tuple-element.48), channel_id=1, source_target_pairs={{0,6},{2,0},{4,2},{6,4},{1,7},{3,1},{5,3},{7,5},{8,14},{10,8},{12,... | collective-permute-start | bytes 786440 | tf_op jit(solution)/shard_map/ppermute | solution.py:264
  56.2 19.6 %collective-permute-start.23 = (bf16[512,256]{1,0:T(8,128)(2,1)S(1)}, bf16[512,256]{1,0:T(8,128)(2,1)S(1)}, u32[]{:S(2)}, u32[]{:S(2)}) collective-permute-start(bf16[512,256]{1,0:T(8,128)(2,1)S(1)} %get-tuple-element.49), channel_id=1, source_target_pairs={{0,2},{2,4},{4,6},{6,0},{1,3},{3,5},{5,7},{7,1},{8,10},{10,12},{12... | collective-permute-start | bytes 786440 | tf_op jit(solution)/shard_map/ppermute | solution.py:264
  60.3 15.5 %collective-permute-start.24 = (bf16[512,256]{1,0:T(8,128)(2,1)S(1)}, bf16[512,256]{1,0:T(8,128)(2,1)S(1)}, u32[]{:S(2)}, u32[]{:S(2)}) collective-permute-start(bf16[512,256]{1,0:T(8,128)(2,1)S(1)} %get-tuple-element.50), channel_id=1, source_target_pairs={{0,4},{2,6},{4,0},{6,2},{1,5},{3,7},{5,1},{7,3},{8,12},{10,14},{12... | collective-permute-start | bytes 786440 | tf_op jit(solution)/shard_map/ppermute | solution.py:264
  70.0 13.6 %collective-permute-start.15 = (bf16[512,256]{1,0:T(8,128)(2,1)S(1)}, bf16[512,256]{1,0:T(8,128)(2,1)S(1)}, u32[]{:S(2)}, u32[]{:S(2)}) collective-permute-start(bf16[512,256]{1,0:T(8,128)(2,1)S(1)} %get-tuple-element.37), channel_id=1, source_target_pairs={{0,6},{2,0},{4,2},{6,4},{1,7},{3,1},{5,3},{7,5},{8,14},{10,8},{12,... | collective-permute-start | bytes 786440 | tf_op jit(solution)/shard_map/ppermute | solution.py:264
  73.6 10.0 %collective-permute-start.16 = (bf16[512,256]{1,0:T(8,128)(2,1)S(1)}, bf16[512,256]{1,0:T(8,128)(2,1)S(1)}, u32[]{:S(2)}, u32[]{:S(2)}) collective-permute-start(bf16[512,256]{1,0:T(8,128)(2,1)S(1)} %get-tuple-element.38), channel_id=1, source_target_pairs={{0,2},{2,4},{4,6},{6,0},{1,3},{3,5},{5,7},{7,1},{8,10},{10,12},{12... | collective-permute-start | bytes 786440 | tf_op jit(solution)/shard_map/ppermute | solution.py:264
  73.7 12.5 %collective-permute-start.17 = (bf16[512,256]{1,0:T(8,128)(2,1)S(1)}, bf16[512,256]{1,0:T(8,128)(2,1)S(1)}, u32[]{:S(2)}, u32[]{:S(2)}) collective-permute-start(bf16[512,256]{1,0:T(8,128)(2,1)S(1)} %get-tuple-element.39), channel_id=1, source_target_pairs={{0,4},{2,6},{4,0},{6,2},{1,5},{3,7},{5,1},{7,3},{8,12},{10,14},{12... | collective-permute-start | bytes 786440 | tf_op jit(solution)/shard_map/ppermute | solution.py:264
  76.1 21.8 %collective-permute-start.25 = (bf16[256,256]{1,0:T(8,128)(2,1)S(1)}, bf16[256,256]{1,0:T(8,128)(2,1)S(1)}, u32[]{:S(2)}, u32[]{:S(2)}) collective-permute-start(bf16[256,256]{1,0:T(8,128)(2,1)S(1)} %get-tuple-element.56), channel_id=1, source_target_pairs={{0,24},{8,0},{16,8},{24,16},{1,25},{9,1},{17,9},{25,17},{2,26},{10... | collective-permute-start | bytes 393224 | tf_op jit(solution)/shard_map/ppermute | solution.py:280
  83.6 14.3 %collective-permute-start.26 = (bf16[256,256]{1,0:T(8,128)(2,1)S(1)}, bf16[256,256]{1,0:T(8,128)(2,1)S(1)}, u32[]{:S(2)}, u32[]{:S(2)}) collective-permute-start(bf16[256,256]{1,0:T(8,128)(2,1)S(1)} %get-tuple-element.57), channel_id=1, source_target_pairs={{0,16},{8,24},{16,0},{24,8},{1,17},{9,25},{17,1},{25,9},{2,18},{10... | collective-permute-start | bytes 393224 | tf_op jit(solution)/shard_map/ppermute | solution.py:281
  86.4 22.2 %collective-permute-start.20 = (f32[3,128]{1,0:T(4,128)S(1)}, f32[3,128]{1,0:T(4,128)S(1)}, u32[]{:S(2)}, u32[]{:S(2)}) collective-permute-start(f32[3,128]{1,0:T(4,128)S(1)} %add_add_fusion), channel_id=1, source_target_pairs={{0,96},{32,0},{64,32},{96,64},{1,97},{33,1},{65,33},{97,65},{2,98}... | collective-permute-start | bytes 4616 | tf_op jit(solution)/shard_map/ppermute | solution.py:337
  89.1 19.5 %collective-permute-start.19 = (f32[3,128]{1,0:T(4,128)S(1)}, f32[3,128]{1,0:T(4,128)S(1)}, u32[]{:S(2)}, u32[]{:S(2)}) collective-permute-start(f32[3,128]{1,0:T(4,128)S(1)} %add_add_fusion), channel_id=1, source_target_pairs={{0,64},{32,96},{64,0},{96,32},{1,65},{33,97},{65,1},{97,33},{2,66}... | collective-permute-start | bytes 4616 | tf_op jit(solution)/shard_map/ppermute | solution.py:337
  90.6 13.4 %collective-permute-start.27 = (bf16[256,256]{1,0:T(8,128)(2,1)S(1)}, bf16[256,256]{1,0:T(8,128)(2,1)S(1)}, u32[]{:S(2)}, u32[]{:S(2)}) collective-permute-start(bf16[256,256]{1,0:T(8,128)(2,1)S(1)} %get-tuple-element.59), channel_id=1, source_target_pairs={{0,24},{8,0},{16,8},{24,16},{1,25},{9,1},{17,9},{25,17},{2,26},{10... | collective-permute-start | bytes 393224 | tf_op jit(solution)/shard_map/ppermute | solution.py:280
  97.9 5.3 %collective-permute-start.28 = (bf16[256,256]{1,0:T(8,128)(2,1)S(1)}, bf16[256,256]{1,0:T(8,128)(2,1)S(1)}, u32[]{:S(2)}, u32[]{:S(2)}) collective-permute-start(bf16[256,256]{1,0:T(8,128)(2,1)S(1)} %get-tuple-element.58), channel_id=1, source_target_pairs={{0,16},{8,24},{16,0},{24,8},{1,17},{9,25},{17,1},{25,9},{2,18},{10... | collective-permute-start | bytes 393224 | tf_op jit(solution)/shard_map/ppermute | solution.py:281
  97.9 12.5 %collective-permute-start.21 = (bf16[128,3072]{1,0:T(8,128)(2,1)S(1)}, bf16[128,3072]{1,0:T(8,128)(2,1)S(1)}, u32[]{:S(2)}, u32[]{:S(2)}) collective-permute-start(bf16[128,3072]{1,0:T(8,128)(2,1)S(1)} %pad_maximum_fusion), channel_id=1, source_target_pairs={{0,1},{1,0},{2,3},{3,2},{4,5},{5,4},{6,7},{7,6},{8,9},{9,8},{10,11... | collective-permute-start | bytes 2359304 | tf_op jit(solution)/shard_map/ppermute | solution.py:344
  103.2 5.4 %collective-permute-start.18 = (f32[3,128]{1,0:T(4,128)S(1)}, f32[3,128]{1,0:T(4,128)S(1)}, u32[]{:S(2)}, u32[]{:S(2)}) collective-permute-start(f32[3,128]{1,0:T(4,128)S(1)} %add_add_fusion), channel_id=1, source_target_pairs={{0,32},{32,64},{64,96},{96,0},{1,33},{33,65},{65,97},{97,1},{2,34}... | collective-permute-start | bytes 4616 | tf_op jit(solution)/shard_map/ppermute | solution.py:337
  104.1 5.4 %collective-permute-start.29 = (bf16[128,512]{1,0:T(8,128)(2,1)S(1)}, bf16[128,512]{1,0:T(8,128)(2,1)S(1)}, u32[]{:S(2)}, u32[]{:S(2)}) collective-permute-start(bf16[128,512]{1,0:T(8,128)(2,1)S(1)} %fusion.23), channel_id=1, source_target_pairs={{0,1},{1,0},{2,3},{3,2},{4,5},{5,4},{6,7},{7,6},{8,9},{9,8},{10,11... | collective-permute-start | bytes 393224 | tf_op jit(solution)/shard_map/ppermute | solution.py:346
  (2 other events, 4.5 us)

commit v5 on v4

--- a/solution.py
+++ b/solution.py
@@ -303,7 +303,7 @@
     second = jnp.concatenate([own[:, 2 * HD:], note(weights[:1])], axis=0)
     r1 = lax.ppermute(first, "x", ring(1))
     r2 = lax.ppermute(first, "x", ring(2))
-    near = jnp.concatenate([second] + [lax.ppermute(second, "y", ring(k)) for k in (1, 3, 2)], axis=0)
+    nearest = [lax.ppermute(second, "y", ring(k)) for k in (1, 3, 2)]
 
     weighted = (upstream[0].astype(F32) * weights_row[:, None]).astype(BF)
     qm, gm = half(queries[0], mine_at), half(weighted, mine_at)
@@ -317,6 +317,7 @@
     for k in (1, 3, 2):
         pair = lax.dynamic_slice_in_dim(three, jnp.where(y + k >= 4, ROWS, 0), 2 * ROWS, 0)
         first_pieces.append(lax.ppermute(pair, "y", ring(k)))
+    near = jnp.concatenate([second] + nearest, axis=0)
     second_pieces = [near, lax.ppermute(near, "x", ring(1)), lax.ppermute(near, "x", ring(2))]
 
     at = jnp.stack([4 * x + y, core]).astype(jnp.int32)
@@ -328,22 +329,24 @@
     sums0 = scatter_y(self0, after(sent0, self1), y)
     grad0 = scatter_x(sums0)
     sent1 = send_y(pairs1)
+
     sums1 = scatter_y(self1, sent1, y)
     grad1 = scatter_x(sums1)
 
     total = noted(near)
     total = total + lax.ppermute(after(total, att0), "x", ring(3))
-    total = after(total + noted(second_pieces[1]) + noted(second_pieces[2]), sums1[1])
+    total = after(total + noted(second_pieces[1]) + noted(second_pieces[2]), grad0)
     pieces = [total] + [lax.ppermute(total, "dp", ring(k)) for k in (1, 2, 3)]
     total = jnp.concatenate(pieces, axis=0)
-
-    own_grad = jnp.concatenate([grad0, grad1], axis=1).astype(BF)
 
     parts = [att0, att1, dq0, dq1]
     others = jnp.concatenate([part[HALF:] for part in parts], axis=1)
     others = lax.ppermute(after(others, sums1[1]), "core", SWAP)
+
+    own_grad = jnp.concatenate([grad0, grad1], axis=1).astype(BF)
+
     out_rows, dq_rows = finish(finish_rows, core, total, *parts, others, outs=2, width=QH * HD)
-    got = lax.ppermute(own_grad[HALF:], "core", SWAP)
+    got = lax.ppermute(after(own_grad[HALF:], out_rows), "core", SWAP)
     key_grad, value_grad = finish(finish_keys, core, total, own_grad, got, outs=2, width=KVH * HD)
     return (out_rows[None], dq_rows[None], key_grad[None], value_grad[None])
 

time: 113 us -> 114 us (level)
  waiting for transfers between devices: 21.3 us -> 26.5 us
  starting transfers between devices: 67 us -> 63.8 us
    ppermute x1, starting transfers between devices: 9.59 us -> 3.41 us  [body(): total = total + lax.ppermute(after(total, att0), 'x', ring(3))]
    ppermute x2, starting transfers between devices: 14.8 us -> 9.09 us  [scatter_x(): t1 = lax.ppermute(sums[1], 'x', ring(3))]
    ppermute x2, starting transfers between devices: 0.01 us -> 5.67 us  [scatter_x(): t2 = lax.ppermute(sums[2], 'x', ring(2))]
    ppermute x3, waiting for transfers between devices: 0.01 us -> 4.91 us  [body(): pieces = [total] + [lax.ppermute(total, 'dp', ring(k)) for k in (1, 2, 3)]]
    ppermute x6, starting transfers between devices: 11.8 us -> 15.7 us  [send_y(): lax.ppermute(pair, 'y', ring(4 - k))]
    ppermute x6, waiting for transfers between devices: 2.52 us -> 5.23 us  [send_y(): lax.ppermute(pair, 'y', ring(4 - k))]
    ppermute x2, waiting for transfers between devices: 2.44 us -> 0.01 us  [scatter_x(): t2 = lax.ppermute(sums[2], 'x', ring(2))]
    ppermute x4, starting transfers between devices: 11.6 us -> 9.2 us  [the longest x3 7.16 us: body(): nearest = [lax.ppermute(second, 'y', ring(k)) for k in (1, 3, 2)]]
  transfers between devices with their start and end apart: 30 -> 30, of which waited for: 8 -> 10; matrix products, arithmetic and copies ran while one was open for 2% -> 2% of each run, Pallas kernels for 15% -> 14%
where the time goes in v5:
time: 114 us
  starting transfers between devices  63.8 us (56%)
  waiting for transfers between devices  26.5 us (23%)
  Pallas kernels  17.9 us (16%)
  local copies, waits for them, and re-layouts  3.08 us (3%)
  other arithmetic  1.4 us (1%)
    pallas_call x2, Pallas kernels, attention(): pl.pallas_call(functools.partial(attention_kernel, head, places_of, len(p...  15.8 us
    ppermute x6, starting transfers between devices, send_y(): lax.ppermute(pair, 'y', ring(4 - k))  15.7 us
    ppermute x3, waiting for transfers between devices, body(): first_pieces.append(lax.ppermute(pair, 'y', ring(k)))  10.1 us
    ppermute x2, starting transfers between devices, scatter_x(): t1 = lax.ppermute(sums[1], 'x', ring(3))  9.09 us
    ppermute x3, starting transfers between devices, body(): nearest = [lax.ppermute(second, 'y', ring(k)) for k in (1, 3, 2)]  7.16 us
    ppermute x3, starting transfers between devices, body(): pieces = [total] + [lax.ppermute(total, 'dp', ring(k)) for k in (1, 2, 3)]  6.89 us
    ppermute x2, starting transfers between devices, scatter_x(): t2 = lax.ppermute(sums[2], 'x', ring(2))  5.67 us
    ppermute x6, waiting for transfers between devices, send_y(): lax.ppermute(pair, 'y', ring(4 - k))  5.23 us
  transfers between devices with their start and end apart: 30, of which 10 were waited for; matrix products, arithmetic and copies ran while one was open for 2% of the time, Pallas kernels for 14%

profile of v5, /device:TPU:1, one launch (start us, length us, event | category | flops | bytes accessed | tf_op | source)
XLA Modules:
  0.0 113.7 jit_solution(7710637394110041209)
XLA Ops:
  1.4 1.4 %collective-permute-start = (f32[8,128]{1,0:T(8,128)S(1)}, f32[8,128]{1,0:T(8,128)S(1)}, u32[]{:S(2)}, u32[]{:S(2)}) collective-permute-start(f32[8,128]{1,0:T(8,128)S(1)} %broadcast_in_dim.67), channel_id=1, source_target_pairs={{0,1},{1,0},{2,3},{3,2},{4,5},{5,4},{6,7},{7,6},{8,9},{9,8},{10,11... | collective-permute-start | bytes 12296 | tf_op jit(solution)/shard_map/ppermute | solution.py:299
  2.8 1.0 dynamic-slice_bitcast_fusion.4
  4.3 1.1 copy-done.2
  5.7 2.9 %collective-permute-start.8 = (bf16[256,256]{1,0:T(8,128)(2,1)S(1)}, bf16[256,256]{1,0:T(8,128)(2,1)S(1)}, u32[]{:S(2)}, u32[]{:S(2)}) collective-permute-start(bf16[256,256]{1,0:T(8,128)(2,1)S(1)} %get-tuple-element.70.refs_4_), channel_id=1, source_target_pairs={{0,16},{8,24},{16,0},{24,8},{1,17},{9,25},{17,1},{25,9},{2,18},{10... | collective-permute-start | bytes 393224 | tf_op jit(solution)/shard_map/ppermute | solution.py:305
  8.9 1.4 %collective-permute-start.2 = (bf16[272,256]{1,0:T(8,128)(2,1)S(1)}, bf16[272,256]{1,0:T(8,128)(2,1)S(1)}, u32[]{:S(2)}, u32[]{:S(2)}) collective-permute-start(bf16[272,256]{1,0:T(8,128)(2,1)S(1)} %maximum_maximum_fusion), channel_id=1, source_target_pairs={{0,2},{2,4},{4,6},{6,0},{1,3},{3,5},{5,7},{7,1},{8,10},{10,12},{12... | collective-permute-start | bytes 417800 | tf_op jit(solution)/shard_map/ppermute | solution.py:306
  10.3 1.3 %collective-permute-start.5 = (bf16[128,1536]{1,0:T(8,128)(2,1)S(1)}, bf16[128,1536]{1,0:T(8,128)(2,1)S(1)}, u32[]{:S(2)}, u32[]{:S(2)}) collective-permute-start(bf16[128,1536]{1,0:T(8,128)(2,1)S(1)} %get-tuple-element.31), channel_id=1, source_target_pairs={{0,1},{1,0},{2,3},{3,2},{4,5},{5,4},{6,7},{7,6},{8,9},{9,8},{10,11... | collective-permute-start | bytes 1179656 | tf_op jit(solution)/shard_map/ppermute | solution.py:311
  11.8 3.0 %collective-permute-start.4 = (bf16[272,256]{1,0:T(8,128)(2,1)S(1)}, bf16[272,256]{1,0:T(8,128)(2,1)S(1)}, u32[]{:S(2)}, u32[]{:S(2)}) collective-permute-start(bf16[272,256]{1,0:T(8,128)(2,1)S(1)} %maximum_maximum_fusion), channel_id=1, source_target_pairs={{0,4},{2,6},{4,0},{6,2},{1,5},{3,7},{5,1},{7,3},{8,12},{10,14},{12... | collective-permute-start | bytes 417800 | tf_op jit(solution)/shard_map/ppermute | solution.py:306
  15.2 2.8 %collective-permute-start.3 = (bf16[272,256]{1,0:T(8,128)(2,1)S(1)}, bf16[272,256]{1,0:T(8,128)(2,1)S(1)}, u32[]{:S(2)}, u32[]{:S(2)}) collective-permute-start(bf16[272,256]{1,0:T(8,128)(2,1)S(1)} %maximum_maximum_fusion), channel_id=1, source_target_pairs={{0,6},{2,0},{4,2},{6,4},{1,7},{3,1},{5,3},{7,5},{8,14},{10,8},{12,... | collective-permute-start | bytes 417800 | tf_op jit(solution)/shard_map/ppermute | solution.py:306
  18.1 4.6 %collective-permute-done.3 = bf16[272,256]{1,0:T(8,128)(2,1)S(1)} collective-permute-done((bf16[272,256]{1,0:T(8,128)(2,1)S(1)}, bf16[272,256]{1,0:T(8,128)(2,1)S(1)}, u32[]{:S(2)}, u32[]{:S(2)}) %collective-permute-start.3) | collective-permute-done | bytes 139296 | tf_op jit(solution)/shard_map/ppermute | solution.py:306
  22.8 1.3 %collective-permute-start.11 = (bf16[512,256]{1,0:T(8,128)(2,1)S(1)}, bf16[512,256]{1,0:T(8,128)(2,1)S(1)}, u32[]{:S(2)}, u32[]{:S(2)}) collective-permute-start(bf16[512,256]{1,0:T(8,128)(2,1)S(1)} %get-tuple-element.66), channel_id=1, source_target_pairs={{0,4},{2,6},{4,0},{6,2},{1,5},{3,7},{5,1},{7,3},{8,12},{10,14},{12... | collective-permute-start | bytes 786440 | tf_op jit(solution)/shard_map/ppermute | solution.py:319
  24.1 2.3 %collective-permute-start.10 = (bf16[512,256]{1,0:T(8,128)(2,1)S(1)}, bf16[512,256]{1,0:T(8,128)(2,1)S(1)}, u32[]{:S(2)}, u32[]{:S(2)}) collective-permute-start(bf16[512,256]{1,0:T(8,128)(2,1)S(1)} %get-tuple-element.67), channel_id=1, source_target_pairs={{0,6},{2,0},{4,2},{6,4},{1,7},{3,1},{5,3},{7,5},{8,14},{10,8},{12,... | collective-permute-start | bytes 786440 | tf_op jit(solution)/shard_map/ppermute | solution.py:319
  27.1 1.3 %collective-permute-start.13 = (bf16[1088,256]{1,0:T(8,128)(2,1)S(1)}, bf16[1088,256]{1,0:T(8,128)(2,1)S(1)}, u32[]{:S(2)}, u32[]{:S(2)}) collective-permute-start(bf16[1088,256]{1,0:T(8,128)(2,1)S(1)} %constant_dynamic-update-slice_fusion.refs_4_), channel_id=1, source_target_pairs={{0,8},{8,16},{16,24},{24,0},{1,9},{9,17},{17,25},{25,1},{2,10},{10... | collective-permute-start | bytes 1671176 | tf_op jit(solution)/shard_map/ppermute | solution.py:321
  28.4 3.4 %collective-permute-done.11.refs_9_ = bf16[512,256]{1,0:T(8,128)(2,1)S(1)} collective-permute-done((bf16[512,256]{1,0:T(8,128)(2,1)S(1)}, bf16[512,256]{1,0:T(8,128)(2,1)S(1)}, u32[]{:S(2)}, u32[]{:S(2)}) %collective-permute-start.11) | collective-permute-done | bytes 262176 | tf_op jit(solution)/shard_map/ppermute | solution.py:319
  31.7 6.7 %collective-permute-done.10.refs_8_ = bf16[512,256]{1,0:T(8,128)(2,1)S(1)} collective-permute-done((bf16[512,256]{1,0:T(8,128)(2,1)S(1)}, bf16[512,256]{1,0:T(8,128)(2,1)S(1)}, u32[]{:S(2)}, u32[]{:S(2)}) %collective-permute-start.10) | collective-permute-done | bytes 262176 | tf_op jit(solution)/shard_map/ppermute | solution.py:319
  38.5 7.8 %shard_map.93 = (bf16[256,768]{1,0:T(8,128)(2,1)S(1)}, bf16[256,768]{1,0:T(8,128)(2,1)S(1)}, bf16[3,256,256]{2,1,0:T(8,128)(2,1)S(1)}, bf16[512,256]{1,0:T(8,128...) custom-call(s32[2]{0:T(128)S(1)} %pad_add_fusion.at_ref, s32[8]{0:T(128)S(1)} %bitcast.47, ...), custom_call_target="tpu_custom_call" | custom-call | flops 21743271936 | bytes 6000000 | tf_op jit(solution)/shard_map/pallas_call | solution.py:172
  46.3 6.9 %collective-permute-start.15 = (bf16[512,256]{1,0:T(8,128)(2,1)S(1)}, bf16[512,256]{1,0:T(8,128)(2,1)S(1)}, u32[]{:S(2)}, u32[]{:S(2)}) collective-permute-start(bf16[512,256]{1,0:T(8,128)(2,1)S(1)} %get-tuple-element.37), channel_id=1, source_target_pairs={{0,6},{2,0},{4,2},{6,4},{1,7},{3,1},{5,3},{7,5},{8,14},{10,8},{12,... | collective-permute-start | bytes 786440 | tf_op jit(solution)/shard_map/ppermute | solution.py:264
  53.2 1.4 %collective-permute-start.17 = (bf16[512,256]{1,0:T(8,128)(2,1)S(1)}, bf16[512,256]{1,0:T(8,128)(2,1)S(1)}, u32[]{:S(2)}, u32[]{:S(2)}) collective-permute-start(bf16[512,256]{1,0:T(8,128)(2,1)S(1)} %get-tuple-element.39), channel_id=1, source_target_pairs={{0,4},{2,6},{4,0},{6,2},{1,5},{3,7},{5,1},{7,3},{8,12},{10,14},{12... | collective-permute-start | bytes 786440 | tf_op jit(solution)/shard_map/ppermute | solution.py:264
  54.6 7.9 %shard_map.94 = (bf16[256,768]{1,0:T(8,128)(2,1)S(1)}, bf16[256,768]{1,0:T(8,128)(2,1)S(1)}, bf16[3,256,256]{2,1,0:T(8,128)(2,1)S(1)}, bf16[512,256]{1,0:T(8,128...) custom-call(s32[2]{0:T(128)S(1)} %pad_add_fusion.at_ref, s32[8]{0:T(128)S(1)} %bitcast.48, ...), custom_call_target="tpu_custom_call" | custom-call | flops 21743271936 | bytes 6000000 | tf_op jit(solution)/shard_map/pallas_call | solution.py:172
  62.6 6.1 %collective-permute-start.23 = (bf16[512,256]{1,0:T(8,128)(2,1)S(1)}, bf16[512,256]{1,0:T(8,128)(2,1)S(1)}, u32[]{:S(2)}, u32[]{:S(2)}) collective-permute-start(bf16[512,256]{1,0:T(8,128)(2,1)S(1)} %get-tuple-element.49), channel_id=1, source_target_pairs={{0,6},{2,0},{4,2},{6,4},{1,7},{3,1},{5,3},{7,5},{8,14},{10,8},{12,... | collective-permute-start | bytes 786440 | tf_op jit(solution)/shard_map/ppermute | solution.py:264
  68.8 1.3 %collective-permute-start.25 = (bf16[512,256]{1,0:T(8,128)(2,1)S(1)}, bf16[512,256]{1,0:T(8,128)(2,1)S(1)}, u32[]{:S(2)}, u32[]{:S(2)}) collective-permute-start(bf16[512,256]{1,0:T(8,128)(2,1)S(1)} %get-tuple-element.51), channel_id=1, source_target_pairs={{0,4},{2,6},{4,0},{6,2},{1,5},{3,7},{5,1},{7,3},{8,12},{10,14},{12... | collective-permute-start | bytes 786440 | tf_op jit(solution)/shard_map/ppermute | solution.py:264
  70.1 3.4 %collective-permute-start.12 = (f32[3,128]{1,0:T(4,128)S(1)}, f32[3,128]{1,0:T(4,128)S(1)}, u32[]{:S(2)}, u32[]{:S(2)}) collective-permute-start(f32[3,128]{1,0:T(4,128)S(1)} %convert_add_fusion.6), channel_id=1, source_target_pairs={{0,24},{8,0},{16,8},{24,16},{1,25},{9,1},{17,9},{25,17},{2,26},{10... | collective-permute-start | bytes 4616 | tf_op jit(solution)/shard_map/ppermute | solution.py:337
  74.0 5.2 %collective-permute-done.23 = bf16[512,256]{1,0:T(8,128)(2,1)S(1)} collective-permute-done((bf16[512,256]{1,0:T(8,128)(2,1)S(1)}, bf16[512,256]{1,0:T(8,128)(2,1)S(1)}, u32[]{:S(2)}, u32[]{:S(2)}) %collective-permute-start.23) | collective-permute-done | bytes 262176 | tf_op jit(solution)/shard_map/ppermute | solution.py:264
  79.2 3.2 %collective-permute-start.19 = (bf16[256,256]{1,0:T(8,128)(2,1)S(1)}, bf16[256,256]{1,0:T(8,128)(2,1)S(1)}, u32[]{:S(2)}, u32[]{:S(2)}) collective-permute-start(bf16[256,256]{1,0:T(8,128)(2,1)S(1)} %get-tuple-element.61), channel_id=1, source_target_pairs={{0,16},{8,24},{16,0},{24,8},{1,17},{9,25},{17,1},{25,9},{2,18},{10... | collective-permute-start | bytes 393224 | tf_op jit(solution)/shard_map/ppermute | solution.py:281
  82.7 2.2 %collective-permute-start.26 = (bf16[128,3072]{1,0:T(8,128)(2,1)S(1)}, bf16[128,3072]{1,0:T(8,128)(2,1)S(1)}, u32[]{:S(2)}, u32[]{:S(2)}) collective-permute-start(bf16[128,3072]{1,0:T(8,128)(2,1)S(1)} %pad_maximum_fusion), channel_id=1, source_target_pairs={{0,1},{1,0},{2,3},{3,2},{4,5},{5,4},{6,7},{7,6},{8,9},{9,8},{10,11... | collective-permute-start | bytes 2359304 | tf_op jit(solution)/shard_map/ppermute | solution.py:344
  84.9 9.0 %collective-permute-start.27 = (bf16[256,256]{1,0:T(8,128)(2,1)S(1)}, bf16[256,256]{1,0:T(8,128)(2,1)S(1)}, u32[]{:S(2)}, u32[]{:S(2)}) collective-permute-start(bf16[256,256]{1,0:T(8,128)(2,1)S(1)} %get-tuple-element.59), channel_id=1, source_target_pairs={{0,24},{8,0},{16,8},{24,16},{1,25},{9,1},{17,9},{25,17},{2,26},{10... | collective-permute-start | bytes 393224 | tf_op jit(solution)/shard_map/ppermute | solution.py:280
  93.9 2.5 %collective-permute-start.28 = (bf16[256,256]{1,0:T(8,128)(2,1)S(1)}, bf16[256,256]{1,0:T(8,128)(2,1)S(1)}, u32[]{:S(2)}, u32[]{:S(2)}) collective-permute-start(bf16[256,256]{1,0:T(8,128)(2,1)S(1)} %get-tuple-element.58), channel_id=1, source_target_pairs={{0,16},{8,24},{16,0},{24,8},{1,17},{9,25},{17,1},{25,9},{2,18},{10... | collective-permute-start | bytes 393224 | tf_op jit(solution)/shard_map/ppermute | solution.py:281
  96.5 6.9 %collective-permute-start.22 = (f32[3,128]{1,0:T(4,128)S(1)}, f32[3,128]{1,0:T(4,128)S(1)}, u32[]{:S(2)}, u32[]{:S(2)}) collective-permute-start(f32[3,128]{1,0:T(4,128)S(1)} %add_add_fusion), channel_id=1, source_target_pairs={{0,96},{32,0},{64,32},{96,64},{1,97},{33,1},{65,33},{97,65},{2,98}... | collective-permute-start | bytes 4616 | tf_op jit(solution)/shard_map/ppermute | solution.py:339
  104.2 3.2 %collective-permute-done.21 = f32[3,128]{1,0:T(4,128)S(1)} collective-permute-done((f32[3,128]{1,0:T(4,128)S(1)}, f32[3,128]{1,0:T(4,128)S(1)}, u32[]{:S(2)}, u32[]{:S(2)}) %collective-permute-start.21) | collective-permute-done | bytes 1568 | tf_op jit(solution)/shard_map/ppermute | solution.py:339
  107.4 1.0 collective-permute-done.20
  108.5 1.3 %shard_map.95 = (bf16[128,3072]{1,0:T(8,128)(2,1)}, bf16[128,3072]{1,0:T(8,128)(2,1)}) custom-call(s32[1]{0:T(128)} %bitcast.core_ref, f32[12,128]{1,0:T(8,128)S(1)} %pad_maximum_fusion.5.total_ref, bf16[256,768]{1,0:T(8,128)(2,1)S(1)} %get-tuple-element.34.att0, bf16[256,768]{1,0:T(8,128)(2,1)S(1)} %get-tuple-element.46.att1, ...), custom_call_target="tpu_custom_call" | custom-call | tf_op jit(solution)/shard_map/pallas_call | solution.py:230
  109.9 2.0 %collective-permute-start.29 = (bf16[128,512]{1,0:T(8,128)(2,1)S(1)}, bf16[128,512]{1,0:T(8,128)(2,1)S(1)}, u32[]{:S(2)}, u32[]{:S(2)}) collective-permute-start(bf16[128,512]{1,0:T(8,128)(2,1)S(1)} %fusion.22), channel_id=1, source_target_pairs={{0,1},{1,0},{2,3},{3,2},{4,5},{5,4},{6,7},{7,6},{8,9},{9,8},{10,11... | collective-permute-start | bytes 393224 | tf_op jit(solution)/shard_map/ppermute | solution.py:349
  111.9 1.0 collective-permute-done.29.got
  (85 shorter events, 5.9 us)
Async XLA Ops:
  0.6 3.3 %copy-start.3 = (f32[1,128]{1,0:T(1,128)S(1)}, f32[1,128]{1,0:T(1,128)}, u32[]{:S(2)}) copy-start(f32[1,128]{1,0:T(1,128)} %param.10) | copy-start | bytes 1540
  1.4 4.1 %collective-permute-start = (f32[8,128]{1,0:T(8,128)S(1)}, f32[8,128]{1,0:T(8,128)S(1)}, u32[]{:S(2)}, u32[]{:S(2)}) collective-permute-start(f32[8,128]{1,0:T(8,128)S(1)} %broadcast_in_dim.67), channel_id=1, source_target_pairs={{0,1},{1,0},{2,3},{3,2},{4,5},{5,4},{6,7},{7,6},{8,9},{9,8},{10,11... | collective-permute-start | bytes 12296 | tf_op jit(solution)/shard_map/ppermute | solution.py:299
  3.8 1.8 %collective-permute-start.1 = (bf16[128,512]{1,0:T(8,128)(2,1)S(1)}, bf16[128,512]{1,0:T(8,128)(2,1)S(1)}, u32[]{:S(2)}, u32[]{:S(2)}) collective-permute-start(bf16[128,512]{1,0:T(8,128)(2,1)S(1)} %pad_maximum_fusion.4), channel_id=1, source_target_pairs={{0,1},{1,0},{2,3},{3,2},{4,5},{5,4},{6,7},{7,6},{8,9},{9,8},{10,11... | collective-permute-start | bytes 393224 | tf_op jit(solution)/shard_map/ppermute | solution.py:300
  5.7 6.2 %collective-permute-start.8 = (bf16[256,256]{1,0:T(8,128)(2,1)S(1)}, bf16[256,256]{1,0:T(8,128)(2,1)S(1)}, u32[]{:S(2)}, u32[]{:S(2)}) collective-permute-start(bf16[256,256]{1,0:T(8,128)(2,1)S(1)} %get-tuple-element.70.refs_4_), channel_id=1, source_target_pairs={{0,16},{8,24},{16,0},{24,8},{1,17},{9,25},{17,1},{25,9},{2,18},{10... | collective-permute-start | bytes 393224 | tf_op jit(solution)/shard_map/ppermute | solution.py:305
  8.6 6.7 %collective-permute-start.7 = (bf16[256,256]{1,0:T(8,128)(2,1)S(1)}, bf16[256,256]{1,0:T(8,128)(2,1)S(1)}, u32[]{:S(2)}, u32[]{:S(2)}) collective-permute-start(bf16[256,256]{1,0:T(8,128)(2,1)S(1)} %get-tuple-element.70.refs_4_), channel_id=1, source_target_pairs={{0,8},{8,16},{16,24},{24,0},{1,9},{9,17},{17,25},{25,1},{2,10},{10... | collective-permute-start | bytes 393224 | tf_op jit(solution)/shard_map/ppermute | solution.py:304
  8.9 9.2 %collective-permute-start.2 = (bf16[272,256]{1,0:T(8,128)(2,1)S(1)}, bf16[272,256]{1,0:T(8,128)(2,1)S(1)}, u32[]{:S(2)}, u32[]{:S(2)}) collective-permute-start(bf16[272,256]{1,0:T(8,128)(2,1)S(1)} %maximum_maximum_fusion), channel_id=1, source_target_pairs={{0,2},{2,4},{4,6},{6,0},{1,3},{3,5},{5,7},{7,1},{8,10},{10,12},{12... | collective-permute-start | bytes 417800 | tf_op jit(solution)/shard_map/ppermute | solution.py:306
  10.3 12.5 %collective-permute-start.5 = (bf16[128,1536]{1,0:T(8,128)(2,1)S(1)}, bf16[128,1536]{1,0:T(8,128)(2,1)S(1)}, u32[]{:S(2)}, u32[]{:S(2)}) collective-permute-start(bf16[128,1536]{1,0:T(8,128)(2,1)S(1)} %get-tuple-element.31), channel_id=1, source_target_pairs={{0,1},{1,0},{2,3},{3,2},{4,5},{5,4},{6,7},{7,6},{8,9},{9,8},{10,11... | collective-permute-start | bytes 1179656 | tf_op jit(solution)/shard_map/ppermute | solution.py:311
  11.6 11.2 %collective-permute-start.6 = (bf16[128,1536]{1,0:T(8,128)(2,1)S(1)}, bf16[128,1536]{1,0:T(8,128)(2,1)S(1)}, u32[]{:S(2)}, u32[]{:S(2)}) collective-permute-start(bf16[128,1536]{1,0:T(8,128)(2,1)S(1)} %get-tuple-element.32), channel_id=1, source_target_pairs={{0,1},{1,0},{2,3},{3,2},{4,5},{5,4},{6,7},{7,6},{8,9},{9,8},{10,11... | collective-permute-start | bytes 1179656 | tf_op jit(solution)/shard_map/ppermute | solution.py:312
  11.8 15.1 %collective-permute-start.4 = (bf16[272,256]{1,0:T(8,128)(2,1)S(1)}, bf16[272,256]{1,0:T(8,128)(2,1)S(1)}, u32[]{:S(2)}, u32[]{:S(2)}) collective-permute-start(bf16[272,256]{1,0:T(8,128)(2,1)S(1)} %maximum_maximum_fusion), channel_id=1, source_target_pairs={{0,4},{2,6},{4,0},{6,2},{1,5},{3,7},{5,1},{7,3},{8,12},{10,14},{12... | collective-permute-start | bytes 417800 | tf_op jit(solution)/shard_map/ppermute | solution.py:306
  15.2 7.5 %collective-permute-start.3 = (bf16[272,256]{1,0:T(8,128)(2,1)S(1)}, bf16[272,256]{1,0:T(8,128)(2,1)S(1)}, u32[]{:S(2)}, u32[]{:S(2)}) collective-permute-start(bf16[272,256]{1,0:T(8,128)(2,1)S(1)} %maximum_maximum_fusion), channel_id=1, source_target_pairs={{0,6},{2,0},{4,2},{6,4},{1,7},{3,1},{5,3},{7,5},{8,14},{10,8},{12,... | collective-permute-start | bytes 417800 | tf_op jit(solution)/shard_map/ppermute | solution.py:306
  22.7 15.7 %copy-start = (s32[1,8]{1,0:T(1,128)S(1)}, s32[1,8]{1,0:T(1,128)}, u32[]{:S(2)}) copy-start(s32[1,8]{1,0:T(1,128)} %param.11) | copy-start | bytes 100
  22.8 8.9 %collective-permute-start.11 = (bf16[512,256]{1,0:T(8,128)(2,1)S(1)}, bf16[512,256]{1,0:T(8,128)(2,1)S(1)}, u32[]{:S(2)}, u32[]{:S(2)}) collective-permute-start(bf16[512,256]{1,0:T(8,128)(2,1)S(1)} %get-tuple-element.66), channel_id=1, source_target_pairs={{0,4},{2,6},{4,0},{6,2},{1,5},{3,7},{5,1},{7,3},{8,12},{10,14},{12... | collective-permute-start | bytes 786440 | tf_op jit(solution)/shard_map/ppermute | solution.py:319
  24.1 14.3 %collective-permute-start.10 = (bf16[512,256]{1,0:T(8,128)(2,1)S(1)}, bf16[512,256]{1,0:T(8,128)(2,1)S(1)}, u32[]{:S(2)}, u32[]{:S(2)}) collective-permute-start(bf16[512,256]{1,0:T(8,128)(2,1)S(1)} %get-tuple-element.67), channel_id=1, source_target_pairs={{0,6},{2,0},{4,2},{6,4},{1,7},{3,1},{5,3},{7,5},{8,14},{10,8},{12,... | collective-permute-start | bytes 786440 | tf_op jit(solution)/shard_map/ppermute | solution.py:319
  26.4 12.1 %collective-permute-start.9 = (bf16[512,256]{1,0:T(8,128)(2,1)S(1)}, bf16[512,256]{1,0:T(8,128)(2,1)S(1)}, u32[]{:S(2)}, u32[]{:S(2)}) collective-permute-start(bf16[512,256]{1,0:T(8,128)(2,1)S(1)} %get-tuple-element.68), channel_id=1, source_target_pairs={{0,2},{2,4},{4,6},{6,0},{1,3},{3,5},{5,7},{7,1},{8,10},{10,12},{12... | collective-permute-start | bytes 786440 | tf_op jit(solution)/shard_map/ppermute | solution.py:319
  26.9 27.7 %collective-permute-start.14 = (bf16[1088,256]{1,0:T(8,128)(2,1)S(1)}, bf16[1088,256]{1,0:T(8,128)(2,1)S(1)}, u32[]{:S(2)}, u32[]{:S(2)}) collective-permute-start(bf16[1088,256]{1,0:T(8,128)(2,1)S(1)} %constant_dynamic-update-slice_fusion.refs_4_), channel_id=1, source_target_pairs={{0,16},{8,24},{16,0},{24,8},{1,17},{9,25},{17,1},{25,9},{2,18},{10... | collective-permute-start | bytes 1671176 | tf_op jit(solution)/shard_map/ppermute | solution.py:321
  27.1 27.6 %collective-permute-start.13 = (bf16[1088,256]{1,0:T(8,128)(2,1)S(1)}, bf16[1088,256]{1,0:T(8,128)(2,1)S(1)}, u32[]{:S(2)}, u32[]{:S(2)}) collective-permute-start(bf16[1088,256]{1,0:T(8,128)(2,1)S(1)} %constant_dynamic-update-slice_fusion.refs_4_), channel_id=1, source_target_pairs={{0,8},{8,16},{16,24},{24,0},{1,9},{9,17},{17,25},{25,1},{2,10},{10... | collective-permute-start | bytes 1671176 | tf_op jit(solution)/shard_map/ppermute | solution.py:321
  46.3 22.4 %collective-permute-start.15 = (bf16[512,256]{1,0:T(8,128)(2,1)S(1)}, bf16[512,256]{1,0:T(8,128)(2,1)S(1)}, u32[]{:S(2)}, u32[]{:S(2)}) collective-permute-start(bf16[512,256]{1,0:T(8,128)(2,1)S(1)} %get-tuple-element.37), channel_id=1, source_target_pairs={{0,6},{2,0},{4,2},{6,4},{1,7},{3,1},{5,3},{7,5},{8,14},{10,8},{12,... | collective-permute-start | bytes 786440 | tf_op jit(solution)/shard_map/ppermute | solution.py:264
  53.2 16.9 %collective-permute-start.16 = (bf16[512,256]{1,0:T(8,128)(2,1)S(1)}, bf16[512,256]{1,0:T(8,128)(2,1)S(1)}, u32[]{:S(2)}, u32[]{:S(2)}) collective-permute-start(bf16[512,256]{1,0:T(8,128)(2,1)S(1)} %get-tuple-element.38), channel_id=1, source_target_pairs={{0,2},{2,4},{4,6},{6,0},{1,3},{3,5},{5,7},{7,1},{8,10},{10,12},{12... | collective-permute-start | bytes 786440 | tf_op jit(solution)/shard_map/ppermute | solution.py:264
  53.2 20.3 %collective-permute-start.17 = (bf16[512,256]{1,0:T(8,128)(2,1)S(1)}, bf16[512,256]{1,0:T(8,128)(2,1)S(1)}, u32[]{:S(2)}, u32[]{:S(2)}) collective-permute-start(bf16[512,256]{1,0:T(8,128)(2,1)S(1)} %get-tuple-element.39), channel_id=1, source_target_pairs={{0,4},{2,6},{4,0},{6,2},{1,5},{3,7},{5,1},{7,3},{8,12},{10,14},{12... | collective-permute-start | bytes 786440 | tf_op jit(solution)/shard_map/ppermute | solution.py:264
  62.6 16.6 %collective-permute-start.23 = (bf16[512,256]{1,0:T(8,128)(2,1)S(1)}, bf16[512,256]{1,0:T(8,128)(2,1)S(1)}, u32[]{:S(2)}, u32[]{:S(2)}) collective-permute-start(bf16[512,256]{1,0:T(8,128)(2,1)S(1)} %get-tuple-element.49), channel_id=1, source_target_pairs={{0,6},{2,0},{4,2},{6,4},{1,7},{3,1},{5,3},{7,5},{8,14},{10,8},{12,... | collective-permute-start | bytes 786440 | tf_op jit(solution)/shard_map/ppermute | solution.py:264
  68.8 13.7 %collective-permute-start.24 = (bf16[512,256]{1,0:T(8,128)(2,1)S(1)}, bf16[512,256]{1,0:T(8,128)(2,1)S(1)}, u32[]{:S(2)}, u32[]{:S(2)}) collective-permute-start(bf16[512,256]{1,0:T(8,128)(2,1)S(1)} %get-tuple-element.50), channel_id=1, source_target_pairs={{0,2},{2,4},{4,6},{6,0},{1,3},{3,5},{5,7},{7,1},{8,10},{10,12},{12... | collective-permute-start | bytes 786440 | tf_op jit(solution)/shard_map/ppermute | solution.py:264
  68.8 13.7 %collective-permute-start.25 = (bf16[512,256]{1,0:T(8,128)(2,1)S(1)}, bf16[512,256]{1,0:T(8,128)(2,1)S(1)}, u32[]{:S(2)}, u32[]{:S(2)}) collective-permute-start(bf16[512,256]{1,0:T(8,128)(2,1)S(1)} %get-tuple-element.51), channel_id=1, source_target_pairs={{0,4},{2,6},{4,0},{6,2},{1,5},{3,7},{5,1},{7,3},{8,12},{10,14},{12... | collective-permute-start | bytes 786440 | tf_op jit(solution)/shard_map/ppermute | solution.py:264
  70.1 14.8 %collective-permute-start.12 = (f32[3,128]{1,0:T(4,128)S(1)}, f32[3,128]{1,0:T(4,128)S(1)}, u32[]{:S(2)}, u32[]{:S(2)}) collective-permute-start(f32[3,128]{1,0:T(4,128)S(1)} %convert_add_fusion.6), channel_id=1, source_target_pairs={{0,24},{8,0},{16,8},{24,16},{1,25},{9,1},{17,9},{25,17},{2,26},{10... | collective-permute-start | bytes 4616 | tf_op jit(solution)/shard_map/ppermute | solution.py:337
  73.9 22.5 %collective-permute-start.18 = (bf16[256,256]{1,0:T(8,128)(2,1)S(1)}, bf16[256,256]{1,0:T(8,128)(2,1)S(1)}, u32[]{:S(2)}, u32[]{:S(2)}) collective-permute-start(bf16[256,256]{1,0:T(8,128)(2,1)S(1)} %get-tuple-element.60), channel_id=1, source_target_pairs={{0,24},{8,0},{16,8},{24,16},{1,25},{9,1},{17,9},{25,17},{2,26},{10... | collective-permute-start | bytes 393224 | tf_op jit(solution)/shard_map/ppermute | solution.py:280
  79.2 17.2 %collective-permute-start.19 = (bf16[256,256]{1,0:T(8,128)(2,1)S(1)}, bf16[256,256]{1,0:T(8,128)(2,1)S(1)}, u32[]{:S(2)}, u32[]{:S(2)}) collective-permute-start(bf16[256,256]{1,0:T(8,128)(2,1)S(1)} %get-tuple-element.61), channel_id=1, source_target_pairs={{0,16},{8,24},{16,0},{24,8},{1,17},{9,25},{17,1},{25,9},{2,18},{10... | collective-permute-start | bytes 393224 | tf_op jit(solution)/shard_map/ppermute | solution.py:281
  82.7 25.8 %collective-permute-start.26 = (bf16[128,3072]{1,0:T(8,128)(2,1)S(1)}, bf16[128,3072]{1,0:T(8,128)(2,1)S(1)}, u32[]{:S(2)}, u32[]{:S(2)}) collective-permute-start(bf16[128,3072]{1,0:T(8,128)(2,1)S(1)} %pad_maximum_fusion), channel_id=1, source_target_pairs={{0,1},{1,0},{2,3},{3,2},{4,5},{5,4},{6,7},{7,6},{8,9},{9,8},{10,11... | collective-permute-start | bytes 2359304 | tf_op jit(solution)/shard_map/ppermute | solution.py:344
  84.9 23.4 %collective-permute-start.27 = (bf16[256,256]{1,0:T(8,128)(2,1)S(1)}, bf16[256,256]{1,0:T(8,128)(2,1)S(1)}, u32[]{:S(2)}, u32[]{:S(2)}) collective-permute-start(bf16[256,256]{1,0:T(8,128)(2,1)S(1)} %get-tuple-element.59), channel_id=1, source_target_pairs={{0,24},{8,0},{16,8},{24,16},{1,25},{9,1},{17,9},{25,17},{2,26},{10... | collective-permute-start | bytes 393224 | tf_op jit(solution)/shard_map/ppermute | solution.py:280
  93.9 14.4 %collective-permute-start.28 = (bf16[256,256]{1,0:T(8,128)(2,1)S(1)}, bf16[256,256]{1,0:T(8,128)(2,1)S(1)}, u32[]{:S(2)}, u32[]{:S(2)}) collective-permute-start(bf16[256,256]{1,0:T(8,128)(2,1)S(1)} %get-tuple-element.58), channel_id=1, source_target_pairs={{0,16},{8,24},{16,0},{24,8},{1,17},{9,25},{17,1},{25,9},{2,18},{10... | collective-permute-start | bytes 393224 | tf_op jit(solution)/shard_map/ppermute | solution.py:281
  96.5 7.6 %collective-permute-start.22 = (f32[3,128]{1,0:T(4,128)S(1)}, f32[3,128]{1,0:T(4,128)S(1)}, u32[]{:S(2)}, u32[]{:S(2)}) collective-permute-start(f32[3,128]{1,0:T(4,128)S(1)} %add_add_fusion), channel_id=1, source_target_pairs={{0,96},{32,0},{64,32},{96,64},{1,97},{33,1},{65,33},{97,65},{2,98}... | collective-permute-start | bytes 4616 | tf_op jit(solution)/shard_map/ppermute | solution.py:339
  103.4 3.9 %collective-permute-start.21 = (f32[3,128]{1,0:T(4,128)S(1)}, f32[3,128]{1,0:T(4,128)S(1)}, u32[]{:S(2)}, u32[]{:S(2)}) collective-permute-start(f32[3,128]{1,0:T(4,128)S(1)} %add_add_fusion), channel_id=1, source_target_pairs={{0,64},{32,96},{64,0},{96,32},{1,65},{33,97},{65,1},{97,33},{2,66}... | collective-permute-start | bytes 4616 | tf_op jit(solution)/shard_map/ppermute | solution.py:339
  104.2 4.2 %collective-permute-start.20 = (f32[3,128]{1,0:T(4,128)S(1)}, f32[3,128]{1,0:T(4,128)S(1)}, u32[]{:S(2)}, u32[]{:S(2)}) collective-permute-start(f32[3,128]{1,0:T(4,128)S(1)} %add_add_fusion), channel_id=1, source_target_pairs={{0,32},{32,64},{64,96},{96,0},{1,33},{33,65},{65,97},{97,1},{2,34}... | collective-permute-start | bytes 4616 | tf_op jit(solution)/shard_map/ppermute | solution.py:339
  109.9 3.0 %collective-permute-start.29 = (bf16[128,512]{1,0:T(8,128)(2,1)S(1)}, bf16[128,512]{1,0:T(8,128)(2,1)S(1)}, u32[]{:S(2)}, u32[]{:S(2)}) collective-permute-start(bf16[128,512]{1,0:T(8,128)(2,1)S(1)} %fusion.22), channel_id=1, source_target_pairs={{0,1},{1,0},{2,3},{3,2},{4,5},{5,4},{6,7},{7,6},{8,9},{9,8},{10,11... | collective-permute-start | bytes 393224 | tf_op jit(solution)/shard_map/ppermute | solution.py:349
  (2 other events, 4.5 us)

commit v6 on v5

--- a/solution.py
+++ b/solution.py
@@ -334,7 +334,7 @@
     grad1 = scatter_x(sums1)
 
     total = noted(near)
-    total = total + lax.ppermute(after(total, att0), "x", ring(3))
+    total = total + lax.ppermute(after(total, sums0[1]), "x", ring(3))
     total = after(total + noted(second_pieces[1]) + noted(second_pieces[2]), grad0)
     pieces = [total] + [lax.ppermute(total, "dp", ring(k)) for k in (1, 2, 3)]
     total = jnp.concatenate(pieces, axis=0)
@@ -343,10 +343,10 @@
     others = jnp.concatenate([part[HALF:] for part in parts], axis=1)
     others = lax.ppermute(after(others, sums1[1]), "core", SWAP)
 
-    own_grad = jnp.concatenate([grad0, grad1], axis=1).astype(BF)
+    own_grad = jnp.concatenate([grad0, after(grad1, total)], axis=1).astype(BF)
 
     out_rows, dq_rows = finish(finish_rows, core, total, *parts, others, outs=2, width=QH * HD)
-    got = lax.ppermute(after(own_grad[HALF:], out_rows), "core", SWAP)
+    got = after(lax.ppermute(own_grad[HALF:], "core", SWAP), out_rows)
     key_grad, value_grad = finish(finish_keys, core, total, own_grad, got, outs=2, width=KVH * HD)
     return (out_rows[None], dq_rows[None], key_grad[None], value_grad[None])
 

time: 114 us -> 111 us (0.974); the launches traced: 114 us -> 113 us
  waiting for transfers between devices: 26.5 us -> 22 us
  starting transfers between devices: 63.8 us -> 67.3 us
    ppermute x2, starting transfers between devices: 5.44 us -> 13.6 us  [the longest x1 11.8 us: body(): total = total + lax.ppermute(after(total, sums0[1]), 'x', ring(3))]
    ppermute x6, waiting for transfers between devices: 5.23 us -> 0.02 us  [send_y(): lax.ppermute(pair, 'y', ring(4 - k))]
    ppermute x2, starting transfers between devices: 5.67 us -> 1.72 us  [scatter_x(): t2 = lax.ppermute(sums[2], 'x', ring(2))]
    ppermute x6, starting transfers between devices: 15.7 us -> 13.3 us  [send_y(): lax.ppermute(pair, 'y', ring(4 - k))]
    ppermute x1, starting transfers between devices: 2.24 us -> 3.67 us  [body(): others = lax.ppermute(after(others, sums1[1]), 'core', SWAP)]
    ppermute x3, starting transfers between devices: 6.89 us -> 8.07 us  [body(): pieces = [total] + [lax.ppermute(total, 'dp', ring(k)) for k in (1, 2, 3)]]
    ppermute x1, waiting for transfers between devices: 0.01 us -> 1.16 us  [body(): lax.ppermute(near, 'x', ring(1))]
  transfers between devices with their start and end apart: 30 -> 30, of which waited for: 10 -> 10; matrix products, arithmetic and copies ran while one was open for 2% -> 2% of each run, Pallas kernels for 14% -> 15%
where the time goes in v6:
time: 111 us; the launch traced here: 113 us
  starting transfers between devices  67.3 us (61%)
  waiting for transfers between devices  22 us (20%)
  Pallas kernels  17.9 us (16%)
  local copies, waits for them, and re-layouts  3.08 us (3%)
  other arithmetic  1.39 us (1%)
    pallas_call x2, Pallas kernels, attention(): pl.pallas_call(functools.partial(attention_kernel, head, places_of, len(p...  15.7 us
    ppermute x6, starting transfers between devices, send_y(): lax.ppermute(pair, 'y', ring(4 - k))  13.3 us
    ppermute x1, starting transfers between devices, body(): total = total + lax.ppermute(after(total, sums0[1]), 'x', ring(3))  11.8 us
    ppermute x3, waiting for transfers between devices, body(): first_pieces.append(lax.ppermute(pair, 'y', ring(k)))  10.1 us
    ppermute x2, starting transfers between devices, scatter_x(): t1 = lax.ppermute(sums[1], 'x', ring(3))  8.16 us
    ppermute x3, starting transfers between devices, body(): pieces = [total] + [lax.ppermute(total, 'dp', ring(k)) for k in (1, 2, 3)]  8.07 us
    ppermute x3, starting transfers between devices, body(): nearest = [lax.ppermute(second, 'y', ring(k)) for k in (1, 3, 2)]  7.16 us
    ppermute x3, waiting for transfers between devices, body(): pieces = [total] + [lax.ppermute(total, 'dp', ring(k)) for k in (1, 2, 3)]  4.91 us
  transfers between devices with their start and end apart: 30, of which 10 were waited for; matrix products, arithmetic and copies ran while one was open for 2% of the time, Pallas kernels for 15%

profile of v6, /device:TPU:1, one launch (start us, length us, event | category | flops | bytes accessed | tf_op | source)
XLA Modules:
  0.0 112.8 jit_solution(12667359172585116368)
XLA Ops:
  1.4 1.4 %collective-permute-start = (f32[8,128]{1,0:T(8,128)S(1)}, f32[8,128]{1,0:T(8,128)S(1)}, u32[]{:S(2)}, u32[]{:S(2)}) collective-permute-start(f32[8,128]{1,0:T(8,128)S(1)} %broadcast_in_dim.67), channel_id=1, source_target_pairs={{0,1},{1,0},{2,3},{3,2},{4,5},{5,4},{6,7},{7,6},{8,9},{9,8},{10,11... | collective-permute-start | bytes 12296 | tf_op jit(solution)/shard_map/ppermute | solution.py:299
  2.8 1.0 dynamic-slice_bitcast_fusion.4
  4.3 1.1 copy-done.2
  5.7 2.9 %collective-permute-start.8 = (bf16[256,256]{1,0:T(8,128)(2,1)S(1)}, bf16[256,256]{1,0:T(8,128)(2,1)S(1)}, u32[]{:S(2)}, u32[]{:S(2)}) collective-permute-start(bf16[256,256]{1,0:T(8,128)(2,1)S(1)} %get-tuple-element.72.refs_4_), channel_id=1, source_target_pairs={{0,16},{8,24},{16,0},{24,8},{1,17},{9,25},{17,1},{25,9},{2,18},{10... | collective-permute-start | bytes 393224 | tf_op jit(solution)/shard_map/ppermute | solution.py:305
  8.9 1.4 %collective-permute-start.2 = (bf16[272,256]{1,0:T(8,128)(2,1)S(1)}, bf16[272,256]{1,0:T(8,128)(2,1)S(1)}, u32[]{:S(2)}, u32[]{:S(2)}) collective-permute-start(bf16[272,256]{1,0:T(8,128)(2,1)S(1)} %maximum_maximum_fusion), channel_id=1, source_target_pairs={{0,2},{2,4},{4,6},{6,0},{1,3},{3,5},{5,7},{7,1},{8,10},{10,12},{12... | collective-permute-start | bytes 417800 | tf_op jit(solution)/shard_map/ppermute | solution.py:306
  10.3 1.3 %collective-permute-start.5 = (bf16[128,1536]{1,0:T(8,128)(2,1)S(1)}, bf16[128,1536]{1,0:T(8,128)(2,1)S(1)}, u32[]{:S(2)}, u32[]{:S(2)}) collective-permute-start(bf16[128,1536]{1,0:T(8,128)(2,1)S(1)} %get-tuple-element.32), channel_id=1, source_target_pairs={{0,1},{1,0},{2,3},{3,2},{4,5},{5,4},{6,7},{7,6},{8,9},{9,8},{10,11... | collective-permute-start | bytes 1179656 | tf_op jit(solution)/shard_map/ppermute | solution.py:311
  11.8 3.0 %collective-permute-start.4 = (bf16[272,256]{1,0:T(8,128)(2,1)S(1)}, bf16[272,256]{1,0:T(8,128)(2,1)S(1)}, u32[]{:S(2)}, u32[]{:S(2)}) collective-permute-start(bf16[272,256]{1,0:T(8,128)(2,1)S(1)} %maximum_maximum_fusion), channel_id=1, source_target_pairs={{0,4},{2,6},{4,0},{6,2},{1,5},{3,7},{5,1},{7,3},{8,12},{10,14},{12... | collective-permute-start | bytes 417800 | tf_op jit(solution)/shard_map/ppermute | solution.py:306
  15.2 2.8 %collective-permute-start.3 = (bf16[272,256]{1,0:T(8,128)(2,1)S(1)}, bf16[272,256]{1,0:T(8,128)(2,1)S(1)}, u32[]{:S(2)}, u32[]{:S(2)}) collective-permute-start(bf16[272,256]{1,0:T(8,128)(2,1)S(1)} %maximum_maximum_fusion), channel_id=1, source_target_pairs={{0,6},{2,0},{4,2},{6,4},{1,7},{3,1},{5,3},{7,5},{8,14},{10,8},{12,... | collective-permute-start | bytes 417800 | tf_op jit(solution)/shard_map/ppermute | solution.py:306
  18.1 4.6 %collective-permute-done.3 = bf16[272,256]{1,0:T(8,128)(2,1)S(1)} collective-permute-done((bf16[272,256]{1,0:T(8,128)(2,1)S(1)}, bf16[272,256]{1,0:T(8,128)(2,1)S(1)}, u32[]{:S(2)}, u32[]{:S(2)}) %collective-permute-start.3) | collective-permute-done | bytes 139296 | tf_op jit(solution)/shard_map/ppermute | solution.py:306
  22.8 1.3 %collective-permute-start.11 = (bf16[512,256]{1,0:T(8,128)(2,1)S(1)}, bf16[512,256]{1,0:T(8,128)(2,1)S(1)}, u32[]{:S(2)}, u32[]{:S(2)}) collective-permute-start(bf16[512,256]{1,0:T(8,128)(2,1)S(1)} %get-tuple-element.68), channel_id=1, source_target_pairs={{0,4},{2,6},{4,0},{6,2},{1,5},{3,7},{5,1},{7,3},{8,12},{10,14},{12... | collective-permute-start | bytes 786440 | tf_op jit(solution)/shard_map/ppermute | solution.py:319
  24.1 2.3 %collective-permute-start.10 = (bf16[512,256]{1,0:T(8,128)(2,1)S(1)}, bf16[512,256]{1,0:T(8,128)(2,1)S(1)}, u32[]{:S(2)}, u32[]{:S(2)}) collective-permute-start(bf16[512,256]{1,0:T(8,128)(2,1)S(1)} %get-tuple-element.69), channel_id=1, source_target_pairs={{0,6},{2,0},{4,2},{6,4},{1,7},{3,1},{5,3},{7,5},{8,14},{10,8},{12,... | collective-permute-start | bytes 786440 | tf_op jit(solution)/shard_map/ppermute | solution.py:319
  27.1 1.3 %collective-permute-start.15 = (bf16[1088,256]{1,0:T(8,128)(2,1)S(1)}, bf16[1088,256]{1,0:T(8,128)(2,1)S(1)}, u32[]{:S(2)}, u32[]{:S(2)}) collective-permute-start(bf16[1088,256]{1,0:T(8,128)(2,1)S(1)} %constant_dynamic-update-slice_fusion.refs_4_), channel_id=1, source_target_pairs={{0,8},{8,16},{16,24},{24,0},{1,9},{9,17},{17,25},{25,1},{2,10},{10... | collective-permute-start | bytes 1671176 | tf_op jit(solution)/shard_map/ppermute | solution.py:321
  28.4 3.4 %collective-permute-done.11.refs_9_ = bf16[512,256]{1,0:T(8,128)(2,1)S(1)} collective-permute-done((bf16[512,256]{1,0:T(8,128)(2,1)S(1)}, bf16[512,256]{1,0:T(8,128)(2,1)S(1)}, u32[]{:S(2)}, u32[]{:S(2)}) %collective-permute-start.11) | collective-permute-done | bytes 262176 | tf_op jit(solution)/shard_map/ppermute | solution.py:319
  31.7 6.7 %collective-permute-done.10.refs_8_ = bf16[512,256]{1,0:T(8,128)(2,1)S(1)} collective-permute-done((bf16[512,256]{1,0:T(8,128)(2,1)S(1)}, bf16[512,256]{1,0:T(8,128)(2,1)S(1)}, u32[]{:S(2)}, u32[]{:S(2)}) %collective-permute-start.10) | collective-permute-done | bytes 262176 | tf_op jit(solution)/shard_map/ppermute | solution.py:319
  38.5 7.8 %shard_map.93 = (bf16[256,768]{1,0:T(8,128)(2,1)S(1)}, bf16[256,768]{1,0:T(8,128)(2,1)S(1)}, bf16[3,256,256]{2,1,0:T(8,128)(2,1)S(1)}, bf16[512,256]{1,0:T(8,128...) custom-call(s32[2]{0:T(128)S(1)} %pad_add_fusion.at_ref, s32[8]{0:T(128)S(1)} %bitcast.47, ...), custom_call_target="tpu_custom_call" | custom-call | flops 21743271936 | bytes 6000000 | tf_op jit(solution)/shard_map/pallas_call | solution.py:172
  46.3 5.6 %collective-permute-start.12 = (bf16[512,256]{1,0:T(8,128)(2,1)S(1)}, bf16[512,256]{1,0:T(8,128)(2,1)S(1)}, u32[]{:S(2)}, u32[]{:S(2)}) collective-permute-start(bf16[512,256]{1,0:T(8,128)(2,1)S(1)} %get-tuple-element.36), channel_id=1, source_target_pairs={{0,6},{2,0},{4,2},{6,4},{1,7},{3,1},{5,3},{7,5},{8,14},{10,8},{12,... | collective-permute-start | bytes 786440 | tf_op jit(solution)/shard_map/ppermute | solution.py:264
  52.0 1.4 %collective-permute-start.14 = (bf16[512,256]{1,0:T(8,128)(2,1)S(1)}, bf16[512,256]{1,0:T(8,128)(2,1)S(1)}, u32[]{:S(2)}, u32[]{:S(2)}) collective-permute-start(bf16[512,256]{1,0:T(8,128)(2,1)S(1)} %get-tuple-element.38), channel_id=1, source_target_pairs={{0,4},{2,6},{4,0},{6,2},{1,5},{3,7},{5,1},{7,3},{8,12},{10,14},{12... | collective-permute-start | bytes 786440 | tf_op jit(solution)/shard_map/ppermute | solution.py:264
  53.4 1.2 %collective-permute-done.15.refs_5_ = bf16[1088,256]{1,0:T(8,128)(2,1)S(1)} collective-permute-done((bf16[1088,256]{1,0:T(8,128)(2,1)S(1)}, bf16[1088,256]{1,0:T(8,128)(2,1)S(1)}, u32[]{:S(2)}, u32[]{:S(2)}) %collective-permute-start.15) | collective-permute-done | bytes 557088 | tf_op jit(solution)/shard_map/ppermute | solution.py:321
  54.6 7.9 %shard_map.94 = (bf16[256,768]{1,0:T(8,128)(2,1)S(1)}, bf16[256,768]{1,0:T(8,128)(2,1)S(1)}, bf16[3,256,256]{2,1,0:T(8,128)(2,1)S(1)}, bf16[512,256]{1,0:T(8,128...) custom-call(s32[2]{0:T(128)S(1)} %pad_add_fusion.at_ref, s32[8]{0:T(128)S(1)} %bitcast.48, ...), custom_call_target="tpu_custom_call" | custom-call | flops 21743271936 | bytes 6000000 | tf_op jit(solution)/shard_map/pallas_call | solution.py:172
  62.5 5.0 %collective-permute-start.23 = (bf16[512,256]{1,0:T(8,128)(2,1)S(1)}, bf16[512,256]{1,0:T(8,128)(2,1)S(1)}, u32[]{:S(2)}, u32[]{:S(2)}) collective-permute-start(bf16[512,256]{1,0:T(8,128)(2,1)S(1)} %get-tuple-element.50), channel_id=1, source_target_pairs={{0,6},{2,0},{4,2},{6,4},{1,7},{3,1},{5,3},{7,5},{8,14},{10,8},{12,... | collective-permute-start | bytes 786440 | tf_op jit(solution)/shard_map/ppermute | solution.py:264
  67.5 1.3 %collective-permute-start.25 = (bf16[512,256]{1,0:T(8,128)(2,1)S(1)}, bf16[512,256]{1,0:T(8,128)(2,1)S(1)}, u32[]{:S(2)}, u32[]{:S(2)}) collective-permute-start(bf16[512,256]{1,0:T(8,128)(2,1)S(1)} %get-tuple-element.52), channel_id=1, source_target_pairs={{0,4},{2,6},{4,0},{6,2},{1,5},{3,7},{5,1},{7,3},{8,12},{10,14},{12... | collective-permute-start | bytes 786440 | tf_op jit(solution)/shard_map/ppermute | solution.py:264
  69.1 11.8 %collective-permute-start.17 = (f32[3,128]{1,0:T(4,128)S(1)}, f32[3,128]{1,0:T(4,128)S(1)}, u32[]{:S(2)}, u32[]{:S(2)}) collective-permute-start(f32[3,128]{1,0:T(4,128)S(1)} %convert_add_fusion.6), channel_id=1, source_target_pairs={{0,24},{8,0},{16,8},{24,16},{1,25},{9,1},{17,9},{25,17},{2,26},{10... | collective-permute-start | bytes 4616 | tf_op jit(solution)/shard_map/ppermute | solution.py:337
  81.6 1.7 %collective-permute-start.19 = (bf16[256,256]{1,0:T(8,128)(2,1)S(1)}, bf16[256,256]{1,0:T(8,128)(2,1)S(1)}, u32[]{:S(2)}, u32[]{:S(2)}) collective-permute-start(bf16[256,256]{1,0:T(8,128)(2,1)S(1)} %get-tuple-element.62), channel_id=1, source_target_pairs={{0,16},{8,24},{16,0},{24,8},{1,17},{9,25},{17,1},{25,9},{2,18},{10... | collective-permute-start | bytes 393224 | tf_op jit(solution)/shard_map/ppermute | solution.py:281
  83.7 8.1 %collective-permute-start.27 = (bf16[256,256]{1,0:T(8,128)(2,1)S(1)}, bf16[256,256]{1,0:T(8,128)(2,1)S(1)}, u32[]{:S(2)}, u32[]{:S(2)}) collective-permute-start(bf16[256,256]{1,0:T(8,128)(2,1)S(1)} %get-tuple-element.61), channel_id=1, source_target_pairs={{0,24},{8,0},{16,8},{24,16},{1,25},{9,1},{17,9},{25,17},{2,26},{10... | collective-permute-start | bytes 393224 | tf_op jit(solution)/shard_map/ppermute | solution.py:280
  91.8 3.7 %collective-permute-start.26 = (bf16[128,3072]{1,0:T(8,128)(2,1)S(1)}, bf16[128,3072]{1,0:T(8,128)(2,1)S(1)}, u32[]{:S(2)}, u32[]{:S(2)}) collective-permute-start(bf16[128,3072]{1,0:T(8,128)(2,1)S(1)} %pad_maximum_fusion), channel_id=1, source_target_pairs={{0,1},{1,0},{2,3},{3,2},{4,5},{5,4},{6,7},{7,6},{8,9},{9,8},{10,11... | collective-permute-start | bytes 2359304 | tf_op jit(solution)/shard_map/ppermute | solution.py:344
  95.6 8.1 %collective-permute-start.22 = (f32[3,128]{1,0:T(4,128)S(1)}, f32[3,128]{1,0:T(4,128)S(1)}, u32[]{:S(2)}, u32[]{:S(2)}) collective-permute-start(f32[3,128]{1,0:T(4,128)S(1)} %add_add_fusion), channel_id=1, source_target_pairs={{0,96},{32,0},{64,32},{96,64},{1,97},{33,1},{65,33},{97,65},{2,98}... | collective-permute-start | bytes 4616 | tf_op jit(solution)/shard_map/ppermute | solution.py:339
  103.6 0.7 collective-permute-done.22
  104.4 3.2 %collective-permute-done.21 = f32[3,128]{1,0:T(4,128)S(1)} collective-permute-done((f32[3,128]{1,0:T(4,128)S(1)}, f32[3,128]{1,0:T(4,128)S(1)}, u32[]{:S(2)}, u32[]{:S(2)}) %collective-permute-start.21) | collective-permute-done | bytes 1568 | tf_op jit(solution)/shard_map/ppermute | solution.py:339
  107.6 1.0 collective-permute-done.20
  108.7 1.8 %collective-permute-start.29 = (bf16[128,512]{1,0:T(8,128)(2,1)S(1)}, bf16[128,512]{1,0:T(8,128)(2,1)S(1)}, u32[]{:S(2)}, u32[]{:S(2)}) collective-permute-start(bf16[128,512]{1,0:T(8,128)(2,1)S(1)} %fusion.21), channel_id=1, source_target_pairs={{0,1},{1,0},{2,3},{3,2},{4,5},{5,4},{6,7},{7,6},{8,9},{9,8},{10,11... | collective-permute-start | bytes 393224 | tf_op jit(solution)/shard_map/ppermute | solution.py:349
  110.6 1.3 %shard_map.95 = (bf16[128,3072]{1,0:T(8,128)(2,1)}, bf16[128,3072]{1,0:T(8,128)(2,1)}) custom-call(s32[1]{0:T(128)} %bitcast.core_ref, f32[12,128]{1,0:T(8,128)S(1)} %pad_maximum_fusion.5.total_ref, bf16[256,768]{1,0:T(8,128)(2,1)S(1)} %get-tuple-element.39.att0, bf16[256,768]{1,0:T(8,128)(2,1)S(1)} %get-tuple-element.47.att1, ...), custom_call_target="tpu_custom_call" | custom-call | tf_op jit(solution)/shard_map/pallas_call | solution.py:230
  111.9 0.8 shard_map.96
  (85 shorter events, 4.9 us)
Async XLA Ops:
  0.6 3.3 %copy-start.3 = (f32[1,128]{1,0:T(1,128)S(1)}, f32[1,128]{1,0:T(1,128)}, u32[]{:S(2)}) copy-start(f32[1,128]{1,0:T(1,128)} %param.10) | copy-start | bytes 1540
  1.4 4.1 %collective-permute-start = (f32[8,128]{1,0:T(8,128)S(1)}, f32[8,128]{1,0:T(8,128)S(1)}, u32[]{:S(2)}, u32[]{:S(2)}) collective-permute-start(f32[8,128]{1,0:T(8,128)S(1)} %broadcast_in_dim.67), channel_id=1, source_target_pairs={{0,1},{1,0},{2,3},{3,2},{4,5},{5,4},{6,7},{7,6},{8,9},{9,8},{10,11... | collective-permute-start | bytes 12296 | tf_op jit(solution)/shard_map/ppermute | solution.py:299
  3.8 1.8 %collective-permute-start.1 = (bf16[128,512]{1,0:T(8,128)(2,1)S(1)}, bf16[128,512]{1,0:T(8,128)(2,1)S(1)}, u32[]{:S(2)}, u32[]{:S(2)}) collective-permute-start(bf16[128,512]{1,0:T(8,128)(2,1)S(1)} %pad_maximum_fusion.4), channel_id=1, source_target_pairs={{0,1},{1,0},{2,3},{3,2},{4,5},{5,4},{6,7},{7,6},{8,9},{9,8},{10,11... | collective-permute-start | bytes 393224 | tf_op jit(solution)/shard_map/ppermute | solution.py:300
  5.7 6.2 %collective-permute-start.8 = (bf16[256,256]{1,0:T(8,128)(2,1)S(1)}, bf16[256,256]{1,0:T(8,128)(2,1)S(1)}, u32[]{:S(2)}, u32[]{:S(2)}) collective-permute-start(bf16[256,256]{1,0:T(8,128)(2,1)S(1)} %get-tuple-element.72.refs_4_), channel_id=1, source_target_pairs={{0,16},{8,24},{16,0},{24,8},{1,17},{9,25},{17,1},{25,9},{2,18},{10... | collective-permute-start | bytes 393224 | tf_op jit(solution)/shard_map/ppermute | solution.py:305
  8.6 6.7 %collective-permute-start.7 = (bf16[256,256]{1,0:T(8,128)(2,1)S(1)}, bf16[256,256]{1,0:T(8,128)(2,1)S(1)}, u32[]{:S(2)}, u32[]{:S(2)}) collective-permute-start(bf16[256,256]{1,0:T(8,128)(2,1)S(1)} %get-tuple-element.72.refs_4_), channel_id=1, source_target_pairs={{0,8},{8,16},{16,24},{24,0},{1,9},{9,17},{17,25},{25,1},{2,10},{10... | collective-permute-start | bytes 393224 | tf_op jit(solution)/shard_map/ppermute | solution.py:304
  8.9 9.2 %collective-permute-start.2 = (bf16[272,256]{1,0:T(8,128)(2,1)S(1)}, bf16[272,256]{1,0:T(8,128)(2,1)S(1)}, u32[]{:S(2)}, u32[]{:S(2)}) collective-permute-start(bf16[272,256]{1,0:T(8,128)(2,1)S(1)} %maximum_maximum_fusion), channel_id=1, source_target_pairs={{0,2},{2,4},{4,6},{6,0},{1,3},{3,5},{5,7},{7,1},{8,10},{10,12},{12... | collective-permute-start | bytes 417800 | tf_op jit(solution)/shard_map/ppermute | solution.py:306
  10.3 12.5 %collective-permute-start.5 = (bf16[128,1536]{1,0:T(8,128)(2,1)S(1)}, bf16[128,1536]{1,0:T(8,128)(2,1)S(1)}, u32[]{:S(2)}, u32[]{:S(2)}) collective-permute-start(bf16[128,1536]{1,0:T(8,128)(2,1)S(1)} %get-tuple-element.32), channel_id=1, source_target_pairs={{0,1},{1,0},{2,3},{3,2},{4,5},{5,4},{6,7},{7,6},{8,9},{9,8},{10,11... | collective-permute-start | bytes 1179656 | tf_op jit(solution)/shard_map/ppermute | solution.py:311
  11.6 11.2 %collective-permute-start.6 = (bf16[128,1536]{1,0:T(8,128)(2,1)S(1)}, bf16[128,1536]{1,0:T(8,128)(2,1)S(1)}, u32[]{:S(2)}, u32[]{:S(2)}) collective-permute-start(bf16[128,1536]{1,0:T(8,128)(2,1)S(1)} %get-tuple-element.33), channel_id=1, source_target_pairs={{0,1},{1,0},{2,3},{3,2},{4,5},{5,4},{6,7},{7,6},{8,9},{9,8},{10,11... | collective-permute-start | bytes 1179656 | tf_op jit(solution)/shard_map/ppermute | solution.py:312
  11.8 15.1 %collective-permute-start.4 = (bf16[272,256]{1,0:T(8,128)(2,1)S(1)}, bf16[272,256]{1,0:T(8,128)(2,1)S(1)}, u32[]{:S(2)}, u32[]{:S(2)}) collective-permute-start(bf16[272,256]{1,0:T(8,128)(2,1)S(1)} %maximum_maximum_fusion), channel_id=1, source_target_pairs={{0,4},{2,6},{4,0},{6,2},{1,5},{3,7},{5,1},{7,3},{8,12},{10,14},{12... | collective-permute-start | bytes 417800 | tf_op jit(solution)/shard_map/ppermute | solution.py:306
  15.2 7.5 %collective-permute-start.3 = (bf16[272,256]{1,0:T(8,128)(2,1)S(1)}, bf16[272,256]{1,0:T(8,128)(2,1)S(1)}, u32[]{:S(2)}, u32[]{:S(2)}) collective-permute-start(bf16[272,256]{1,0:T(8,128)(2,1)S(1)} %maximum_maximum_fusion), channel_id=1, source_target_pairs={{0,6},{2,0},{4,2},{6,4},{1,7},{3,1},{5,3},{7,5},{8,14},{10,8},{12,... | collective-permute-start | bytes 417800 | tf_op jit(solution)/shard_map/ppermute | solution.py:306
  22.7 15.7 %copy-start = (s32[1,8]{1,0:T(1,128)S(1)}, s32[1,8]{1,0:T(1,128)}, u32[]{:S(2)}) copy-start(s32[1,8]{1,0:T(1,128)} %param.11) | copy-start | bytes 100
  22.8 8.9 %collective-permute-start.11 = (bf16[512,256]{1,0:T(8,128)(2,1)S(1)}, bf16[512,256]{1,0:T(8,128)(2,1)S(1)}, u32[]{:S(2)}, u32[]{:S(2)}) collective-permute-start(bf16[512,256]{1,0:T(8,128)(2,1)S(1)} %get-tuple-element.68), channel_id=1, source_target_pairs={{0,4},{2,6},{4,0},{6,2},{1,5},{3,7},{5,1},{7,3},{8,12},{10,14},{12... | collective-permute-start | bytes 786440 | tf_op jit(solution)/shard_map/ppermute | solution.py:319
  24.1 14.3 %collective-permute-start.10 = (bf16[512,256]{1,0:T(8,128)(2,1)S(1)}, bf16[512,256]{1,0:T(8,128)(2,1)S(1)}, u32[]{:S(2)}, u32[]{:S(2)}) collective-permute-start(bf16[512,256]{1,0:T(8,128)(2,1)S(1)} %get-tuple-element.69), channel_id=1, source_target_pairs={{0,6},{2,0},{4,2},{6,4},{1,7},{3,1},{5,3},{7,5},{8,14},{10,8},{12,... | collective-permute-start | bytes 786440 | tf_op jit(solution)/shard_map/ppermute | solution.py:319
  26.4 12.1 %collective-permute-start.9 = (bf16[512,256]{1,0:T(8,128)(2,1)S(1)}, bf16[512,256]{1,0:T(8,128)(2,1)S(1)}, u32[]{:S(2)}, u32[]{:S(2)}) collective-permute-start(bf16[512,256]{1,0:T(8,128)(2,1)S(1)} %get-tuple-element.70), channel_id=1, source_target_pairs={{0,2},{2,4},{4,6},{6,0},{1,3},{3,5},{5,7},{7,1},{8,10},{10,12},{12... | collective-permute-start | bytes 786440 | tf_op jit(solution)/shard_map/ppermute | solution.py:319
  26.9 26.5 %collective-permute-start.16 = (bf16[1088,256]{1,0:T(8,128)(2,1)S(1)}, bf16[1088,256]{1,0:T(8,128)(2,1)S(1)}, u32[]{:S(2)}, u32[]{:S(2)}) collective-permute-start(bf16[1088,256]{1,0:T(8,128)(2,1)S(1)} %constant_dynamic-update-slice_fusion.refs_4_), channel_id=1, source_target_pairs={{0,16},{8,24},{16,0},{24,8},{1,17},{9,25},{17,1},{25,9},{2,18},{10... | collective-permute-start | bytes 1671176 | tf_op jit(solution)/shard_map/ppermute | solution.py:321
  27.1 27.5 %collective-permute-start.15 = (bf16[1088,256]{1,0:T(8,128)(2,1)S(1)}, bf16[1088,256]{1,0:T(8,128)(2,1)S(1)}, u32[]{:S(2)}, u32[]{:S(2)}) collective-permute-start(bf16[1088,256]{1,0:T(8,128)(2,1)S(1)} %constant_dynamic-update-slice_fusion.refs_4_), channel_id=1, source_target_pairs={{0,8},{8,16},{16,24},{24,0},{1,9},{9,17},{17,25},{25,1},{2,10},{10... | collective-permute-start | bytes 1671176 | tf_op jit(solution)/shard_map/ppermute | solution.py:321
  46.3 21.2 %collective-permute-start.12 = (bf16[512,256]{1,0:T(8,128)(2,1)S(1)}, bf16[512,256]{1,0:T(8,128)(2,1)S(1)}, u32[]{:S(2)}, u32[]{:S(2)}) collective-permute-start(bf16[512,256]{1,0:T(8,128)(2,1)S(1)} %get-tuple-element.36), channel_id=1, source_target_pairs={{0,6},{2,0},{4,2},{6,4},{1,7},{3,1},{5,3},{7,5},{8,14},{10,8},{12,... | collective-permute-start | bytes 786440 | tf_op jit(solution)/shard_map/ppermute | solution.py:264
  51.9 16.8 %collective-permute-start.13 = (bf16[512,256]{1,0:T(8,128)(2,1)S(1)}, bf16[512,256]{1,0:T(8,128)(2,1)S(1)}, u32[]{:S(2)}, u32[]{:S(2)}) collective-permute-start(bf16[512,256]{1,0:T(8,128)(2,1)S(1)} %get-tuple-element.37), channel_id=1, source_target_pairs={{0,2},{2,4},{4,6},{6,0},{1,3},{3,5},{5,7},{7,1},{8,10},{10,12},{12... | collective-permute-start | bytes 786440 | tf_op jit(solution)/shard_map/ppermute | solution.py:264
  52.0 16.8 %collective-permute-start.14 = (bf16[512,256]{1,0:T(8,128)(2,1)S(1)}, bf16[512,256]{1,0:T(8,128)(2,1)S(1)}, u32[]{:S(2)}, u32[]{:S(2)}) collective-permute-start(bf16[512,256]{1,0:T(8,128)(2,1)S(1)} %get-tuple-element.38), channel_id=1, source_target_pairs={{0,4},{2,6},{4,0},{6,2},{1,5},{3,7},{5,1},{7,3},{8,12},{10,14},{12... | collective-permute-start | bytes 786440 | tf_op jit(solution)/shard_map/ppermute | solution.py:264
  62.5 20.8 %collective-permute-start.23 = (bf16[512,256]{1,0:T(8,128)(2,1)S(1)}, bf16[512,256]{1,0:T(8,128)(2,1)S(1)}, u32[]{:S(2)}, u32[]{:S(2)}) collective-permute-start(bf16[512,256]{1,0:T(8,128)(2,1)S(1)} %get-tuple-element.50), channel_id=1, source_target_pairs={{0,6},{2,0},{4,2},{6,4},{1,7},{3,1},{5,3},{7,5},{8,14},{10,8},{12,... | collective-permute-start | bytes 786440 | tf_op jit(solution)/shard_map/ppermute | solution.py:264
  67.5 15.9 %collective-permute-start.24 = (bf16[512,256]{1,0:T(8,128)(2,1)S(1)}, bf16[512,256]{1,0:T(8,128)(2,1)S(1)}, u32[]{:S(2)}, u32[]{:S(2)}) collective-permute-start(bf16[512,256]{1,0:T(8,128)(2,1)S(1)} %get-tuple-element.51), channel_id=1, source_target_pairs={{0,2},{2,4},{4,6},{6,0},{1,3},{3,5},{5,7},{7,1},{8,10},{10,12},{12... | collective-permute-start | bytes 786440 | tf_op jit(solution)/shard_map/ppermute | solution.py:264
  67.5 15.9 %collective-permute-start.25 = (bf16[512,256]{1,0:T(8,128)(2,1)S(1)}, bf16[512,256]{1,0:T(8,128)(2,1)S(1)}, u32[]{:S(2)}, u32[]{:S(2)}) collective-permute-start(bf16[512,256]{1,0:T(8,128)(2,1)S(1)} %get-tuple-element.52), channel_id=1, source_target_pairs={{0,4},{2,6},{4,0},{6,2},{1,5},{3,7},{5,1},{7,3},{8,12},{10,14},{12... | collective-permute-start | bytes 786440 | tf_op jit(solution)/shard_map/ppermute | solution.py:264
  69.1 12.5 %collective-permute-start.17 = (f32[3,128]{1,0:T(4,128)S(1)}, f32[3,128]{1,0:T(4,128)S(1)}, u32[]{:S(2)}, u32[]{:S(2)}) collective-permute-start(f32[3,128]{1,0:T(4,128)S(1)} %convert_add_fusion.6), channel_id=1, source_target_pairs={{0,24},{8,0},{16,8},{24,16},{1,25},{9,1},{17,9},{25,17},{2,26},{10... | collective-permute-start | bytes 4616 | tf_op jit(solution)/shard_map/ppermute | solution.py:337
  81.0 14.5 %collective-permute-start.18 = (bf16[256,256]{1,0:T(8,128)(2,1)S(1)}, bf16[256,256]{1,0:T(8,128)(2,1)S(1)}, u32[]{:S(2)}, u32[]{:S(2)}) collective-permute-start(bf16[256,256]{1,0:T(8,128)(2,1)S(1)} %get-tuple-element.63), channel_id=1, source_target_pairs={{0,24},{8,0},{16,8},{24,16},{1,25},{9,1},{17,9},{25,17},{2,26},{10... | collective-permute-start | bytes 393224 | tf_op jit(solution)/shard_map/ppermute | solution.py:280
  81.6 13.8 %collective-permute-start.19 = (bf16[256,256]{1,0:T(8,128)(2,1)S(1)}, bf16[256,256]{1,0:T(8,128)(2,1)S(1)}, u32[]{:S(2)}, u32[]{:S(2)}) collective-permute-start(bf16[256,256]{1,0:T(8,128)(2,1)S(1)} %get-tuple-element.62), channel_id=1, source_target_pairs={{0,16},{8,24},{16,0},{24,8},{1,17},{9,25},{17,1},{25,9},{2,18},{10... | collective-permute-start | bytes 393224 | tf_op jit(solution)/shard_map/ppermute | solution.py:281
  83.7 24.9 %collective-permute-start.27 = (bf16[256,256]{1,0:T(8,128)(2,1)S(1)}, bf16[256,256]{1,0:T(8,128)(2,1)S(1)}, u32[]{:S(2)}, u32[]{:S(2)}) collective-permute-start(bf16[256,256]{1,0:T(8,128)(2,1)S(1)} %get-tuple-element.61), channel_id=1, source_target_pairs={{0,24},{8,0},{16,8},{24,16},{1,25},{9,1},{17,9},{25,17},{2,26},{10... | collective-permute-start | bytes 393224 | tf_op jit(solution)/shard_map/ppermute | solution.py:280
  91.8 16.8 %collective-permute-start.28 = (bf16[256,256]{1,0:T(8,128)(2,1)S(1)}, bf16[256,256]{1,0:T(8,128)(2,1)S(1)}, u32[]{:S(2)}, u32[]{:S(2)}) collective-permute-start(bf16[256,256]{1,0:T(8,128)(2,1)S(1)} %get-tuple-element.60), channel_id=1, source_target_pairs={{0,16},{8,24},{16,0},{24,8},{1,17},{9,25},{17,1},{25,9},{2,18},{10... | collective-permute-start | bytes 393224 | tf_op jit(solution)/shard_map/ppermute | solution.py:281
  91.8 18.8 %collective-permute-start.26 = (bf16[128,3072]{1,0:T(8,128)(2,1)S(1)}, bf16[128,3072]{1,0:T(8,128)(2,1)S(1)}, u32[]{:S(2)}, u32[]{:S(2)}) collective-permute-start(bf16[128,3072]{1,0:T(8,128)(2,1)S(1)} %pad_maximum_fusion), channel_id=1, source_target_pairs={{0,1},{1,0},{2,3},{3,2},{4,5},{5,4},{6,7},{7,6},{8,9},{9,8},{10,11... | collective-permute-start | bytes 2359304 | tf_op jit(solution)/shard_map/ppermute | solution.py:344
  95.6 8.8 %collective-permute-start.22 = (f32[3,128]{1,0:T(4,128)S(1)}, f32[3,128]{1,0:T(4,128)S(1)}, u32[]{:S(2)}, u32[]{:S(2)}) collective-permute-start(f32[3,128]{1,0:T(4,128)S(1)} %add_add_fusion), channel_id=1, source_target_pairs={{0,96},{32,0},{64,32},{96,64},{1,97},{33,1},{65,33},{97,65},{2,98}... | collective-permute-start | bytes 4616 | tf_op jit(solution)/shard_map/ppermute | solution.py:339
  103.6 3.9 %collective-permute-start.21 = (f32[3,128]{1,0:T(4,128)S(1)}, f32[3,128]{1,0:T(4,128)S(1)}, u32[]{:S(2)}, u32[]{:S(2)}) collective-permute-start(f32[3,128]{1,0:T(4,128)S(1)} %add_add_fusion), channel_id=1, source_target_pairs={{0,64},{32,96},{64,0},{96,32},{1,65},{33,97},{65,1},{97,33},{2,66}... | collective-permute-start | bytes 4616 | tf_op jit(solution)/shard_map/ppermute | solution.py:339
  104.4 4.2 %collective-permute-start.20 = (f32[3,128]{1,0:T(4,128)S(1)}, f32[3,128]{1,0:T(4,128)S(1)}, u32[]{:S(2)}, u32[]{:S(2)}) collective-permute-start(f32[3,128]{1,0:T(4,128)S(1)} %add_add_fusion), channel_id=1, source_target_pairs={{0,32},{32,64},{64,96},{96,0},{1,33},{33,65},{65,97},{97,1},{2,34}... | collective-permute-start | bytes 4616 | tf_op jit(solution)/shard_map/ppermute | solution.py:339
  108.7 3.2 %collective-permute-start.29 = (bf16[128,512]{1,0:T(8,128)(2,1)S(1)}, bf16[128,512]{1,0:T(8,128)(2,1)S(1)}, u32[]{:S(2)}, u32[]{:S(2)}) collective-permute-start(bf16[128,512]{1,0:T(8,128)(2,1)S(1)} %fusion.21), channel_id=1, source_target_pairs={{0,1},{1,0},{2,3},{3,2},{4,5},{5,4},{6,7},{7,6},{8,9},{9,8},{10,11... | collective-permute-start | bytes 393224 | tf_op jit(solution)/shard_map/ppermute | solution.py:349
  (2 other events, 4.5 us)

commit v7 on v6

--- a/solution.py
+++ b/solution.py
@@ -295,12 +295,11 @@
         k, v = half(key_rows[0], at), half(value_rows[0], at)
         return jnp.concatenate([k[:, :HD], v[:, :HD], k[:, HD:], v[:, HD:]], axis=1)
 
-    weights = jnp.broadcast_to(weights_row[None], (8, HD))
-    weights = weights + lax.ppermute(weights, "core", SWAP)
+    weights = loss_weight + lax.ppermute(loss_weight, "core", SWAP)
     kv_other = lax.ppermute(heads(other_at), "core", SWAP)
     own = jnp.concatenate([heads(mine_at), kv_other], axis=0)
     first = own[:, :2 * HD]
-    second = jnp.concatenate([own[:, 2 * HD:], note(weights[:1])], axis=0)
+    second = jnp.concatenate([own[:, 2 * HD:], note(weights)], axis=0)
     r1 = lax.ppermute(first, "x", ring(1))
     r2 = lax.ppermute(first, "x", ring(2))
     nearest = [lax.ppermute(second, "y", ring(k)) for k in (1, 3, 2)]

time: 111 us -> 110 us (level); the launches traced: 113 us -> 110 us
  starting transfers between devices: 67.3 us -> 64 us
    ppermute x1, starting transfers between devices: 11.8 us -> 0.58 us  [body(): total = total + lax.ppermute(after(total, sums0[1]), 'x', ring(3))]
    ppermute x2, starting transfers between devices: 8.16 us -> 17.3 us  [scatter_x(): t1 = lax.ppermute(sums[1], 'x', ring(3))]
    ppermute x2, starting transfers between devices: 1.72 us -> 9 us  [scatter_x(): t2 = lax.ppermute(sums[2], 'x', ring(2))]
    ppermute x3, starting transfers between devices: 8.07 us -> 0.99 us  [body(): pieces = [total] + [lax.ppermute(total, 'dp', ring(k)) for k in (1, 2, 3)]]
    ppermute x6, starting transfers between devices: 13.3 us -> 10.8 us  [send_y(): lax.ppermute(pair, 'y', ring(4 - k))]
    ppermute x1, waiting for transfers between devices: 1.16 us -> 2.89 us  [body(): lax.ppermute(near, 'x', ring(1))]
  transfers between devices with their start and end apart: 30 -> 30, of which waited for: 10 -> 9; matrix products, arithmetic and copies ran while one was open for 2% -> 2% of each run, Pallas kernels for 15% -> 16%
where the time goes in v7:
time: 110 us
  starting transfers between devices  64 us (58%)
  waiting for transfers between devices  23 us (21%)
  Pallas kernels  17.9 us (16%)
  local copies, waits for them, and re-layouts  2.35 us (2%)
  other arithmetic  1.38 us (1%)
    ppermute x2, starting transfers between devices, scatter_x(): t1 = lax.ppermute(sums[1], 'x', ring(3))  17.3 us
    pallas_call x2, Pallas kernels, attention(): pl.pallas_call(functools.partial(attention_kernel, head, places_of, len(p...  15.7 us
    ppermute x6, starting transfers between devices, send_y(): lax.ppermute(pair, 'y', ring(4 - k))  10.8 us
    ppermute x3, waiting for transfers between devices, body(): first_pieces.append(lax.ppermute(pair, 'y', ring(k)))  9.66 us
    ppermute x2, starting transfers between devices, scatter_x(): t2 = lax.ppermute(sums[2], 'x', ring(2))  9 us
    ppermute x3, starting transfers between devices, body(): nearest = [lax.ppermute(second, 'y', ring(k)) for k in (1, 3, 2)]  7.16 us
    ppermute x3, waiting for transfers between devices, body(): pieces = [total] + [lax.ppermute(total, 'dp', ring(k)) for k in (1, 2, 3)]  5.16 us
    ppermute x3, waiting for transfers between devices, body(): nearest = [lax.ppermute(second, 'y', ring(k)) for k in (1, 3, 2)]  4.47 us
  transfers between devices with their start and end apart: 30, of which 9 were waited for; matrix products, arithmetic and copies ran while one was open for 2% of the time, Pallas kernels for 16%

profile of v7, /device:TPU:1, one launch (start us, length us, event | category | flops | bytes accessed | tf_op | source)
XLA Modules:
  0.0 109.6 jit_solution(17470610244986965296)
XLA Ops:
  0.7 1.5 %collective-permute-start = (f32[1,128]{1,0:T(1,128)}, f32[1,128]{1,0:T(1,128)S(1)}, u32[]{:S(2)}, u32[]{:S(2)}) collective-permute-start(f32[1,128]{1,0:T(1,128)} %param.10), channel_id=1, source_target_pairs={{0,1},{1,0},{2,3},{3,2},{4,5},{5,4},{6,7},{7,6},{8,9},{9,8},{10,11... | collective-permute-start | bytes 1544 | tf_op jit(solution)/shard_map/ppermute | solution.py:298
  2.2 1.0 dynamic-slice_bitcast_fusion.4
  3.7 1.1 copy-done.2
  5.1 2.9 %collective-permute-start.8 = (bf16[256,256]{1,0:T(8,128)(2,1)S(1)}, bf16[256,256]{1,0:T(8,128)(2,1)S(1)}, u32[]{:S(2)}, u32[]{:S(2)}) collective-permute-start(bf16[256,256]{1,0:T(8,128)(2,1)S(1)} %get-tuple-element.72.refs_4_), channel_id=1, source_target_pairs={{0,16},{8,24},{16,0},{24,8},{1,17},{9,25},{17,1},{25,9},{2,18},{10... | collective-permute-start | bytes 393224 | tf_op jit(solution)/shard_map/ppermute | solution.py:304
  8.3 1.4 %collective-permute-start.2 = (bf16[272,256]{1,0:T(8,128)(2,1)S(1)}, bf16[272,256]{1,0:T(8,128)(2,1)S(1)}, u32[]{:S(2)}, u32[]{:S(2)}) collective-permute-start(bf16[272,256]{1,0:T(8,128)(2,1)S(1)} %maximum_maximum_fusion), channel_id=1, source_target_pairs={{0,2},{2,4},{4,6},{6,0},{1,3},{3,5},{5,7},{7,1},{8,10},{10,12},{12... | collective-permute-start | bytes 417800 | tf_op jit(solution)/shard_map/ppermute | solution.py:305
  9.7 1.3 %collective-permute-start.5 = (bf16[128,1536]{1,0:T(8,128)(2,1)S(1)}, bf16[128,1536]{1,0:T(8,128)(2,1)S(1)}, u32[]{:S(2)}, u32[]{:S(2)}) collective-permute-start(bf16[128,1536]{1,0:T(8,128)(2,1)S(1)} %get-tuple-element.32), channel_id=1, source_target_pairs={{0,1},{1,0},{2,3},{3,2},{4,5},{5,4},{6,7},{7,6},{8,9},{9,8},{10,11... | collective-permute-start | bytes 1179656 | tf_op jit(solution)/shard_map/ppermute | solution.py:310
  11.3 3.0 %collective-permute-start.4 = (bf16[272,256]{1,0:T(8,128)(2,1)S(1)}, bf16[272,256]{1,0:T(8,128)(2,1)S(1)}, u32[]{:S(2)}, u32[]{:S(2)}) collective-permute-start(bf16[272,256]{1,0:T(8,128)(2,1)S(1)} %maximum_maximum_fusion), channel_id=1, source_target_pairs={{0,4},{2,6},{4,0},{6,2},{1,5},{3,7},{5,1},{7,3},{8,12},{10,14},{12... | collective-permute-start | bytes 417800 | tf_op jit(solution)/shard_map/ppermute | solution.py:305
  14.7 2.8 %collective-permute-start.3 = (bf16[272,256]{1,0:T(8,128)(2,1)S(1)}, bf16[272,256]{1,0:T(8,128)(2,1)S(1)}, u32[]{:S(2)}, u32[]{:S(2)}) collective-permute-start(bf16[272,256]{1,0:T(8,128)(2,1)S(1)} %maximum_maximum_fusion), channel_id=1, source_target_pairs={{0,6},{2,0},{4,2},{6,4},{1,7},{3,1},{5,3},{7,5},{8,14},{10,8},{12,... | collective-permute-start | bytes 417800 | tf_op jit(solution)/shard_map/ppermute | solution.py:305
  17.5 4.5 %collective-permute-done.3 = bf16[272,256]{1,0:T(8,128)(2,1)S(1)} collective-permute-done((bf16[272,256]{1,0:T(8,128)(2,1)S(1)}, bf16[272,256]{1,0:T(8,128)(2,1)S(1)}, u32[]{:S(2)}, u32[]{:S(2)}) %collective-permute-start.3) | collective-permute-done | bytes 139296 | tf_op jit(solution)/shard_map/ppermute | solution.py:305
  22.1 1.4 %collective-permute-start.11 = (bf16[512,256]{1,0:T(8,128)(2,1)S(1)}, bf16[512,256]{1,0:T(8,128)(2,1)S(1)}, u32[]{:S(2)}, u32[]{:S(2)}) collective-permute-start(bf16[512,256]{1,0:T(8,128)(2,1)S(1)} %get-tuple-element.68), channel_id=1, source_target_pairs={{0,4},{2,6},{4,0},{6,2},{1,5},{3,7},{5,1},{7,3},{8,12},{10,14},{12... | collective-permute-start | bytes 786440 | tf_op jit(solution)/shard_map/ppermute | solution.py:318
  23.5 2.1 %collective-permute-start.10 = (bf16[512,256]{1,0:T(8,128)(2,1)S(1)}, bf16[512,256]{1,0:T(8,128)(2,1)S(1)}, u32[]{:S(2)}, u32[]{:S(2)}) collective-permute-start(bf16[512,256]{1,0:T(8,128)(2,1)S(1)} %get-tuple-element.69), channel_id=1, source_target_pairs={{0,6},{2,0},{4,2},{6,4},{1,7},{3,1},{5,3},{7,5},{8,14},{10,8},{12,... | collective-permute-start | bytes 786440 | tf_op jit(solution)/shard_map/ppermute | solution.py:318
  26.5 1.4 %collective-permute-start.15 = (bf16[1088,256]{1,0:T(8,128)(2,1)S(1)}, bf16[1088,256]{1,0:T(8,128)(2,1)S(1)}, u32[]{:S(2)}, u32[]{:S(2)}) collective-permute-start(bf16[1088,256]{1,0:T(8,128)(2,1)S(1)} %constant_dynamic-update-slice_fusion.refs_4_), channel_id=1, source_target_pairs={{0,8},{8,16},{16,24},{24,0},{1,9},{9,17},{17,25},{25,1},{2,10},{10... | collective-permute-start | bytes 1671176 | tf_op jit(solution)/shard_map/ppermute | solution.py:320
  27.9 2.9 %collective-permute-done.11.refs_9_ = bf16[512,256]{1,0:T(8,128)(2,1)S(1)} collective-permute-done((bf16[512,256]{1,0:T(8,128)(2,1)S(1)}, bf16[512,256]{1,0:T(8,128)(2,1)S(1)}, u32[]{:S(2)}, u32[]{:S(2)}) %collective-permute-start.11) | collective-permute-done | bytes 262176 | tf_op jit(solution)/shard_map/ppermute | solution.py:318
  30.9 6.7 %collective-permute-done.10.refs_8_ = bf16[512,256]{1,0:T(8,128)(2,1)S(1)} collective-permute-done((bf16[512,256]{1,0:T(8,128)(2,1)S(1)}, bf16[512,256]{1,0:T(8,128)(2,1)S(1)}, u32[]{:S(2)}, u32[]{:S(2)}) %collective-permute-start.10) | collective-permute-done | bytes 262176 | tf_op jit(solution)/shard_map/ppermute | solution.py:318
  37.6 7.8 %shard_map.93 = (bf16[256,768]{1,0:T(8,128)(2,1)S(1)}, bf16[256,768]{1,0:T(8,128)(2,1)S(1)}, bf16[3,256,256]{2,1,0:T(8,128)(2,1)S(1)}, bf16[512,256]{1,0:T(8,128...) custom-call(s32[2]{0:T(128)S(1)} %pad_add_fusion.at_ref, s32[8]{0:T(128)S(1)} %bitcast.47, ...), custom_call_target="tpu_custom_call" | custom-call | flops 21743271936 | bytes 6000000 | tf_op jit(solution)/shard_map/pallas_call | solution.py:172
  45.5 4.4 %collective-permute-start.12 = (bf16[512,256]{1,0:T(8,128)(2,1)S(1)}, bf16[512,256]{1,0:T(8,128)(2,1)S(1)}, u32[]{:S(2)}, u32[]{:S(2)}) collective-permute-start(bf16[512,256]{1,0:T(8,128)(2,1)S(1)} %get-tuple-element.36), channel_id=1, source_target_pairs={{0,6},{2,0},{4,2},{6,4},{1,7},{3,1},{5,3},{7,5},{8,14},{10,8},{12,... | collective-permute-start | bytes 786440 | tf_op jit(solution)/shard_map/ppermute | solution.py:264
  49.9 1.4 %collective-permute-start.14 = (bf16[512,256]{1,0:T(8,128)(2,1)S(1)}, bf16[512,256]{1,0:T(8,128)(2,1)S(1)}, u32[]{:S(2)}, u32[]{:S(2)}) collective-permute-start(bf16[512,256]{1,0:T(8,128)(2,1)S(1)} %get-tuple-element.38), channel_id=1, source_target_pairs={{0,4},{2,6},{4,0},{6,2},{1,5},{3,7},{5,1},{7,3},{8,12},{10,14},{12... | collective-permute-start | bytes 786440 | tf_op jit(solution)/shard_map/ppermute | solution.py:264
  51.3 2.9 %collective-permute-done.15.refs_5_ = bf16[1088,256]{1,0:T(8,128)(2,1)S(1)} collective-permute-done((bf16[1088,256]{1,0:T(8,128)(2,1)S(1)}, bf16[1088,256]{1,0:T(8,128)(2,1)S(1)}, u32[]{:S(2)}, u32[]{:S(2)}) %collective-permute-start.15) | collective-permute-done | bytes 557088 | tf_op jit(solution)/shard_map/ppermute | solution.py:320
  54.2 7.9 %shard_map.94 = (bf16[256,768]{1,0:T(8,128)(2,1)S(1)}, bf16[256,768]{1,0:T(8,128)(2,1)S(1)}, bf16[3,256,256]{2,1,0:T(8,128)(2,1)S(1)}, bf16[512,256]{1,0:T(8,128...) custom-call(s32[2]{0:T(128)S(1)} %pad_add_fusion.at_ref, s32[8]{0:T(128)S(1)} %bitcast.48, ...), custom_call_target="tpu_custom_call" | custom-call | flops 21743271936 | bytes 6000000 | tf_op jit(solution)/shard_map/pallas_call | solution.py:172
  62.2 3.7 %collective-permute-start.23 = (bf16[512,256]{1,0:T(8,128)(2,1)S(1)}, bf16[512,256]{1,0:T(8,128)(2,1)S(1)}, u32[]{:S(2)}, u32[]{:S(2)}) collective-permute-start(bf16[512,256]{1,0:T(8,128)(2,1)S(1)} %get-tuple-element.50), channel_id=1, source_target_pairs={{0,6},{2,0},{4,2},{6,4},{1,7},{3,1},{5,3},{7,5},{8,14},{10,8},{12,... | collective-permute-start | bytes 786440 | tf_op jit(solution)/shard_map/ppermute | solution.py:264
  65.9 1.3 %collective-permute-start.25 = (bf16[512,256]{1,0:T(8,128)(2,1)S(1)}, bf16[512,256]{1,0:T(8,128)(2,1)S(1)}, u32[]{:S(2)}, u32[]{:S(2)}) collective-permute-start(bf16[512,256]{1,0:T(8,128)(2,1)S(1)} %get-tuple-element.52), channel_id=1, source_target_pairs={{0,4},{2,6},{4,0},{6,2},{1,5},{3,7},{5,1},{7,3},{8,12},{10,14},{12... | collective-permute-start | bytes 786440 | tf_op jit(solution)/shard_map/ppermute | solution.py:264
  68.1 16.3 %collective-permute-start.18 = (bf16[256,256]{1,0:T(8,128)(2,1)S(1)}, bf16[256,256]{1,0:T(8,128)(2,1)S(1)}, u32[]{:S(2)}, u32[]{:S(2)}) collective-permute-start(bf16[256,256]{1,0:T(8,128)(2,1)S(1)} %get-tuple-element.63), channel_id=1, source_target_pairs={{0,24},{8,0},{16,8},{24,16},{1,25},{9,1},{17,9},{25,17},{2,26},{10... | collective-permute-start | bytes 393224 | tf_op jit(solution)/shard_map/ppermute | solution.py:280
  84.4 2.0 %collective-permute-start.19 = (bf16[256,256]{1,0:T(8,128)(2,1)S(1)}, bf16[256,256]{1,0:T(8,128)(2,1)S(1)}, u32[]{:S(2)}, u32[]{:S(2)}) collective-permute-start(bf16[256,256]{1,0:T(8,128)(2,1)S(1)} %get-tuple-element.62), channel_id=1, source_target_pairs={{0,16},{8,24},{16,0},{24,8},{1,17},{9,25},{17,1},{25,9},{2,18},{10... | collective-permute-start | bytes 393224 | tf_op jit(solution)/shard_map/ppermute | solution.py:281
  86.7 1.0 collective-permute-start.27
  87.7 7.0 %collective-permute-start.28 = (bf16[256,256]{1,0:T(8,128)(2,1)S(1)}, bf16[256,256]{1,0:T(8,128)(2,1)S(1)}, u32[]{:S(2)}, u32[]{:S(2)}) collective-permute-start(bf16[256,256]{1,0:T(8,128)(2,1)S(1)} %get-tuple-element.60), channel_id=1, source_target_pairs={{0,16},{8,24},{16,0},{24,8},{1,17},{9,25},{17,1},{25,9},{2,18},{10... | collective-permute-start | bytes 393224 | tf_op jit(solution)/shard_map/ppermute | solution.py:281
  94.7 3.9 %collective-permute-start.26 = (bf16[128,3072]{1,0:T(8,128)(2,1)S(1)}, bf16[128,3072]{1,0:T(8,128)(2,1)S(1)}, u32[]{:S(2)}, u32[]{:S(2)}) collective-permute-start(bf16[128,3072]{1,0:T(8,128)(2,1)S(1)} %pad_maximum_fusion), channel_id=1, source_target_pairs={{0,1},{1,0},{2,3},{3,2},{4,5},{5,4},{6,7},{7,6},{8,9},{9,8},{10,11... | collective-permute-start | bytes 2359304 | tf_op jit(solution)/shard_map/ppermute | solution.py:343
  98.7 1.0 collective-permute-start.22
  99.7 1.5 %collective-permute-done.22 = f32[3,128]{1,0:T(4,128)S(1)} collective-permute-done((f32[3,128]{1,0:T(4,128)S(1)}, f32[3,128]{1,0:T(4,128)S(1)}, u32[]{:S(2)}, u32[]{:S(2)}) %collective-permute-start.22) | collective-permute-done | bytes 1568 | tf_op jit(solution)/shard_map/ppermute | solution.py:338
  101.2 2.4 %collective-permute-done.21 = f32[3,128]{1,0:T(4,128)S(1)} collective-permute-done((f32[3,128]{1,0:T(4,128)S(1)}, f32[3,128]{1,0:T(4,128)S(1)}, u32[]{:S(2)}, u32[]{:S(2)}) %collective-permute-start.21) | collective-permute-done | bytes 1568 | tf_op jit(solution)/shard_map/ppermute | solution.py:338
  103.6 1.2 %collective-permute-done.20 = f32[3,128]{1,0:T(4,128)S(1)} collective-permute-done((f32[3,128]{1,0:T(4,128)S(1)}, f32[3,128]{1,0:T(4,128)S(1)}, u32[]{:S(2)}, u32[]{:S(2)}) %collective-permute-start.20) | collective-permute-done | bytes 1568 | tf_op jit(solution)/shard_map/ppermute | solution.py:338
  105.0 2.4 %collective-permute-start.29 = (bf16[128,512]{1,0:T(8,128)(2,1)S(1)}, bf16[128,512]{1,0:T(8,128)(2,1)S(1)}, u32[]{:S(2)}, u32[]{:S(2)}) collective-permute-start(bf16[128,512]{1,0:T(8,128)(2,1)S(1)} %fusion.21), channel_id=1, source_target_pairs={{0,1},{1,0},{2,3},{3,2},{4,5},{5,4},{6,7},{7,6},{8,9},{9,8},{10,11... | collective-permute-start | bytes 393224 | tf_op jit(solution)/shard_map/ppermute | solution.py:348
  107.5 1.3 %shard_map.95 = (bf16[128,3072]{1,0:T(8,128)(2,1)}, bf16[128,3072]{1,0:T(8,128)(2,1)}) custom-call(s32[1]{0:T(128)} %bitcast.core_ref, f32[12,128]{1,0:T(8,128)S(1)} %pad_maximum_fusion.5.total_ref, bf16[256,768]{1,0:T(8,128)(2,1)S(1)} %get-tuple-element.39.att0, bf16[256,768]{1,0:T(8,128)(2,1)S(1)} %get-tuple-element.47.att1, ...), custom_call_target="tpu_custom_call" | custom-call | tf_op jit(solution)/shard_map/pallas_call | solution.py:230
  (83 shorter events, 5.3 us)
Async XLA Ops:
  0.6 2.8 %copy-start.3 = (f32[1,128]{1,0:T(1,128)S(1)}, f32[1,128]{1,0:T(1,128)}, u32[]{:S(2)}) copy-start(f32[1,128]{1,0:T(1,128)} %param.10) | copy-start | bytes 1540
  0.7 4.3 %collective-permute-start = (f32[1,128]{1,0:T(1,128)}, f32[1,128]{1,0:T(1,128)S(1)}, u32[]{:S(2)}, u32[]{:S(2)}) collective-permute-start(f32[1,128]{1,0:T(1,128)} %param.10), channel_id=1, source_target_pairs={{0,1},{1,0},{2,3},{3,2},{4,5},{5,4},{6,7},{7,6},{8,9},{9,8},{10,11... | collective-permute-start | bytes 1544 | tf_op jit(solution)/shard_map/ppermute | solution.py:298
  3.2 1.8 %collective-permute-start.1 = (bf16[128,512]{1,0:T(8,128)(2,1)S(1)}, bf16[128,512]{1,0:T(8,128)(2,1)S(1)}, u32[]{:S(2)}, u32[]{:S(2)}) collective-permute-start(bf16[128,512]{1,0:T(8,128)(2,1)S(1)} %pad_maximum_fusion.4), channel_id=1, source_target_pairs={{0,1},{1,0},{2,3},{3,2},{4,5},{5,4},{6,7},{7,6},{8,9},{9,8},{10,11... | collective-permute-start | bytes 393224 | tf_op jit(solution)/shard_map/ppermute | solution.py:299
  5.1 6.3 %collective-permute-start.8 = (bf16[256,256]{1,0:T(8,128)(2,1)S(1)}, bf16[256,256]{1,0:T(8,128)(2,1)S(1)}, u32[]{:S(2)}, u32[]{:S(2)}) collective-permute-start(bf16[256,256]{1,0:T(8,128)(2,1)S(1)} %get-tuple-element.72.refs_4_), channel_id=1, source_target_pairs={{0,16},{8,24},{16,0},{24,8},{1,17},{9,25},{17,1},{25,9},{2,18},{10... | collective-permute-start | bytes 393224 | tf_op jit(solution)/shard_map/ppermute | solution.py:304
  8.0 6.7 %collective-permute-start.7 = (bf16[256,256]{1,0:T(8,128)(2,1)S(1)}, bf16[256,256]{1,0:T(8,128)(2,1)S(1)}, u32[]{:S(2)}, u32[]{:S(2)}) collective-permute-start(bf16[256,256]{1,0:T(8,128)(2,1)S(1)} %get-tuple-element.72.refs_4_), channel_id=1, source_target_pairs={{0,8},{8,16},{16,24},{24,0},{1,9},{9,17},{17,25},{25,1},{2,10},{10... | collective-permute-start | bytes 393224 | tf_op jit(solution)/shard_map/ppermute | solution.py:303
  8.3 9.2 %collective-permute-start.2 = (bf16[272,256]{1,0:T(8,128)(2,1)S(1)}, bf16[272,256]{1,0:T(8,128)(2,1)S(1)}, u32[]{:S(2)}, u32[]{:S(2)}) collective-permute-start(bf16[272,256]{1,0:T(8,128)(2,1)S(1)} %maximum_maximum_fusion), channel_id=1, source_target_pairs={{0,2},{2,4},{4,6},{6,0},{1,3},{3,5},{5,7},{7,1},{8,10},{10,12},{12... | collective-permute-start | bytes 417800 | tf_op jit(solution)/shard_map/ppermute | solution.py:305
  9.7 12.3 %collective-permute-start.5 = (bf16[128,1536]{1,0:T(8,128)(2,1)S(1)}, bf16[128,1536]{1,0:T(8,128)(2,1)S(1)}, u32[]{:S(2)}, u32[]{:S(2)}) collective-permute-start(bf16[128,1536]{1,0:T(8,128)(2,1)S(1)} %get-tuple-element.32), channel_id=1, source_target_pairs={{0,1},{1,0},{2,3},{3,2},{4,5},{5,4},{6,7},{7,6},{8,9},{9,8},{10,11... | collective-permute-start | bytes 1179656 | tf_op jit(solution)/shard_map/ppermute | solution.py:310
  10.9 11.1 %collective-permute-start.6 = (bf16[128,1536]{1,0:T(8,128)(2,1)S(1)}, bf16[128,1536]{1,0:T(8,128)(2,1)S(1)}, u32[]{:S(2)}, u32[]{:S(2)}) collective-permute-start(bf16[128,1536]{1,0:T(8,128)(2,1)S(1)} %get-tuple-element.33), channel_id=1, source_target_pairs={{0,1},{1,0},{2,3},{3,2},{4,5},{5,4},{6,7},{7,6},{8,9},{9,8},{10,11... | collective-permute-start | bytes 1179656 | tf_op jit(solution)/shard_map/ppermute | solution.py:311
  11.3 14.8 %collective-permute-start.4 = (bf16[272,256]{1,0:T(8,128)(2,1)S(1)}, bf16[272,256]{1,0:T(8,128)(2,1)S(1)}, u32[]{:S(2)}, u32[]{:S(2)}) collective-permute-start(bf16[272,256]{1,0:T(8,128)(2,1)S(1)} %maximum_maximum_fusion), channel_id=1, source_target_pairs={{0,4},{2,6},{4,0},{6,2},{1,5},{3,7},{5,1},{7,3},{8,12},{10,14},{12... | collective-permute-start | bytes 417800 | tf_op jit(solution)/shard_map/ppermute | solution.py:305
  14.7 7.3 %collective-permute-start.3 = (bf16[272,256]{1,0:T(8,128)(2,1)S(1)}, bf16[272,256]{1,0:T(8,128)(2,1)S(1)}, u32[]{:S(2)}, u32[]{:S(2)}) collective-permute-start(bf16[272,256]{1,0:T(8,128)(2,1)S(1)} %maximum_maximum_fusion), channel_id=1, source_target_pairs={{0,6},{2,0},{4,2},{6,4},{1,7},{3,1},{5,3},{7,5},{8,14},{10,8},{12,... | collective-permute-start | bytes 417800 | tf_op jit(solution)/shard_map/ppermute | solution.py:305
  22.0 15.6 %copy-start = (s32[1,8]{1,0:T(1,128)S(1)}, s32[1,8]{1,0:T(1,128)}, u32[]{:S(2)}) copy-start(s32[1,8]{1,0:T(1,128)} %param.11) | copy-start | bytes 100
  22.1 8.8 %collective-permute-start.11 = (bf16[512,256]{1,0:T(8,128)(2,1)S(1)}, bf16[512,256]{1,0:T(8,128)(2,1)S(1)}, u32[]{:S(2)}, u32[]{:S(2)}) collective-permute-start(bf16[512,256]{1,0:T(8,128)(2,1)S(1)} %get-tuple-element.68), channel_id=1, source_target_pairs={{0,4},{2,6},{4,0},{6,2},{1,5},{3,7},{5,1},{7,3},{8,12},{10,14},{12... | collective-permute-start | bytes 786440 | tf_op jit(solution)/shard_map/ppermute | solution.py:318
  23.5 14.1 %collective-permute-start.10 = (bf16[512,256]{1,0:T(8,128)(2,1)S(1)}, bf16[512,256]{1,0:T(8,128)(2,1)S(1)}, u32[]{:S(2)}, u32[]{:S(2)}) collective-permute-start(bf16[512,256]{1,0:T(8,128)(2,1)S(1)} %get-tuple-element.69), channel_id=1, source_target_pairs={{0,6},{2,0},{4,2},{6,4},{1,7},{3,1},{5,3},{7,5},{8,14},{10,8},{12,... | collective-permute-start | bytes 786440 | tf_op jit(solution)/shard_map/ppermute | solution.py:318
  25.7 11.9 %collective-permute-start.9 = (bf16[512,256]{1,0:T(8,128)(2,1)S(1)}, bf16[512,256]{1,0:T(8,128)(2,1)S(1)}, u32[]{:S(2)}, u32[]{:S(2)}) collective-permute-start(bf16[512,256]{1,0:T(8,128)(2,1)S(1)} %get-tuple-element.70), channel_id=1, source_target_pairs={{0,2},{2,4},{4,6},{6,0},{1,3},{3,5},{5,7},{7,1},{8,10},{10,12},{12... | collective-permute-start | bytes 786440 | tf_op jit(solution)/shard_map/ppermute | solution.py:318
  26.2 25.2 %collective-permute-start.16 = (bf16[1088,256]{1,0:T(8,128)(2,1)S(1)}, bf16[1088,256]{1,0:T(8,128)(2,1)S(1)}, u32[]{:S(2)}, u32[]{:S(2)}) collective-permute-start(bf16[1088,256]{1,0:T(8,128)(2,1)S(1)} %constant_dynamic-update-slice_fusion.refs_4_), channel_id=1, source_target_pairs={{0,16},{8,24},{16,0},{24,8},{1,17},{9,25},{17,1},{25,9},{2,18},{10... | collective-permute-start | bytes 1671176 | tf_op jit(solution)/shard_map/ppermute | solution.py:320
  26.5 27.7 %collective-permute-start.15 = (bf16[1088,256]{1,0:T(8,128)(2,1)S(1)}, bf16[1088,256]{1,0:T(8,128)(2,1)S(1)}, u32[]{:S(2)}, u32[]{:S(2)}) collective-permute-start(bf16[1088,256]{1,0:T(8,128)(2,1)S(1)} %constant_dynamic-update-slice_fusion.refs_4_), channel_id=1, source_target_pairs={{0,8},{8,16},{16,24},{24,0},{1,9},{9,17},{17,25},{25,1},{2,10},{10... | collective-permute-start | bytes 1671176 | tf_op jit(solution)/shard_map/ppermute | solution.py:320
  45.5 20.4 %collective-permute-start.12 = (bf16[512,256]{1,0:T(8,128)(2,1)S(1)}, bf16[512,256]{1,0:T(8,128)(2,1)S(1)}, u32[]{:S(2)}, u32[]{:S(2)}) collective-permute-start(bf16[512,256]{1,0:T(8,128)(2,1)S(1)} %get-tuple-element.36), channel_id=1, source_target_pairs={{0,6},{2,0},{4,2},{6,4},{1,7},{3,1},{5,3},{7,5},{8,14},{10,8},{12,... | collective-permute-start | bytes 786440 | tf_op jit(solution)/shard_map/ppermute | solution.py:264
  49.9 17.2 %collective-permute-start.13 = (bf16[512,256]{1,0:T(8,128)(2,1)S(1)}, bf16[512,256]{1,0:T(8,128)(2,1)S(1)}, u32[]{:S(2)}, u32[]{:S(2)}) collective-permute-start(bf16[512,256]{1,0:T(8,128)(2,1)S(1)} %get-tuple-element.37), channel_id=1, source_target_pairs={{0,2},{2,4},{4,6},{6,0},{1,3},{3,5},{5,7},{7,1},{8,10},{10,12},{12... | collective-permute-start | bytes 786440 | tf_op jit(solution)/shard_map/ppermute | solution.py:264
  49.9 17.2 %collective-permute-start.14 = (bf16[512,256]{1,0:T(8,128)(2,1)S(1)}, bf16[512,256]{1,0:T(8,128)(2,1)S(1)}, u32[]{:S(2)}, u32[]{:S(2)}) collective-permute-start(bf16[512,256]{1,0:T(8,128)(2,1)S(1)} %get-tuple-element.38), channel_id=1, source_target_pairs={{0,4},{2,6},{4,0},{6,2},{1,5},{3,7},{5,1},{7,3},{8,12},{10,14},{12... | collective-permute-start | bytes 786440 | tf_op jit(solution)/shard_map/ppermute | solution.py:264
  62.2 24.2 %collective-permute-start.23 = (bf16[512,256]{1,0:T(8,128)(2,1)S(1)}, bf16[512,256]{1,0:T(8,128)(2,1)S(1)}, u32[]{:S(2)}, u32[]{:S(2)}) collective-permute-start(bf16[512,256]{1,0:T(8,128)(2,1)S(1)} %get-tuple-element.50), channel_id=1, source_target_pairs={{0,6},{2,0},{4,2},{6,4},{1,7},{3,1},{5,3},{7,5},{8,14},{10,8},{12,... | collective-permute-start | bytes 786440 | tf_op jit(solution)/shard_map/ppermute | solution.py:264
  65.9 20.6 %collective-permute-start.24 = (bf16[512,256]{1,0:T(8,128)(2,1)S(1)}, bf16[512,256]{1,0:T(8,128)(2,1)S(1)}, u32[]{:S(2)}, u32[]{:S(2)}) collective-permute-start(bf16[512,256]{1,0:T(8,128)(2,1)S(1)} %get-tuple-element.51), channel_id=1, source_target_pairs={{0,2},{2,4},{4,6},{6,0},{1,3},{3,5},{5,7},{7,1},{8,10},{10,12},{12... | collective-permute-start | bytes 786440 | tf_op jit(solution)/shard_map/ppermute | solution.py:264
  65.9 20.6 %collective-permute-start.25 = (bf16[512,256]{1,0:T(8,128)(2,1)S(1)}, bf16[512,256]{1,0:T(8,128)(2,1)S(1)}, u32[]{:S(2)}, u32[]{:S(2)}) collective-permute-start(bf16[512,256]{1,0:T(8,128)(2,1)S(1)} %get-tuple-element.52), channel_id=1, source_target_pairs={{0,4},{2,6},{4,0},{6,2},{1,5},{3,7},{5,1},{7,3},{8,12},{10,14},{12... | collective-permute-start | bytes 786440 | tf_op jit(solution)/shard_map/ppermute | solution.py:264
  67.4 17.0 %collective-permute-start.17 = (f32[3,128]{1,0:T(4,128)S(1)}, f32[3,128]{1,0:T(4,128)S(1)}, u32[]{:S(2)}, u32[]{:S(2)}) collective-permute-start(f32[3,128]{1,0:T(4,128)S(1)} %convert_add_fusion.6), channel_id=1, source_target_pairs={{0,24},{8,0},{16,8},{24,16},{1,25},{9,1},{17,9},{25,17},{2,26},{10... | collective-permute-start | bytes 4616 | tf_op jit(solution)/shard_map/ppermute | solution.py:336
  68.1 30.5 %collective-permute-start.18 = (bf16[256,256]{1,0:T(8,128)(2,1)S(1)}, bf16[256,256]{1,0:T(8,128)(2,1)S(1)}, u32[]{:S(2)}, u32[]{:S(2)}) collective-permute-start(bf16[256,256]{1,0:T(8,128)(2,1)S(1)} %get-tuple-element.63), channel_id=1, source_target_pairs={{0,24},{8,0},{16,8},{24,16},{1,25},{9,1},{17,9},{25,17},{2,26},{10... | collective-permute-start | bytes 393224 | tf_op jit(solution)/shard_map/ppermute | solution.py:280
  84.4 14.2 %collective-permute-start.19 = (bf16[256,256]{1,0:T(8,128)(2,1)S(1)}, bf16[256,256]{1,0:T(8,128)(2,1)S(1)}, u32[]{:S(2)}, u32[]{:S(2)}) collective-permute-start(bf16[256,256]{1,0:T(8,128)(2,1)S(1)} %get-tuple-element.62), channel_id=1, source_target_pairs={{0,16},{8,24},{16,0},{24,8},{1,17},{9,25},{17,1},{25,9},{2,18},{10... | collective-permute-start | bytes 393224 | tf_op jit(solution)/shard_map/ppermute | solution.py:281
  86.7 18.2 %collective-permute-start.27 = (bf16[256,256]{1,0:T(8,128)(2,1)S(1)}, bf16[256,256]{1,0:T(8,128)(2,1)S(1)}, u32[]{:S(2)}, u32[]{:S(2)}) collective-permute-start(bf16[256,256]{1,0:T(8,128)(2,1)S(1)} %get-tuple-element.61), channel_id=1, source_target_pairs={{0,24},{8,0},{16,8},{24,16},{1,25},{9,1},{17,9},{25,17},{2,26},{10... | collective-permute-start | bytes 393224 | tf_op jit(solution)/shard_map/ppermute | solution.py:280
  87.7 17.2 %collective-permute-start.28 = (bf16[256,256]{1,0:T(8,128)(2,1)S(1)}, bf16[256,256]{1,0:T(8,128)(2,1)S(1)}, u32[]{:S(2)}, u32[]{:S(2)}) collective-permute-start(bf16[256,256]{1,0:T(8,128)(2,1)S(1)} %get-tuple-element.60), channel_id=1, source_target_pairs={{0,16},{8,24},{16,0},{24,8},{1,17},{9,25},{17,1},{25,9},{2,18},{10... | collective-permute-start | bytes 393224 | tf_op jit(solution)/shard_map/ppermute | solution.py:281
  94.7 12.8 %collective-permute-start.26 = (bf16[128,3072]{1,0:T(8,128)(2,1)S(1)}, bf16[128,3072]{1,0:T(8,128)(2,1)S(1)}, u32[]{:S(2)}, u32[]{:S(2)}) collective-permute-start(bf16[128,3072]{1,0:T(8,128)(2,1)S(1)} %pad_maximum_fusion), channel_id=1, source_target_pairs={{0,1},{1,0},{2,3},{3,2},{4,5},{5,4},{6,7},{7,6},{8,9},{9,8},{10,11... | collective-permute-start | bytes 2359304 | tf_op jit(solution)/shard_map/ppermute | solution.py:343
  98.7 2.5 %collective-permute-start.22 = (f32[3,128]{1,0:T(4,128)S(1)}, f32[3,128]{1,0:T(4,128)S(1)}, u32[]{:S(2)}, u32[]{:S(2)}) collective-permute-start(f32[3,128]{1,0:T(4,128)S(1)} %add_add_fusion), channel_id=1, source_target_pairs={{0,96},{32,0},{64,32},{96,64},{1,97},{33,1},{65,33},{97,65},{2,98}... | collective-permute-start | bytes 4616 | tf_op jit(solution)/shard_map/ppermute | solution.py:338
  99.7 3.9 %collective-permute-start.21 = (f32[3,128]{1,0:T(4,128)S(1)}, f32[3,128]{1,0:T(4,128)S(1)}, u32[]{:S(2)}, u32[]{:S(2)}) collective-permute-start(f32[3,128]{1,0:T(4,128)S(1)} %add_add_fusion), channel_id=1, source_target_pairs={{0,64},{32,96},{64,0},{96,32},{1,65},{33,97},{65,1},{97,33},{2,66}... | collective-permute-start | bytes 4616 | tf_op jit(solution)/shard_map/ppermute | solution.py:338
  101.2 3.6 %collective-permute-start.20 = (f32[3,128]{1,0:T(4,128)S(1)}, f32[3,128]{1,0:T(4,128)S(1)}, u32[]{:S(2)}, u32[]{:S(2)}) collective-permute-start(f32[3,128]{1,0:T(4,128)S(1)} %add_add_fusion), channel_id=1, source_target_pairs={{0,32},{32,64},{64,96},{96,0},{1,33},{33,65},{65,97},{97,1},{2,34}... | collective-permute-start | bytes 4616 | tf_op jit(solution)/shard_map/ppermute | solution.py:338
  105.0 3.8 %collective-permute-start.29 = (bf16[128,512]{1,0:T(8,128)(2,1)S(1)}, bf16[128,512]{1,0:T(8,128)(2,1)S(1)}, u32[]{:S(2)}, u32[]{:S(2)}) collective-permute-start(bf16[128,512]{1,0:T(8,128)(2,1)S(1)} %fusion.21), channel_id=1, source_target_pairs={{0,1},{1,0},{2,3},{3,2},{4,5},{5,4},{6,7},{7,6},{8,9},{9,8},{10,11... | collective-permute-start | bytes 393224 | tf_op jit(solution)/shard_map/ppermute | solution.py:348
  (2 other events, 3.9 us)
